TPU v7x, 1024 devices: a whole 4x8x16 slice. The times are simulated.
1024 devices in a mesh: group: 64 (over x, z), tensor: 16 (over y, core).
Axes of the slice: x: 4, y: 8, z: 16, core: 2. Of those that a mesh axis runs over, the one named last changes fastest.
Arguments:
- pre_hidden: bfloat16 [9216, 8192], P('group', 'tensor'), may hold values from -6 to 6
- proj_weight: bfloat16 [8192, 8192], P('tensor'), may hold values from -0.09375 to 0.09375
- text_embed: bfloat16 [24576, 8192], P('group', 'tensor'), may hold values from -6 to 6
- routes_dest: int32 [9216, 1], P('group'), may hold values from 0 to 63; in each aligned block of 144 rows (0 to 143, 144 to 287, ...) at most 3 rows name the same one
- place: int32 [64, 192], P('group'), may hold values from 0 to 383, as said below
- grad_packed: bfloat16 [24576, 8192], P('group', 'tensor'), may hold values from -6 to 6
Outputs:
- packed: bfloat16 [24576, 8192], P('group', 'tensor')
- grad_hidden: bfloat16 [9216, 8192], P('group', 'tensor')
Inputs may be any that keep to these rules, and one draw needn't show every extreme that they name: `routes_dest`: no destination is named by more than 3 image tokens of one owner, a bound that some block reaches. `place`: the offsets of one row are all different.
All inputs are finite; a program needn't handle non-finite values.
Results may differ from a plain program's by a relative error of at most 0.012.
Values may be sent and summed in bfloat16 or wider, within the bound.
No kernel may reach another device: no remote copies, remote signals or barrier semaphores. Data moves between devices by JAX's collectives and lax.ppermute only.
A program may use at most 64 MiB of HBM per device.

v0:
```python
import jax
import jax.numpy as jnp
from jax import lax
from jax.sharding import PartitionSpec as P


def gelu_slope(values):
    cdf = 0.5 * (1.0 + jax.scipy.special.erf(values * 0.7071067811865476))
    dens = jnp.exp(-0.5 * values * values) * 0.3989422804014327
    return cdf + values * dens


def slot_targets(dest_column, capacity, groups):
    onehot = (dest_column[:, None] == jnp.arange(groups, dtype=jnp.int32)[None, :]).astype(
        jnp.int32
    )
    ranks = jnp.sum(jnp.where(onehot == 1, jnp.cumsum(onehot, axis=0) - 1, 0), axis=1)
    return dest_column * capacity + ranks


def on_device(pre_hidden, proj_weight, text_embed, routes_dest, place, grad_packed):
    groups = lax.axis_size("group")
    slots = place.shape[1]
    capacity = slots // groups
    hid_local = pre_hidden.shape[1]
    targets = slot_targets(routes_dest[:, 0], capacity, groups)
    offsets = place[0]
    pre_float = pre_hidden.astype(jnp.float32)
    act = jax.nn.gelu(pre_float, approximate=False).astype(jnp.bfloat16)
    flags_out = jnp.zeros((slots,), jnp.bfloat16).at[targets].set(1.0)
    outgoing = jnp.zeros((slots, hid_local), jnp.bfloat16).at[targets].set(act)
    arrived, flags = (
        lax.all_to_all(
            outgoing.reshape(groups, capacity, hid_local),
            "group",
            split_axis=0,
            concat_axis=0,
            tiled=True,
        ),
        lax.all_to_all(
            flags_out.reshape(groups, capacity), "group", split_axis=0, concat_axis=0, tiled=True
        ),
    )
    arrived = arrived.reshape(slots, hid_local)
    partial_terms = jnp.dot(arrived, proj_weight, preferred_element_type=jnp.float32)
    embed = lax.psum_scatter(
        partial_terms.astype(jnp.bfloat16), "tensor", scatter_dimension=1, tiled=True
    )
    flags = flags.reshape(slots)
    placed = jnp.zeros_like(text_embed).at[offsets].set(embed)
    marks = jnp.zeros((text_embed.shape[0],), jnp.bfloat16).at[offsets].set(flags)
    packed = jnp.where(marks[:, None] > 0, placed, text_embed)
    slot_grad = grad_packed[offsets]
    slot_act_grad = lax.dot_general(
        lax.all_gather(slot_grad, "tensor", axis=1, tiled=True),
        proj_weight,
        (((1,), (1,)), ((), ())),
        preferred_element_type=jnp.float32,
    )
    returned = lax.all_to_all(
        slot_act_grad.reshape(groups, capacity, hid_local).astype(jnp.bfloat16),
        "group",
        split_axis=0,
        concat_axis=0,
        tiled=True,
    ).astype(jnp.float32)
    grad_act = returned.reshape(slots, hid_local)[targets]
    grad_hidden = (grad_act * gelu_slope(pre_float)).astype(jnp.bfloat16)
    return (packed, grad_hidden)


def solution(mesh):
    return jax.shard_map(
        on_device,
        mesh=mesh,
        in_specs=(
            P("group", "tensor"),
            P("tensor", None),
            P("group", "tensor"),
            P("group", None),
            P("group", None),
            P("group", "tensor"),
        ),
        out_specs=(P("group", "tensor"), P("group", "tensor")),
        check_vma=False,
    )
```

profile of v0, /device:TPU:1, one launch (start us, length us, event | category | flops | bytes accessed | tf_op | source)
XLA Modules:
  0.0 149.5 jit_solution(12001123676768212031)
XLA Ops:
  7.2 0.7 compare_select_fusion.1
  8.0 0.2 copy-done
  8.2 1.7 %gather_fusion = bf16[192,512]{1,0:T(8,128)(2,1)} fusion(bf16[384,512]{1,0:T(8,128)(2,1)S(1)} %copy-done, s32[1024]{0:T(1024)S(1)} %pad_clamp_fusion.1), kind=kCustom, calls=%fused_computation | custom fusion | bytes 393984 | tf_op jit(solution)/shard_map/gather | solution.py:53
  9.9 0.7 iota_compare_fusion
  10.6 0.6 reduce-window.6
  11.6 0.7 fusion.75
  12.3 0.7 compare_select_fusion
  13.0 2.2 %scatter_custom_fusion.2 = bf16[192,512]{1,0:T(8,128)(2,1)S(1)} fusion(s32[144]{0:T(256)S(1)} %bitcast.29, bf16[144,512]{1,0:T(8,128)(2,1)} %param.6, f32[]{:T(128)} %constant.37.clone.1, f32[]{:T(128)} %constant.36.clone.1, f32[]{:T(128)} %constant.35.clone.1, f32[]{:T(128)} %constant.34.clone.1, f32[]{:T(128)} %constant.33.clone.1, f32[]{:T(128)} %constant.32.clone.1, ...), kind=kCustom, calls=%fused_computation.57 | custom fusion | flops 4866048 | bytes 344186 | tf_op jit(solution)/shard_map/scatter | solution.py:31
  15.3 41.6 %all_to_all.20 = bf16[64,3,512]{2,1,0:T(4,128)(2,1)S(1)} all-to-all(bf16[64,3,512]{2,1,0:T(4,128)(2,1)S(1)} %reshape.71), channel_id=1, replica_groups=mesh['group'=64,'tensor'=16] {'group'}, dimensions={0} | all-to-all | bytes 393216 | tf_op jit(solution)/shard_map/all_to_all | solution.py:33
  57.1 7.0 %convolution_convert_fusion = bf16[192,8192]{1,0:T(8,128)(2,1)} fusion(bf16[192,512]{1,0:T(8,128)(2,1)S(1)} %reshape.72, bf16[512,8192]{1,0:T(8,128)(2,1)} %param.7), kind=kOutput, calls=%fused_computation.6 | convolution fusion | flops 1612185600 | bytes 11730944 | tf_op jit(solution)/shard_map/dot_general | solution.py:45
  64.2 1.5 scatter_custom_fusion
  65.6 0.8 all_to_all.16
  66.4 7.6 %all-to-all-start = ((bf16[64,1,3]{2,1,0:T(2,128)(2,1)}), bf16[64,1,3]{2,1,0:T(2,128)(2,1)S(1)}, u32[]{:S(2)}, u32[]{:S(2)}) async-start(bf16[64,1,3]{2,1,0:T(2,128)(2,1)} %all_to_all.16), calls=%async_computation | async-start | bytes 65536 | tf_op jit(solution)/shard_map/all_to_all | solution.py:40
  74.1 7.3 %convolution_convert_fusion.1 = bf16[192,512]{1,0:T(8,128)(2,1)S(1)} fusion(bf16[192,8192]{1,0:T(8,128)(2,1)} %all-gather.3.cloned.1.call-done, bf16[512,8192]{1,0:T(8,128)(2,1)} %param.7), kind=kOutput, calls=%fused_computation.7 | convolution fusion | flops 1610711040 | bytes 11730944 | tf_op jit(solution)/shard_map/dot_general | solution.py:54
  81.4 0.8 convert_element_type.28
  82.2 5.1 %all-to-all-done = bf16[64,1,3]{2,1,0:T(2,128)(2,1)S(1)} async-done(((bf16[64,1,3]{2,1,0:T(2,128)(2,1)}), bf16[64,1,3]{2,1,0:T(2,128)(2,1)S(1)}, u32[]{:S(2)}, u32[]{:S(2)}) %all-to-all-start) | async-done | bytes 416 | tf_op jit(solution)/shard_map/all_to_all | solution.py:40
  87.3 9.7 %all-to-all-start.2 = ((bf16[64,3,512]{2,1,0:T(4,128)(2,1)}), bf16[64,3,512]{2,1,0:T(4,128)(2,1)S(1)}, u32[]{:S(2)}, u32[]{:S(2)}) async-start(bf16[64,3,512]{2,1,0:T(4,128)(2,1)} %convert_element_type.28), calls=%async_computation.3 | async-start | bytes 524288 | tf_op jit(solution)/shard_map/all_to_all | solution.py:60
  97.2 1.8 %scatter_custom_fusion.1 = bf16[384]{0:T(512)(128)(2,1)S(1)} fusion(s32[192]{0:T(256)S(1)} %bitcast.33, bf16[192]{0:T(256)(128)(2,1)S(1)} %reshape.106, bf16[]{:T(256)} %constant.41.clone.1), kind=kCustom, calls=%fused_computation.105 | custom fusion | bytes 770 | tf_op jit(solution)/shard_map/scatter | solution.py:51
  99.0 15.5 %all-to-all-done.2 = bf16[64,3,512]{2,1,0:T(4,128)(2,1)S(1)} async-done(((bf16[64,3,512]{2,1,0:T(4,128)(2,1)}), bf16[64,3,512]{2,1,0:T(4,128)(2,1)S(1)}, u32[]{:S(2)}, u32[]{:S(2)}) %all-to-all-start.2) | async-done | bytes 196640 | tf_op jit(solution)/shard_map/all_to_all | solution.py:60
  114.7 0.8 gather_fusion.1
  115.5 0.8 fusion.38
  116.3 23.7 %reduce-scatter.2.cloned.1.call-done = bf16[192,512]{1,0:T(8,128)(2,1)} async-done(((bf16[192,8192]{1,0:T(8,128)(2,1)}), bf16[192,512]{1,0:T(8,128)(2,1)}) %reduce-scatter.2.cloned.1.call-update) | async-done | bytes 196624 | tf_op jit(solution)/shard_map/reduce_scatter | solution.py:46
  140.0 1.8 %scatter_custom_fusion.3 = bf16[384,512]{1,0:T(8,128)(2,1)S(1)} fusion(s32[192]{0:T(256)S(1)} %bitcast.34, bf16[192,512]{1,0:T(8,128)(2,1)} %reduce-scatter.2.cloned.1.call-done, bf16[]{:T(256)} %constant.41.clone.1), kind=kCustom, calls=%fused_computation.55 | custom fusion | bytes 393728 | tf_op jit(solution)/shard_map/scatter | solution.py:50
  141.8 0.9 broadcast_select_fusion
  (24 shorter events, 1.2 us)
Async XLA Ops:
  7.2 1.0 copy-start
  7.2 66.9 %all-gather.3.cloned.1.call-start = ((), (), s32[]{:S(2)}) async-start(), calls=%async_computation.5 | async-start | bytes 3342336 | tf_op jit(solution)/shard_map/all_gather | solution.py:55
  9.9 130.1 %reduce-scatter.2.cloned.1.call-start = ((), (), s32[]{:S(2)}) async-start(), calls=%async_computation.4 | async-start | bytes 3342336 | tf_op jit(solution)/shard_map/reduce_scatter | solution.py:46
  64.2 51.3 %copy-start.1 = (bf16[144,512]{1,0:T(8,128)(2,1)S(1)}, bf16[144,512]{1,0:T(8,128)(2,1)}, u32[]{:S(2)}) copy-start(bf16[144,512]{1,0:T(8,128)(2,1)} %param.6) | copy-start | bytes 442372
  66.4 20.8 %all-to-all-start = ((bf16[64,1,3]{2,1,0:T(2,128)(2,1)}), bf16[64,1,3]{2,1,0:T(2,128)(2,1)S(1)}, u32[]{:S(2)}, u32[]{:S(2)}) async-start(bf16[64,1,3]{2,1,0:T(2,128)(2,1)} %all_to_all.16), calls=%async_computation | async-start | bytes 65536 | tf_op jit(solution)/shard_map/all_to_all | solution.py:40
  74.0 67.7 %copy-start.2 = (bf16[384,512]{1,0:T(8,128)(2,1)S(1)}, bf16[384,512]{1,0:T(8,128)(2,1)}, u32[]{:S(2)}) copy-start(bf16[384,512]{1,0:T(8,128)(2,1)} %param.8) | copy-start | bytes 1179652
  87.3 27.3 %all-to-all-start.2 = ((bf16[64,3,512]{2,1,0:T(4,128)(2,1)}), bf16[64,3,512]{2,1,0:T(4,128)(2,1)S(1)}, u32[]{:S(2)}, u32[]{:S(2)}) async-start(bf16[64,3,512]{2,1,0:T(4,128)(2,1)} %convert_element_type.28), calls=%async_computation.3 | async-start | bytes 524288 | tf_op jit(solution)/shard_map/all_to_all | solution.py:60
Sparse Core Ops, SparseCore 0:
  11.3 57.8 all-gather.2
  72.7 67.2 reduce-scatter.1
where the time goes:
time: 150 us; the launch traced here: 149 us
  waiting for transfers between devices  44.3 us (30%)
  blocking collectives  41.6 us (28%)
  starting transfers between devices  17.4 us (12%)
  matrix products  14.3 us (10%)
  between operations  14.2 us (9%)
  local copies, waits for them, and re-layouts  10.1 us (7%)
  other arithmetic  7.54 us (5%)
    all_to_all x1, blocking collectives, on_device(): lax.all_to_all(outgoing.reshape(groups, capacity, hid_local), 'group', sp...  41.6 us
    reduce_scatter x1, waiting for transfers between devices, on_device(): lax.psum_scatter(partial_terms.astype(jnp.bfloat16), 'tensor', scatter_di...  23.7 us
    all_to_all x1, waiting for transfers between devices, on_device(): lax.all_to_all(slot_act_grad.reshape(groups, capacity, hid_local).astype(...  15.5 us
    all_to_all x1, starting transfers between devices, on_device(): lax.all_to_all(slot_act_grad.reshape(groups, capacity, hid_local).astype(...  9.68 us
    all_to_all x1, starting transfers between devices, on_device(): lax.all_to_all(flags_out.reshape(groups, capacity), 'group', split_axis=0...  7.61 us
    dot_general x1, matrix products, on_device(): lax.dot_general(lax.all_gather(slot_grad, 'tensor', axis=1, tiled=True),...  7.28 us
    dot_general x1, matrix products, on_device(): jnp.dot(arrived, proj_weight, preferred_element_type=jnp.float32)  7.01 us
    all_to_all x1, waiting for transfers between devices, on_device(): lax.all_to_all(flags_out.reshape(groups, capacity), 'group', split_axis=0...  5.07 us
  transfers between devices with their start and end apart: 4, of which 3 were waited for; matrix products, arithmetic and copies ran while one was open for 17% of the time, Pallas kernels for 0%

commit v1 on v0

v1 whole, which is shorter than its diff:
```python
import functools

import jax
import jax.numpy as jnp
from jax import lax
from jax.experimental import pallas as pl
from jax.experimental.pallas import tpu as pltpu
from jax.sharding import Mesh
from jax.sharding import PartitionSpec as P

BF16 = jnp.bfloat16
F32 = jnp.float32
EMPTY = 1.7e38
LIMIT = 1.0e38


def gelu(values):
    return values * 0.5 * (1.0 + lax.erf(values * 0.7071067811865476))


def gelu_slope(values):
    cdf = 0.5 * (1.0 + lax.erf(values * 0.7071067811865476))
    dens = jnp.exp(-0.5 * values * values) * 0.3989422804014327
    return cdf + values * dens


def rows_by_target(dest_row, groups, capacity, slots):
    rows = dest_row.shape[1]
    hit = lax.broadcasted_iota(jnp.int32, (groups, rows), 0) == dest_row
    before = lax.broadcasted_iota(jnp.int32, (rows, rows), 0) < lax.broadcasted_iota(
        jnp.int32, (rows, rows), 1
    )
    onehot = jnp.where(hit, 1.0, 0.0)
    counts = jnp.dot(
        onehot.astype(BF16), jnp.where(before, 1.0, 0.0).astype(BF16), preferred_element_type=F32
    )
    rank = jnp.sum(onehot * counts, axis=0, keepdims=True).astype(jnp.int32)
    target = dest_row * capacity + rank
    return lax.broadcasted_iota(jnp.int32, (slots, rows), 0) == target


def gather_kernel(offsets_ref, grad_ref, out_ref):
    length, slots = grad_ref.shape[0], offsets_ref.shape[1]
    pick = lax.broadcasted_iota(jnp.int32, (length, slots), 0) == offsets_ref[...]
    pick = jnp.where(pick, 1.0, 0.0).astype(BF16)
    out_ref[...] = lax.dot_general(
        pick, grad_ref[...], (((0,), (0,)), ((), ())), preferred_element_type=F32
    ).astype(BF16)


def owner_rows_kernel(groups, capacity, dest_ref, arrived_ref, out_ref):
    slots = arrived_ref.shape[0]
    pick = rows_by_target(dest_ref[...], groups, capacity, slots)
    pick = jnp.where(pick, 1.0, 0.0).astype(BF16)
    rows = lax.dot_general(
        pick, arrived_ref[...], (((0,), (0,)), ((), ())), preferred_element_type=F32
    ).astype(BF16)
    for j in range(out_ref.shape[0]):
        out_ref[j] = rows


def route_kernel(groups, capacity, dest_ref, terms_ref, out_ref):
    slots = out_ref.shape[0]
    total = terms_ref[0].astype(F32)
    for j in range(1, terms_ref.shape[0]):
        total += terms_ref[j].astype(F32)
    hit = rows_by_target(dest_ref[...], groups, capacity, slots)
    pick = jnp.where(hit, 1.0, 0.0)
    sent = jnp.dot(pick.astype(BF16), total.astype(BF16), preferred_element_type=F32)
    used = jnp.sum(pick, axis=1, keepdims=True)
    out_ref[...] = jnp.where(used > 0.5, sent, EMPTY).astype(BF16)


def place_kernel(offsets_ref, arrived_ref, text_ref, out_ref):
    length, slots = text_ref.shape[0], offsets_ref.shape[1]
    arrived = arrived_ref[...].astype(F32)
    used = arrived[:, 0:1] < LIMIT
    rows = jnp.where(used, arrived, 0.0).astype(BF16)
    marks = jnp.where(jnp.broadcast_to(used, (slots, 128)), 1.0, 0.0).astype(BF16)
    pick = lax.broadcasted_iota(jnp.int32, (length, slots), 0) == offsets_ref[...]
    pick = jnp.where(pick, 1.0, 0.0).astype(BF16)
    placed = jnp.dot(pick, rows, preferred_element_type=F32)
    filled = jnp.dot(pick, marks, preferred_element_type=F32)[:, 0:1] > 0.5
    out_ref[...] = jnp.where(filled, placed, text_ref[...].astype(F32)).astype(BF16)


def forward_first_kernel(at_ref, own_ref, other_ref, w_own_ref, w_other_ref, out_ref, act_ref):
    half = own_ref.shape[1]

    @pl.when(pl.program_id(0) == 0)
    def _():
        act_ref[:, :half] = gelu(own_ref[...].astype(F32)).astype(BF16)
        act_ref[:, half:] = gelu(other_ref[...].astype(F32)).astype(BF16)

    total = jnp.dot(act_ref[:, :half], w_own_ref[...], preferred_element_type=F32)
    total += jnp.dot(act_ref[:, half:], w_other_ref[...], preferred_element_type=F32)
    out_ref[0] = total.astype(BF16)


def forward_second_kernel(at_ref, act_ref, w_own_ref, w_other_ref, out_ref):
    half = w_own_ref.shape[0]
    total = jnp.dot(act_ref[:, :half], w_own_ref[...], preferred_element_type=F32)
    total += jnp.dot(act_ref[:, half:], w_other_ref[...], preferred_element_type=F32)
    out_ref[0] = total.astype(BF16)


TRANS = (((1,), (1,)), ((), ()))


def backward_first_kernel(at_ref, grad_ref, w_own_ref, w_other_ref, own_ref, other_ref):
    own = lax.dot_general(grad_ref[0], w_own_ref[...], TRANS, preferred_element_type=F32)
    other = lax.dot_general(grad_ref[0], w_other_ref[...], TRANS, preferred_element_type=F32)

    @pl.when(pl.program_id(0) == 0)
    def _():
        own_ref[...] = own
        other_ref[...] = other

    @pl.when(pl.program_id(0) > 0)
    def _():
        own_ref[...] += own
        other_ref[...] += other


def backward_second_kernel(
    at_ref, grad_ref, w_own_ref, w_other_ref, own_in, other_in, own_ref, other_ref, total_ref
):
    own = lax.dot_general(grad_ref[0], w_own_ref[...], TRANS, preferred_element_type=F32)
    other = lax.dot_general(grad_ref[0], w_other_ref[...], TRANS, preferred_element_type=F32)

    @pl.when(pl.program_id(0) == 0)
    def _():
        own_ref[...] = own_in[...] + own
        total_ref[...] = other_in[...] + other

    @pl.when(pl.program_id(0) > 0)
    def _():
        own_ref[...] += own
        total_ref[...] += other

    @pl.when(pl.program_id(0) == pl.num_programs(0) - 1)
    def _():
        other_ref[...] = total_ref[...].astype(BF16)


def slope_kernel(own_ref, other_ref, pre_ref, out_ref):
    total = own_ref[...] + other_ref[...].astype(F32)
    out_ref[...] = (total * gelu_slope(pre_ref[...].astype(F32))).astype(BF16)


def call(kernel, out, *args, **kw):
    return pl.pallas_call(kernel, out_shape=jax.ShapeDtypeStruct(*out), **kw)(*args)


def on_device(lines, pre_hidden, proj_weight, text_embed, routes_dest, place, grad_packed):
    groups = lax.axis_size("group")
    slots = place.shape[1]
    capacity = slots // groups
    rows, hid = pre_hidden.shape
    width = text_embed.shape[1]
    half = lines // 2
    line, core = lax.axis_index("line"), lax.axis_index("core")
    parity = lax.rem(line, 2)
    same = (2 * parity + core).astype(jnp.int32).reshape(1)
    opposite = (2 * (1 - parity) + core).astype(jnp.int32).reshape(1)
    dest_row = routes_dest.reshape(1, rows)

    cores = [(0, 1), (1, 0)]
    beside = []
    for i in range(lines):
        for c in range(2):
            odd = (i + c) % 2
            beside.append((2 * i + c, 2 * ((i + (-1 if odd else 1)) % lines) + c))
    alike = [list(range(0, lines, 2)), list(range(1, lines, 2))]

    def exchange(x):
        return lax.all_to_all(
            x.reshape(groups, capacity, width), "group", split_axis=0, concat_axis=0, tiled=True
        ).reshape(slots, width)

    slot_grad = call(gather_kernel, ((slots, width), BF16), place, grad_packed)
    returned = exchange(slot_grad)

    pre_other = lax.ppermute(pre_hidden, "core", cores)
    w_other = lax.ppermute(proj_weight, "core", cores)

    w_spec = pl.BlockSpec((hid, width), lambda j, at: (0, 4 * j + at[0]))
    whole = lambda shape: pl.BlockSpec(shape, lambda j, at: (0,) * len(shape))
    term = pl.BlockSpec((1, rows, width), lambda j, at: (j, 0, 0))
    flops = 2 * half * rows * width * 2 * hid
    cost = pl.CostEstimate(flops=flops, bytes_accessed=2 * half * hid * width * 2, transcendentals=0)
    sent, act = pl.pallas_call(
        forward_first_kernel,
        grid_spec=pltpu.PrefetchScalarGridSpec(
            num_scalar_prefetch=1,
            grid=(half,),
            in_specs=[whole((rows, hid)), whole((rows, hid)), w_spec, w_spec],
            out_specs=[term, whole((rows, 2 * hid))],
        ),
        out_shape=[
            jax.ShapeDtypeStruct((half, rows, width), BF16),
            jax.ShapeDtypeStruct((rows, 2 * hid), BF16),
        ],
        cost_estimate=cost,
    )(opposite, pre_hidden, pre_other, proj_weight, w_other)
    beside_terms = lax.ppermute(sent, ("line", "core"), beside)
    kept = pl.pallas_call(
        forward_second_kernel,
        grid_spec=pltpu.PrefetchScalarGridSpec(
            num_scalar_prefetch=1,
            grid=(half,),
            in_specs=[whole((rows, 2 * hid)), w_spec, w_spec],
            out_specs=term,
        ),
        out_shape=jax.ShapeDtypeStruct((half, rows, width), BF16),
        cost_estimate=cost,
    )(same, act, proj_weight, w_other)
    terms = (kept.astype(F32) + beside_terms.astype(F32)).astype(BF16)
    terms = lax.all_to_all(
        terms, "line", split_axis=0, concat_axis=0, tiled=True, axis_index_groups=alike
    )
    outgoing = call(
        functools.partial(route_kernel, groups, capacity), ((slots, width), BF16), dest_row, terms
    )
    arrived = exchange(outgoing)

    mine = call(
        functools.partial(owner_rows_kernel, groups, capacity),
        ((half, rows, width), BF16),
        dest_row,
        returned,
    )
    near = lax.all_to_all(
        mine, "line", split_axis=0, concat_axis=0, tiled=True, axis_index_groups=alike
    )
    far = lax.ppermute(near, ("line", "core"), beside)
    total = whole((rows, hid))
    own, other = pl.pallas_call(
        backward_first_kernel,
        grid_spec=pltpu.PrefetchScalarGridSpec(
            num_scalar_prefetch=1,
            grid=(half,),
            in_specs=[term, w_spec, w_spec],
            out_specs=[total, total],
        ),
        out_shape=[jax.ShapeDtypeStruct((rows, hid), F32)] * 2,
        cost_estimate=cost,
    )(same, near, proj_weight, w_other)
    own, other = pl.pallas_call(
        backward_second_kernel,
        grid_spec=pltpu.PrefetchScalarGridSpec(
            num_scalar_prefetch=1,
            grid=(half,),
            in_specs=[term, w_spec, w_spec, total, total],
            out_specs=[total, total],
            scratch_shapes=[pltpu.VMEM((rows, hid), F32)],
        ),
        out_shape=[
            jax.ShapeDtypeStruct((rows, hid), F32),
            jax.ShapeDtypeStruct((rows, hid), BF16),
        ],
        cost_estimate=cost,
    )(opposite, far, proj_weight, w_other, own, other)
    other = lax.ppermute(other, "core", cores)
    grad_hidden = call(slope_kernel, ((rows, hid), BF16), own, other, pre_hidden)

    packed = call(place_kernel, (text_embed.shape, BF16), place, arrived, text_embed)
    return (packed, grad_hidden)


def solution(mesh):
    groups, lines = mesh.shape["group"], mesh.shape["tensor"] // 2
    chips = Mesh(mesh.devices.reshape(groups, lines, 2), ("group", "line", "core"))
    tensor = ("line", "core")
    return jax.shard_map(
        functools.partial(on_device, lines),
        mesh=chips,
        in_specs=(
            P("group", tensor),
            P(tensor, None),
            P("group", tensor),
            P("group", None),
            P("group", None),
            P("group", tensor),
        ),
        out_specs=(P("group", tensor), P("group", tensor)),
        check_vma=False,
    )
```

time: 150 us -> 142 us (0.947)
  the two profiles are of different devices: /device:TPU:1 before, /device:TPU:14 now
where the time goes in v1:
time: 142 us; the launch traced here: 141 us
  starting transfers between devices  54.4 us (38%)
  waiting for transfers between devices  45.4 us (32%)
  Pallas kernels  30.2 us (21%)
  local copies, waits for them, and re-layouts  8.19 us (6%)
  other arithmetic  2.02 us (1%)
    all_to_all x2, starting transfers between devices, exchange(): lax.all_to_all(x.reshape(groups, capacity, width), 'group', split_axis=0,...  29.8 us
    all_to_all x2, waiting for transfers between devices, exchange(): lax.all_to_all(x.reshape(groups, capacity, width), 'group', split_axis=0,...  22.9 us
    all_to_all x1, waiting for transfers between devices, on_device(): lax.all_to_all(terms, 'line', split_axis=0, concat_axis=0, tiled=True, ax...  14.3 us
    pallas_call x5, Pallas kernels, call(): pl.pallas_call(kernel, out_shape=jax.ShapeDtypeStruct(*out), **kw)(*args)  10.5 us
    ppermute x1, waiting for transfers between devices, on_device(): beside_terms = lax.ppermute(sent, ('line', 'core'), beside)  6.57 us
    all_to_all x1, starting transfers between devices, on_device(): lax.all_to_all(mine, 'line', split_axis=0, concat_axis=0, tiled=True, axi...  6.19 us
    all_to_all x1, starting transfers between devices, on_device(): lax.all_to_all(terms, 'line', split_axis=0, concat_axis=0, tiled=True, ax...  6.01 us
    pallas_call x1, Pallas kernels, on_device(): pl.pallas_call(backward_second_kernel, grid_spec=pltpu.PrefetchScalarGrid...  5.39 us
  transfers between devices with their start and end apart: 9, of which 5 were waited for; matrix products, arithmetic and copies ran while one was open for 5% of the time, Pallas kernels for 20%

profile of v1, /device:TPU:14, one launch (start us, length us, event | category | flops | bytes accessed | tf_op | source)
XLA Modules:
  0.0 140.9 jit_solution(6586933920107065714)
XLA Ops:
  0.6 2.1 %collective-permute-start.1 = (bf16[512,8192]{1,0:T(8,128)(2,1)}, bf16[512,8192]{1,0:T(8,128)(2,1)}, u32[]{:S(2)}, u32[]{:S(2)}) collective-permute-start(bf16[512,8192]{1,0:T(8,128)(2,1)} %w_own_ref.7), channel_id=1, source_target_pairs={{0,1},{1,0},{2,3},{3,2},{4,5},{5,4},{6,7},{7,6},{8,9},{9,8},{10,11... | collective-permute-start | bytes 25165832 | tf_op jit(solution)/shard_map/ppermute | solution.py:185
  2.7 2.0 %shard_map.81 = bf16[192,512]{1,0:T(8,128)(2,1)} custom-call(s32[1,192]{1,0:T(1,128)} %offsets_ref.3, bf16[384,512]{1,0:T(8,128)(2,1)} %grad_ref.1), custom_call_target="tpu_custom_call" | custom-call | tf_op jit(solution)/shard_map/pallas_call | solution.py:152
  4.7 1.7 %reshape.30 = bf16[64,3,512]{2,1,0:T(4,128)(2,1)} reshape(bf16[192,512]{1,0:T(8,128)(2,1)} %shard_map.81) | data formatting | bytes 393216 | tf_op jit(solution)/shard_map/reshape | solution.py:178
  6.4 22.5 %all-to-all-start.2 = ((bf16[64,3,512]{2,1,0:T(4,128)(2,1)}), bf16[64,3,512]{2,1,0:T(4,128)(2,1)S(1)}, u32[]{:S(2)}, u32[]{:S(2)}) async-start(bf16[64,3,512]{2,1,0:T(4,128)(2,1)} %reshape.30), calls=%async_computation.2 | async-start | bytes 524288 | tf_op jit(solution)/shard_map/all_to_all | solution.py:177
  28.9 1.9 %collective-permute-start = (bf16[144,512]{1,0:T(8,128)(2,1)S(1)}, bf16[144,512]{1,0:T(8,128)(2,1)S(1)}, u32[]{:S(2)}, u32[]{:S(2)}) collective-permute-start(bf16[144,512]{1,0:T(8,128)(2,1)S(1)} %copy-done.2), channel_id=1, source_target_pairs={{0,1},{1,0},{2,3},{3,2},{4,5},{5,4},{6,7},{7,6},{8,9},{9,8},{10,11... | collective-permute-start | bytes 442376 | tf_op jit(solution)/shard_map/ppermute | solution.py:184
  30.8 19.6 %all-to-all-done.2 = bf16[64,3,512]{2,1,0:T(4,128)(2,1)S(1)} async-done(((bf16[64,3,512]{2,1,0:T(4,128)(2,1)}), bf16[64,3,512]{2,1,0:T(4,128)(2,1)S(1)}, u32[]{:S(2)}, u32[]{:S(2)}) %all-to-all-start.2) | async-done | bytes 196640 | tf_op jit(solution)/shard_map/all_to_all | solution.py:177
  51.3 2.2 %shard_map.82 = bf16[4,144,512]{2,1,0:T(8,128)(2,1)} custom-call(s32[1,144]{1,0:T(1,128)} %bitcast.3, bf16[192,512]{1,0:T(8,128)(2,1)} %reshape.31.arrived_ref), custom_call_target="tpu_custom_call" | custom-call | tf_op jit(solution)/shard_map/pallas_call | solution.py:152
  53.5 6.2 %all-to-all-start.3 = ((bf16[4,144,512]{2,1,0:T(8,128)(2,1)}), bf16[4,144,512]{2,1,0:T(8,128)(2,1)S(1)}, u32[]{:S(2)}, u32[]{:S(2)}) async-start(bf16[4,144,512]{2,1,0:T(8,128)(2,1)} %shard_map.82), calls=%async_computation.3 | async-start | bytes 1179648 | tf_op jit(solution)/shard_map/all_to_all | solution.py:233
  60.3 4.7 %shard_map.77 = (bf16[4,144,512]{2,1,0:T(8,128)(2,1)}, bf16[144,1024]{1,0:T(8,128)(2,1)}) custom-call(s32[1]{0:T(128)} %bitcast.2.at_ref, bf16[144,512]{1,0:T(8,128)(2,1)} %pre_ref.1, bf16[144,512]{1,0:T(8,128)(2,1)} %copy-done.4, bf16[512,8192]{1,0:T(8,128)(2,1)} %w_own_ref.7, bf16[512,8192]{1,0:T(8,128)(2,1)} %collective-permute-done.1.w_other_ref), custom_call_target="tpu_custom_call" | custom-call | flops 603979776 | bytes 4194304 | tf_op jit(solution)/shard_map/pallas_call | solution.py:192
  65.0 3.2 %collective-permute-start.2 = (bf16[4,144,512]{2,1,0:T(8,128)(2,1)}, bf16[4,144,512]{2,1,0:T(8,128)(2,1)S(1)}, u32[]{:S(2)}, u32[]{:S(2)}) collective-permute-start(bf16[4,144,512]{2,1,0:T(8,128)(2,1)} %get-tuple-element.9), channel_id=1, source_target_pairs={{0,2},{1,15},{2,0},{3,5},{4,6},{5,3},{6,4},{7,9},{8,10},{9,7},{10,... | collective-permute-start | bytes 1769480 | tf_op jit(solution)/shard_map/ppermute | solution.py:206
  68.2 4.6 %shard_map.78 = bf16[4,144,512]{2,1,0:T(8,128)(2,1)} custom-call(s32[1]{0:T(128)} %bitcast.1.at_ref, bf16[144,1024]{1,0:T(8,128)(2,1)} %get-tuple-element.8.act_ref, bf16[512,8192]{1,0:T(8,128)(2,1)} %w_own_ref.7, bf16[512,8192]{1,0:T(8,128)(2,1)} %collective-permute-done.1.w_other_ref), custom_call_target="tpu_custom_call" | custom-call | flops 603979776 | bytes 4194304 | tf_op jit(solution)/shard_map/pallas_call | solution.py:207
  72.8 6.6 %collective-permute-done.2 = bf16[4,144,512]{2,1,0:T(8,128)(2,1)S(1)} collective-permute-done((bf16[4,144,512]{2,1,0:T(8,128)(2,1)}, bf16[4,144,512]{2,1,0:T(8,128)(2,1)S(1)}, u32[]{:S(2)}, u32[]{:S(2)}) %collective-permute-start.2) | collective-permute-done | bytes 589856 | tf_op jit(solution)/shard_map/ppermute | solution.py:206
  79.4 2.0 %add_convert_fusion = bf16[4,144,512]{2,1,0:T(8,128)(2,1)} fusion(bf16[4,144,512]{2,1,0:T(8,128)(2,1)S(1)} %collective-permute-done.2, bf16[4,144,512]{2,1,0:T(8,128)(2,1)} %shard_map.78), kind=kLoop, calls=%fused_computation | loop fusion | flops 1179648 | bytes 1769472 | tf_op jit(solution)/shard_map/convert_element_type | solution.py:218
  81.4 6.0 %all-to-all-start = ((bf16[4,144,512]{2,1,0:T(8,128)(2,1)}), bf16[4,144,512]{2,1,0:T(8,128)(2,1)S(1)}, u32[]{:S(2)}, u32[]{:S(2)}) async-start(bf16[4,144,512]{2,1,0:T(8,128)(2,1)} %add_convert_fusion), calls=%async_computation | async-start | bytes 1179648 | tf_op jit(solution)/shard_map/all_to_all | solution.py:219
  87.4 3.2 %collective-permute-start.3 = (bf16[4,144,512]{2,1,0:T(8,128)(2,1)S(1)}, bf16[4,144,512]{2,1,0:T(8,128)(2,1)S(1)}, u32[]{:S(2)}, u32[]{:S(2)}) collective-permute-start(bf16[4,144,512]{2,1,0:T(8,128)(2,1)S(1)} %all-to-all-done.3.grad_ref), channel_id=1, source_target_pairs={{0,2},{1,15},{2,0},{3,5},{4,6},{5,3},{6,4},{7,9},{8,10},{9,7},{10,... | collective-permute-start | bytes 1769480 | tf_op jit(solution)/shard_map/ppermute | solution.py:236
  90.7 14.3 %all-to-all-done.terms_ref = bf16[4,144,512]{2,1,0:T(8,128)(2,1)S(1)} async-done(((bf16[4,144,512]{2,1,0:T(8,128)(2,1)}), bf16[4,144,512]{2,1,0:T(8,128)(2,1)S(1)}, u32[]{:S(2)}, u32[]{:S(2)}) %all-to-all-start) | async-done | bytes 589856 | tf_op jit(solution)/shard_map/all_to_all | solution.py:219
  105.8 2.1 %shard_map.79 = bf16[192,512]{1,0:T(8,128)(2,1)} custom-call(s32[1,144]{1,0:T(1,128)} %bitcast.4, bf16[4,144,512]{2,1,0:T(8,128)(2,1)} %copy-done.1), custom_call_target="tpu_custom_call" | custom-call | tf_op jit(solution)/shard_map/pallas_call | solution.py:152
  109.7 7.3 %all-to-all-start.1 = ((bf16[64,3,512]{2,1,0:T(4,128)(2,1)}), bf16[64,3,512]{2,1,0:T(4,128)(2,1)S(1)}, u32[]{:S(2)}, u32[]{:S(2)}) async-start(bf16[64,3,512]{2,1,0:T(4,128)(2,1)} %reshape.28), calls=%async_computation.1 | async-start | bytes 524288 | tf_op jit(solution)/shard_map/all_to_all | solution.py:177
  117.0 5.1 %shard_map.83 = (f32[144,512]{1,0:T(8,128)}, f32[144,512]{1,0:T(8,128)}) custom-call(s32[1]{0:T(128)} %bitcast.1.at_ref, bf16[4,144,512]{2,1,0:T(8,128)(2,1)} %copy-done, bf16[512,8192]{1,0:T(8,128)(2,1)} %w_own_ref.7, bf16[512,8192]{1,0:T(8,128)(2,1)} %collective-permute-done.1.w_other_ref), custom_call_target="tpu_custom_call" | custom-call | flops 603979776 | bytes 4194304 | tf_op jit(solution)/shard_map/pallas_call | solution.py:238
  123.0 5.4 %shard_map.84 = (f32[144,512]{1,0:T(8,128)}, bf16[144,512]{1,0:T(8,128)(2,1)}) custom-call(s32[1]{0:T(128)} %bitcast.2.at_ref, bf16[4,144,512]{2,1,0:T(8,128)(2,1)} %copy-done.3, bf16[512,8192]{1,0:T(8,128)(2,1)} %w_own_ref.7, bf16[512,8192]{1,0:T(8,128)(2,1)} %collective-permute-done.1.w_other_ref, f32[144,512]{1,0:T(8,128)} %get-tuple-element.10.own_in, ...), custom_call_target="tpu_custom_call" | custom-call | flops 603979776 | bytes 4194304 | tf_op jit(solution)/shard_map/pallas_call | solution.py:249
  128.4 1.9 %collective-permute-start.4 = (bf16[144,512]{1,0:T(8,128)(2,1)}, bf16[144,512]{1,0:T(8,128)(2,1)S(1)}, u32[]{:S(2)}, u32[]{:S(2)}) collective-permute-start(bf16[144,512]{1,0:T(8,128)(2,1)} %get-tuple-element.13), channel_id=1, source_target_pairs={{0,1},{1,0},{2,3},{3,2},{4,5},{5,4},{6,7},{7,6},{8,9},{9,8},{10,11... | collective-permute-start | bytes 442376 | tf_op jit(solution)/shard_map/ppermute | solution.py:264
  132.5 1.9 %shard_map.85 = bf16[144,512]{1,0:T(8,128)(2,1)} custom-call(f32[144,512]{1,0:T(8,128)} %get-tuple-element.12.own_ref, bf16[144,512]{1,0:T(8,128)(2,1)} %copy-done.5, bf16[144,512]{1,0:T(8,128)(2,1)} %pre_ref.1), custom_call_target="tpu_custom_call" | custom-call | tf_op jit(solution)/shard_map/pallas_call | solution.py:152
  134.4 3.3 %all-to-all-done.1 = bf16[64,3,512]{2,1,0:T(4,128)(2,1)S(1)} async-done(((bf16[64,3,512]{2,1,0:T(4,128)(2,1)}), bf16[64,3,512]{2,1,0:T(4,128)(2,1)S(1)}, u32[]{:S(2)}, u32[]{:S(2)}) %all-to-all-start.1) | async-done | bytes 196640 | tf_op jit(solution)/shard_map/all_to_all | solution.py:177
  138.5 2.3 %shard_map.80 = bf16[384,512]{1,0:T(8,128)(2,1)} custom-call(s32[1,192]{1,0:T(1,128)} %offsets_ref.3, bf16[192,512]{1,0:T(8,128)(2,1)} %reshape.29.arrived_ref, bf16[384,512]{1,0:T(8,128)(2,1)} %text_ref.1), custom_call_target="tpu_custom_call" | custom-call | tf_op jit(solution)/shard_map/pallas_call | solution.py:152
  (20 shorter events, 8.0 us)
Async XLA Ops:
  0.6 28.3 %copy-start.2 = (bf16[144,512]{1,0:T(8,128)(2,1)S(1)}, bf16[144,512]{1,0:T(8,128)(2,1)}, u32[]{:S(2)}) copy-start(bf16[144,512]{1,0:T(8,128)(2,1)} %pre_ref.1) | copy-start | bytes 442372
  0.6 59.0 %collective-permute-start.1 = (bf16[512,8192]{1,0:T(8,128)(2,1)}, bf16[512,8192]{1,0:T(8,128)(2,1)}, u32[]{:S(2)}, u32[]{:S(2)}) collective-permute-start(bf16[512,8192]{1,0:T(8,128)(2,1)} %w_own_ref.7), channel_id=1, source_target_pairs={{0,1},{1,0},{2,3},{3,2},{4,5},{5,4},{6,7},{7,6},{8,9},{9,8},{10,11... | collective-permute-start | bytes 25165832 | tf_op jit(solution)/shard_map/ppermute | solution.py:185
  6.4 44.0 %all-to-all-start.2 = ((bf16[64,3,512]{2,1,0:T(4,128)(2,1)}), bf16[64,3,512]{2,1,0:T(4,128)(2,1)S(1)}, u32[]{:S(2)}, u32[]{:S(2)}) async-start(bf16[64,3,512]{2,1,0:T(4,128)(2,1)} %reshape.30), calls=%async_computation.2 | async-start | bytes 524288 | tf_op jit(solution)/shard_map/all_to_all | solution.py:177
  28.9 30.8 %collective-permute-start = (bf16[144,512]{1,0:T(8,128)(2,1)S(1)}, bf16[144,512]{1,0:T(8,128)(2,1)S(1)}, u32[]{:S(2)}, u32[]{:S(2)}) collective-permute-start(bf16[144,512]{1,0:T(8,128)(2,1)S(1)} %copy-done.2), channel_id=1, source_target_pairs={{0,1},{1,0},{2,3},{3,2},{4,5},{5,4},{6,7},{7,6},{8,9},{9,8},{10,11... | collective-permute-start | bytes 442376 | tf_op jit(solution)/shard_map/ppermute | solution.py:184
  53.5 27.9 %all-to-all-start.3 = ((bf16[4,144,512]{2,1,0:T(8,128)(2,1)}), bf16[4,144,512]{2,1,0:T(8,128)(2,1)S(1)}, u32[]{:S(2)}, u32[]{:S(2)}) async-start(bf16[4,144,512]{2,1,0:T(8,128)(2,1)} %shard_map.82), calls=%async_computation.3 | async-start | bytes 1179648 | tf_op jit(solution)/shard_map/all_to_all | solution.py:233
  59.7 0.7 copy-start.4
  65.0 14.4 %collective-permute-start.2 = (bf16[4,144,512]{2,1,0:T(8,128)(2,1)}, bf16[4,144,512]{2,1,0:T(8,128)(2,1)S(1)}, u32[]{:S(2)}, u32[]{:S(2)}) collective-permute-start(bf16[4,144,512]{2,1,0:T(8,128)(2,1)} %get-tuple-element.9), channel_id=1, source_target_pairs={{0,2},{1,15},{2,0},{3,5},{4,6},{5,3},{6,4},{7,9},{8,10},{9,7},{10,... | collective-permute-start | bytes 1769480 | tf_op jit(solution)/shard_map/ppermute | solution.py:206
  81.4 28.3 %copy-start = (bf16[4,144,512]{2,1,0:T(8,128)(2,1)}, bf16[4,144,512]{2,1,0:T(8,128)(2,1)S(1)}, u32[]{:S(2)}) copy-start(bf16[4,144,512]{2,1,0:T(8,128)(2,1)S(1)} %all-to-all-done.3.grad_ref) | copy-start | bytes 1769476
  81.4 23.6 %all-to-all-start = ((bf16[4,144,512]{2,1,0:T(8,128)(2,1)}), bf16[4,144,512]{2,1,0:T(8,128)(2,1)S(1)}, u32[]{:S(2)}, u32[]{:S(2)}) async-start(bf16[4,144,512]{2,1,0:T(8,128)(2,1)} %add_convert_fusion), calls=%async_computation | async-start | bytes 1179648 | tf_op jit(solution)/shard_map/all_to_all | solution.py:219
  87.4 34.7 %collective-permute-start.3 = (bf16[4,144,512]{2,1,0:T(8,128)(2,1)S(1)}, bf16[4,144,512]{2,1,0:T(8,128)(2,1)S(1)}, u32[]{:S(2)}, u32[]{:S(2)}) collective-permute-start(bf16[4,144,512]{2,1,0:T(8,128)(2,1)S(1)} %all-to-all-done.3.grad_ref), channel_id=1, source_target_pairs={{0,2},{1,15},{2,0},{3,5},{4,6},{5,3},{6,4},{7,9},{8,10},{9,7},{10,... | collective-permute-start | bytes 1769480 | tf_op jit(solution)/shard_map/ppermute | solution.py:236
  105.0 0.8 copy-start.1
  109.7 28.0 %all-to-all-start.1 = ((bf16[64,3,512]{2,1,0:T(4,128)(2,1)}), bf16[64,3,512]{2,1,0:T(4,128)(2,1)S(1)}, u32[]{:S(2)}, u32[]{:S(2)}) async-start(bf16[64,3,512]{2,1,0:T(4,128)(2,1)} %reshape.28), calls=%async_computation.1 | async-start | bytes 524288 | tf_op jit(solution)/shard_map/all_to_all | solution.py:177
  122.1 0.9 copy-start.3
  128.4 3.5 %collective-permute-start.4 = (bf16[144,512]{1,0:T(8,128)(2,1)}, bf16[144,512]{1,0:T(8,128)(2,1)S(1)}, u32[]{:S(2)}, u32[]{:S(2)}) collective-permute-start(bf16[144,512]{1,0:T(8,128)(2,1)} %get-tuple-element.13), channel_id=1, source_target_pairs={{0,1},{1,0},{2,3},{3,2},{4,5},{5,4},{6,7},{7,6},{8,9},{9,8},{10,11... | collective-permute-start | bytes 442376 | tf_op jit(solution)/shard_map/ppermute | solution.py:264
  131.8 0.7 copy-start.5

commit v2 on v1

v2 whole, which is shorter than its diff:
```python
import functools

import jax
import jax.numpy as jnp
from jax import lax
from jax.experimental import pallas as pl
from jax.experimental.pallas import tpu as pltpu
from jax.sharding import Mesh
from jax.sharding import PartitionSpec as P

BF16 = jnp.bfloat16
F32 = jnp.float32
EMPTY = 1.7e38
LIMIT = 1.0e38


def gelu(values):
    return values * 0.5 * (1.0 + lax.erf(values * 0.7071067811865476))


def gelu_slope(values):
    cdf = 0.5 * (1.0 + lax.erf(values * 0.7071067811865476))
    dens = jnp.exp(-0.5 * values * values) * 0.3989422804014327
    return cdf + values * dens


def rows_by_target(dest_row, groups, capacity, slots):
    rows = dest_row.shape[1]
    hit = lax.broadcasted_iota(jnp.int32, (groups, rows), 0) == dest_row
    before = lax.broadcasted_iota(jnp.int32, (rows, rows), 0) < lax.broadcasted_iota(
        jnp.int32, (rows, rows), 1
    )
    onehot = jnp.where(hit, 1.0, 0.0)
    counts = jnp.dot(
        onehot.astype(BF16), jnp.where(before, 1.0, 0.0).astype(BF16), preferred_element_type=F32
    )
    rank = jnp.sum(onehot * counts, axis=0, keepdims=True).astype(jnp.int32)
    target = dest_row * capacity + rank
    return lax.broadcasted_iota(jnp.int32, (slots, rows), 0) == target


def gather_kernel(offsets_ref, grad_ref, out_ref):
    length, slots = grad_ref.shape[0], offsets_ref.shape[1]
    pick = lax.broadcasted_iota(jnp.int32, (length, slots), 0) == offsets_ref[...]
    pick = jnp.where(pick, 1.0, 0.0).astype(BF16)
    out_ref[...] = lax.dot_general(
        pick, grad_ref[...], (((0,), (0,)), ((), ())), preferred_element_type=F32
    ).astype(BF16)


def owner_rows_kernel(groups, capacity, dest_ref, arrived_ref, token_ref, out_ref):
    slots = arrived_ref.shape[0]
    pick = rows_by_target(dest_ref[...], groups, capacity, slots)
    pick = jnp.where(pick, 1.0, 0.0).astype(BF16)
    rows = lax.dot_general(
        pick, arrived_ref[...], (((0,), (0,)), ((), ())), preferred_element_type=F32
    ).astype(BF16)
    out_ref[...] = rows


def route_kernel(groups, capacity, dest_ref, total_ref, *refs):
    term_refs, out_ref = refs[:-1], refs[-1]
    slots = out_ref.shape[0]
    total = total_ref[...]
    for term_ref in term_refs:
        total += term_ref[...].astype(F32)
    hit = rows_by_target(dest_ref[...], groups, capacity, slots)
    pick = jnp.where(hit, 1.0, 0.0)
    sent = jnp.dot(pick.astype(BF16), total.astype(BF16), preferred_element_type=F32)
    used = jnp.sum(pick, axis=1, keepdims=True)
    out_ref[...] = jnp.where(used > 0.5, sent, EMPTY).astype(BF16)


def place_kernel(offsets_ref, arrived_ref, text_ref, out_ref):
    length, slots = text_ref.shape[0], offsets_ref.shape[1]
    arrived = arrived_ref[...].astype(F32)
    used = arrived[:, 0:1] < LIMIT
    rows = jnp.where(used, arrived, 0.0).astype(BF16)
    marks = jnp.where(jnp.broadcast_to(used, (slots, 128)), 1.0, 0.0).astype(BF16)
    pick = lax.broadcasted_iota(jnp.int32, (length, slots), 0) == offsets_ref[...]
    pick = jnp.where(pick, 1.0, 0.0).astype(BF16)
    placed = jnp.dot(pick, rows, preferred_element_type=F32)
    filled = jnp.dot(pick, marks, preferred_element_type=F32)[:, 0:1] > 0.5
    out_ref[...] = jnp.where(filled, placed, text_ref[...].astype(F32)).astype(BF16)


TRANS = (((1,), (1,)), ((), ()))


def fetch(at_ref, sources, held_ref, sems):
    blocks, width = held_ref.shape[1], held_ref.shape[3]
    copies = []
    for j in range(blocks):
        columns = pl.ds(pl.multiple_of(at_ref[j] * width, width), width)
        pair = []
        for k, source in enumerate(sources):
            pair.append(
                pltpu.make_async_copy(source.at[:, columns], held_ref.at[k, j], sems.at[k, j])
            )
            pair[-1].start()
        copies.append(pair)
    return copies


def forward_first_kernel(
    at_ref, own_ref, other_ref, w_own_ref, w_other_ref, out_ref, act_ref, held_ref, sems
):
    copies = fetch(at_ref, (w_own_ref, w_other_ref), held_ref, sems)
    half = own_ref.shape[1]
    act_ref[:, :half] = gelu(own_ref[...].astype(F32)).astype(BF16)
    act_ref[:, half:] = gelu(other_ref[...].astype(F32)).astype(BF16)
    for j, pair in enumerate(copies):
        for copy in pair:
            copy.wait()
        total = jnp.dot(act_ref[:, :half], held_ref[0, j], preferred_element_type=F32)
        total += jnp.dot(act_ref[:, half:], held_ref[1, j], preferred_element_type=F32)
        out_ref[j] = total.astype(BF16)


def forward_second_kernel(at_ref, act_ref, w_own_ref, w_other_ref, out_ref, held_ref, sems):
    copies = fetch(at_ref, (w_own_ref, w_other_ref), held_ref, sems)
    half = held_ref.shape[2]
    for j, pair in enumerate(copies):
        for copy in pair:
            copy.wait()
        total = jnp.dot(act_ref[:, :half], held_ref[0, j], preferred_element_type=F32)
        total += jnp.dot(act_ref[:, half:], held_ref[1, j], preferred_element_type=F32)
        out_ref[j] = total.astype(BF16)


def add_kernel(kept_ref, beside_ref, token_ref, total_ref, *term_refs):
    token_ref[...] = jnp.zeros_like(token_ref)
    total_ref[...] = kept_ref[0].astype(F32) + beside_ref[0].astype(F32)
    for j, term_ref in enumerate(term_refs, 1):
        term_ref[...] = (kept_ref[j].astype(F32) + beside_ref[j].astype(F32)).astype(BF16)


def backward_first_kernel(blocks, at_ref, *refs):
    grad_refs, refs = refs[:blocks], refs[blocks:]
    pre_ref, w_own_ref, w_other_ref, own_ref, other_ref, slope_ref, held_ref, sems = refs
    copies = fetch(at_ref, (w_own_ref, w_other_ref), held_ref, sems)
    slope_ref[...] = gelu_slope(pre_ref[...].astype(F32))
    own, other = 0.0, 0.0
    for grad_ref, j, pair in zip(grad_refs, range(blocks), copies):
        for copy in pair:
            copy.wait()
        own += lax.dot_general(grad_ref[...], held_ref[0, j], TRANS, preferred_element_type=F32)
        other += lax.dot_general(grad_ref[...], held_ref[1, j], TRANS, preferred_element_type=F32)
    own_ref[...] = own
    other_ref[...] = other


def backward_second_kernel(
    at_ref, grad_ref, own_in, other_in, w_own_ref, w_other_ref, own_ref, other_ref, held_ref, sems
):
    copies = fetch(at_ref, (w_own_ref, w_other_ref), held_ref, sems)
    own, other = own_in[...], other_in[...]
    for j, pair in enumerate(copies):
        for copy in pair:
            copy.wait()
        own += lax.dot_general(grad_ref[j], held_ref[0, j], TRANS, preferred_element_type=F32)
        other += lax.dot_general(grad_ref[j], held_ref[1, j], TRANS, preferred_element_type=F32)
    own_ref[...] = own
    other_ref[...] = other.astype(BF16)


def slope_kernel(own_ref, other_ref, slope_ref, out_ref):
    total = own_ref[...] + other_ref[...].astype(F32)
    out_ref[...] = (total * slope_ref[...]).astype(BF16)


VMEM = pl.BlockSpec(memory_space=pltpu.VMEM)
HBM = pl.BlockSpec(memory_space=pltpu.HBM)
SMEM = pl.BlockSpec(memory_space=pltpu.SMEM)


def near_core(x):
    return pltpu.with_memory_space_constraint(x, pltpu.VMEM)


def in_hbm(x):
    return pltpu.with_memory_space_constraint(x, pltpu.HBM)


def call(kernel, outs, *args, final=False, first=False):
    out_shape = [jax.ShapeDtypeStruct(*o) if final else pltpu.VMEM(*o) for o in outs]
    got = pl.pallas_call(
        kernel,
        in_specs=[VMEM] * len(args),
        out_specs=[VMEM] * len(outs),
        out_shape=out_shape,
    )(*[a if first else near_core(a) for a in args])
    return got if len(outs) > 1 else got[0]


def product(kernel, outs, at, args, weights, blocks):
    hid, width = weights[0].shape[0], weights[0].shape[1] // (4 * blocks)
    rows = args[0].shape[-2]
    got = pl.pallas_call(
        kernel,
        in_specs=[SMEM] + [VMEM] * len(args) + [HBM] * 2,
        out_specs=[VMEM] * len(outs),
        out_shape=[pltpu.VMEM(*o) for o in outs],
        scratch_shapes=[
            pltpu.VMEM((2, blocks, hid, width), BF16),
            pltpu.SemaphoreType.DMA((2, blocks)),
        ],
        cost_estimate=pl.CostEstimate(
            flops=2 * rows * blocks * width * 2 * hid,
            bytes_accessed=4 * blocks * hid * width,
            transcendentals=0,
        ),
        compiler_params=pltpu.CompilerParams(vmem_limit_bytes=24 * 1024 * 1024),
    )(at, *[near_core(a) for a in args], *[in_hbm(w) for w in weights])
    return got if len(outs) > 1 else got[0]


def on_device(lines, pre_hidden, proj_weight, text_embed, routes_dest, place, grad_packed):
    groups = lax.axis_size("group")
    slots = place.shape[1]
    capacity = slots // groups
    rows, hid = pre_hidden.shape
    width = text_embed.shape[1]
    half = lines // 2
    line, core = lax.axis_index("line"), lax.axis_index("core")
    beside_line = line + 1 - 2 * lax.rem(line + core, 2) + lines
    steps = 2 * jnp.arange(half, dtype=jnp.int32)
    same = 2 * lax.rem(line + steps, lines) + core
    opposite = 2 * lax.rem(beside_line + steps, lines) + core
    dest_row = routes_dest.reshape(1, rows)

    cores = [(0, 1), (1, 0)]
    beside = []
    for i in range(lines):
        for c in range(2):
            odd = (i + c) % 2
            beside.append((2 * i + c, 2 * ((i + (-1 if odd else 1)) % lines) + c))

    def shift(x, by):
        return lax.ppermute(x, "line", [(i, (i + by) % lines) for i in range(lines)])

    def by_group(x):
        return x.reshape(groups, 4, capacity * width // 4)

    def exchange(x):
        x = lax.all_to_all(x, "group", split_axis=0, concat_axis=0, tiled=True)
        return x.reshape(slots, width)

    w_other = lax.ppermute(proj_weight, "core", cores)
    pre_other = lax.ppermute(pre_hidden, "core", cores)
    weights = (proj_weight, w_other)

    gathered = call(gather_kernel, [((slots, width), BF16)], place, grad_packed, first=True)
    returned = exchange(by_group(gathered))

    terms_out = ((half, rows, width), BF16)
    sent, act = product(
        forward_first_kernel,
        [terms_out, ((rows, 2 * hid), BF16)],
        opposite,
        (pre_hidden, pre_other),
        weights,
        half,
    )
    beside_terms = lax.ppermute(sent, ("line", "core"), beside)
    kept = product(forward_second_kernel, [terms_out], same, (act,), weights, half)
    token, total, *terms = call(
        add_kernel,
        [((8, 128), F32), ((rows, width), F32)] + [((rows, width), BF16)] * (half - 1),
        kept,
        beside_terms,
    )
    terms = [shift(term, 2 * j) for j, term in enumerate(terms, 1)]
    outgoing = call(
        functools.partial(route_kernel, groups, capacity),
        [((slots, width), BF16)],
        dest_row,
        total,
        *terms,
    )
    outgoing = by_group(outgoing)
    arrived = exchange(outgoing)

    mine = call(
        functools.partial(owner_rows_kernel, groups, capacity),
        [((rows, width), BF16)],
        dest_row,
        returned,
        token,
    )
    near = [mine] + [shift(mine, -2 * j) for j in range(1, half)]
    *near, _ = lax.optimization_barrier((*near, outgoing))
    far = lax.ppermute(jnp.stack(near), ("line", "core"), beside)
    wide = ((rows, hid), F32)
    own, other, slope = product(
        functools.partial(backward_first_kernel, half),
        [wide] * 3,
        same,
        (*near, pre_hidden),
        weights,
        half,
    )
    own, other = product(
        backward_second_kernel,
        [wide, ((rows, hid), BF16)],
        opposite,
        (far, own, other),
        weights,
        half,
    )
    other = lax.ppermute(other, "core", cores)
    grad_hidden = call(slope_kernel, [((rows, hid), BF16)], own, other, slope, final=True)

    packed = call(
        place_kernel, [(text_embed.shape, BF16)], place, arrived, text_embed, final=True
    )
    return (packed, grad_hidden)


def solution(mesh):
    groups, lines = mesh.shape["group"], mesh.shape["tensor"] // 2
    chips = Mesh(mesh.devices.reshape(groups, lines, 2), ("group", "line", "core"))
    tensor = ("line", "core")
    return jax.shard_map(
        functools.partial(on_device, lines),
        mesh=chips,
        in_specs=(
            P("group", tensor),
            P(tensor, None),
            P("group", tensor),
            P("group", None),
            P("group", None),
            P("group", tensor),
        ),
        out_specs=(P("group", tensor), P("group", tensor)),
        check_vma=False,
    )
```

time: 142 us -> 121 us (0.85)
  the two profiles are of different devices: /device:TPU:14 before, /device:TPU:24 now
where the time goes in v2:
time: 121 us
  starting transfers between devices  75 us (62%)
  waiting for transfers between devices  24.3 us (20%)
  Pallas kernels  17.5 us (14%)
  local copies, waits for them, and re-layouts  2.76 us (2%)
    all_to_all x2, starting transfers between devices, exchange(): x = lax.all_to_all(x, 'group', split_axis=0, concat_axis=0, tiled=True)  36.8 us
    ppermute x6, starting transfers between devices, shift(): lax.ppermute(x, 'line', [(i, (i + by) % lines) for i in range(lines)])  24.4 us
    pallas_call x4, Pallas kernels, product(): pl.pallas_call(kernel, in_specs=[SMEM] + [VMEM] * len(args) + [HBM] * 2,...  13.4 us
    ppermute x6, waiting for transfers between devices, shift(): lax.ppermute(x, 'line', [(i, (i + by) % lines) for i in range(lines)])  8.97 us
    all_to_all x2, waiting for transfers between devices, exchange(): x = lax.all_to_all(x, 'group', split_axis=0, concat_axis=0, tiled=True)  8.11 us
    ppermute x1, waiting for transfers between devices, on_device(): beside_terms = lax.ppermute(sent, ('line', 'core'), beside)  6.23 us
    ppermute x1, starting transfers between devices, on_device(): far = lax.ppermute(jnp.stack(near), ('line', 'core'), beside)  4.3 us
    pallas_call x6, Pallas kernels, call(): pl.pallas_call(kernel, in_specs=[VMEM] * len(args), out_specs=[VMEM] * le...  4.11 us
  transfers between devices with their start and end apart: 13, of which 5 were waited for; matrix products, arithmetic and copies ran while one was open for 1% of the time, Pallas kernels for 14%

profile of v2, /device:TPU:24, one launch (start us, length us, event | category | flops | bytes accessed | tf_op | source)
XLA Modules:
  0.0 120.6 jit_solution(17113167492961487988)
XLA Ops:
  0.6 1.9 %collective-permute-start.1 = (bf16[512,8192]{1,0:T(8,128)(2,1)}, bf16[512,8192]{1,0:T(8,128)(2,1)}, u32[]{:S(2)}, u32[]{:S(2)}) collective-permute-start(bf16[512,8192]{1,0:T(8,128)(2,1)} %w_own_ref.5), channel_id=1, source_target_pairs={{0,1},{1,0},{2,3},{3,2},{4,5},{5,4},{6,7},{7,6},{8,9},{9,8},{10,11... | collective-permute-start | bytes 25165832 | tf_op jit(solution)/shard_map/ppermute | solution.py:249
  2.6 2.4 %collective-permute-start = (bf16[144,512]{1,0:T(8,128)(2,1)}, bf16[144,512]{1,0:T(8,128)(2,1)S(1)}, u32[]{:S(2)}, u32[]{:S(2)}) collective-permute-start(bf16[144,512]{1,0:T(8,128)(2,1)} %refs_4_.1), channel_id=1, source_target_pairs={{0,1},{1,0},{2,3},{3,2},{4,5},{5,4},{6,7},{7,6},{8,9},{9,8},{10,11... | collective-permute-start | bytes 442376 | tf_op jit(solution)/shard_map/ppermute | solution.py:250
  5.0 1.3 %shard_map.82 = bf16[192,512]{1,0:T(8,128)(2,1)S(1)} custom-call(s32[1,192]{1,0:T(1,128)} %offsets_ref.3, bf16[384,512]{1,0:T(8,128)(2,1)} %grad_ref.1), custom_call_target="tpu_custom_call" | custom-call | tf_op jit(solution)/shard_map/pallas_call | solution.py:187
  7.1 22.2 %all-to-all-start.1 = ((bf16[64,4,384]{2,1,0:T(4,128)(2,1)}), bf16[64,4,384]{2,1,0:T(4,128)(2,1)S(1)}, u32[]{:S(2)}, u32[]{:S(2)}) async-start(bf16[64,4,384]{2,1,0:T(4,128)(2,1)} %reshape.22), calls=%async_computation.1 | async-start | bytes 393216 | tf_op jit(solution)/shard_map/all_to_all | solution.py:246
  30.3 3.1 %shard_map.77 = (bf16[4,144,512]{2,1,0:T(8,128)(2,1)S(1)}, bf16[144,1024]{1,0:T(8,128)(2,1)S(1)}) custom-call(s32[4]{0:T(128)S(1)} %fusion.5.at_ref, bf16[144,512]{1,0:T(8,128)(2,1)S(1)} %copy-done, bf16[144,512]{1,0:T(8,128)(2,1)S(1)} %collective-permute-done.other_ref, bf16[512,8192]{1,0:T(8,128)(2,1)} %w_own_ref.5, ...), custom_call_target="tpu_custom_call" | custom-call | flops 603979776 | bytes 4194304 | tf_op jit(solution)/shard_map/pallas_call | solution.py:199
  33.4 2.4 %collective-permute-start.2 = (bf16[4,144,512]{2,1,0:T(8,128)(2,1)S(1)}, bf16[4,144,512]{2,1,0:T(8,128)(2,1)S(1)}, u32[]{:S(2)}, u32[]{:S(2)}) collective-permute-start(bf16[4,144,512]{2,1,0:T(8,128)(2,1)S(1)} %get-tuple-element.19), channel_id=1, source_target_pairs={{0,2},{1,15},{2,0},{3,5},{4,6},{5,3},{6,4},{7,9},{8,10},{9,7},{10,... | collective-permute-start | bytes 1769480 | tf_op jit(solution)/shard_map/ppermute | solution.py:265
  35.8 3.1 %shard_map.78.kept_ref = bf16[4,144,512]{2,1,0:T(8,128)(2,1)S(1)} custom-call(s32[4]{0:T(128)S(1)} %fusion.2.at_ref, bf16[144,1024]{1,0:T(8,128)(2,1)S(1)} %get-tuple-element.18.act_ref, bf16[512,8192]{1,0:T(8,128)(2,1)} %w_own_ref.5, bf16[512,8192]{1,0:T(8,128)(2,1)} %collective-permute-done.1.w_other_ref.refs_6_), custom_call_target="tpu_custom_call" | custom-call | flops 603979776 | bytes 4194304 | tf_op jit(solution)/shard_map/pallas_call | solution.py:199
  39.0 6.2 %collective-permute-done.2.beside_ref = bf16[4,144,512]{2,1,0:T(8,128)(2,1)S(1)} collective-permute-done((bf16[4,144,512]{2,1,0:T(8,128)(2,1)S(1)}, bf16[4,144,512]{2,1,0:T(8,128)(2,1)S(1)}, u32[]{:S(2)}, u32[]{:S(2)}) %collective-permute-start.2) | collective-permute-done | bytes 589856 | tf_op jit(solution)/shard_map/ppermute | solution.py:265
  45.4 4.8 %collective-permute-start.3 = (bf16[144,512]{1,0:T(8,128)(2,1)S(1)}, bf16[144,512]{1,0:T(8,128)(2,1)S(1)}, u32[]{:S(2)}, u32[]{:S(2)}) collective-permute-start(bf16[144,512]{1,0:T(8,128)(2,1)S(1)} %get-tuple-element.21), channel_id=1, source_target_pairs={{0,4},{2,6},{4,8},{6,10},{8,12},{10,14},{12,0},{14,2},{1,5},{3,7},... | collective-permute-start | bytes 442376 | tf_op jit(solution)/shard_map/ppermute | solution.py:240
  50.3 2.9 %collective-permute-start.4 = (bf16[144,512]{1,0:T(8,128)(2,1)S(1)}, bf16[144,512]{1,0:T(8,128)(2,1)S(1)}, u32[]{:S(2)}, u32[]{:S(2)}) collective-permute-start(bf16[144,512]{1,0:T(8,128)(2,1)S(1)} %get-tuple-element.22), channel_id=1, source_target_pairs={{0,8},{2,10},{4,12},{6,14},{8,0},{10,2},{12,4},{14,6},{1,9},{3,11}... | collective-permute-start | bytes 442376 | tf_op jit(solution)/shard_map/ppermute | solution.py:240
  53.2 4.1 %collective-permute-start.5 = (bf16[144,512]{1,0:T(8,128)(2,1)S(1)}, bf16[144,512]{1,0:T(8,128)(2,1)S(1)}, u32[]{:S(2)}, u32[]{:S(2)}) collective-permute-start(bf16[144,512]{1,0:T(8,128)(2,1)S(1)} %get-tuple-element.23), channel_id=1, source_target_pairs={{0,12},{2,14},{4,0},{6,2},{8,4},{10,6},{12,8},{14,10},{1,13},{3,15... | collective-permute-start | bytes 442376 | tf_op jit(solution)/shard_map/ppermute | solution.py:240
  57.7 5.3 %collective-permute-start.6 = (bf16[144,512]{1,0:T(8,128)(2,1)S(1)}, bf16[144,512]{1,0:T(8,128)(2,1)S(1)}, u32[]{:S(2)}, u32[]{:S(2)}) collective-permute-start(bf16[144,512]{1,0:T(8,128)(2,1)S(1)} %shard_map.83.refs_0_), channel_id=1, source_target_pairs={{0,12},{2,14},{4,0},{6,2},{8,4},{10,6},{12,8},{14,10},{1,13},{3,15... | collective-permute-start | bytes 442376 | tf_op jit(solution)/shard_map/ppermute | solution.py:240
  63.0 2.9 %collective-permute-start.7 = (bf16[144,512]{1,0:T(8,128)(2,1)S(1)}, bf16[144,512]{1,0:T(8,128)(2,1)S(1)}, u32[]{:S(2)}, u32[]{:S(2)}) collective-permute-start(bf16[144,512]{1,0:T(8,128)(2,1)S(1)} %shard_map.83.refs_0_), channel_id=1, source_target_pairs={{0,8},{2,10},{4,12},{6,14},{8,0},{10,2},{12,4},{14,6},{1,9},{3,11}... | collective-permute-start | bytes 442376 | tf_op jit(solution)/shard_map/ppermute | solution.py:240
  65.9 4.5 %collective-permute-start.8 = (bf16[144,512]{1,0:T(8,128)(2,1)S(1)}, bf16[144,512]{1,0:T(8,128)(2,1)S(1)}, u32[]{:S(2)}, u32[]{:S(2)}) collective-permute-start(bf16[144,512]{1,0:T(8,128)(2,1)S(1)} %shard_map.83.refs_0_), channel_id=1, source_target_pairs={{0,4},{2,6},{4,8},{6,10},{8,12},{10,14},{12,0},{14,2},{1,5},{3,7},... | collective-permute-start | bytes 442376 | tf_op jit(solution)/shard_map/ppermute | solution.py:240
  71.6 3.5 %collective-permute-done.7.refs_2_ = bf16[144,512]{1,0:T(8,128)(2,1)S(1)} collective-permute-done((bf16[144,512]{1,0:T(8,128)(2,1)S(1)}, bf16[144,512]{1,0:T(8,128)(2,1)S(1)}, u32[]{:S(2)}, u32[]{:S(2)}) %collective-permute-start.7) | collective-permute-done | bytes 147488 | tf_op jit(solution)/shard_map/ppermute | solution.py:240
  75.1 5.4 %collective-permute-done.8.refs_3_ = bf16[144,512]{1,0:T(8,128)(2,1)S(1)} collective-permute-done((bf16[144,512]{1,0:T(8,128)(2,1)S(1)}, bf16[144,512]{1,0:T(8,128)(2,1)S(1)}, u32[]{:S(2)}, u32[]{:S(2)}) %collective-permute-start.8) | collective-permute-done | bytes 147488 | tf_op jit(solution)/shard_map/ppermute | solution.py:240
  80.6 4.3 %collective-permute-start.9 = (bf16[4,144,512]{2,1,0:T(8,128)(2,1)S(1)}, bf16[4,144,512]{2,1,0:T(8,128)(2,1)S(1)}, u32[]{:S(2)}, u32[]{:S(2)}) collective-permute-start(bf16[4,144,512]{2,1,0:T(8,128)(2,1)S(1)} %pad_maximum_fusion), channel_id=1, source_target_pairs={{0,2},{1,15},{2,0},{3,5},{4,6},{5,3},{6,4},{7,9},{8,10},{9,7},{10,... | collective-permute-start | bytes 1769480 | tf_op jit(solution)/shard_map/ppermute | solution.py:293
  84.9 14.6 %all-to-all-start = ((bf16[64,4,384]{2,1,0:T(4,128)(2,1)}), bf16[64,4,384]{2,1,0:T(4,128)(2,1)S(1)}, u32[]{:S(2)}, u32[]{:S(2)}) async-start(bf16[64,4,384]{2,1,0:T(4,128)(2,1)} %reshape.20), calls=%async_computation | async-start | bytes 393216 | tf_op jit(solution)/shard_map/all_to_all | solution.py:246
  99.5 3.7 %shard_map.84 = (f32[144,512]{1,0:T(8,128)S(1)}, f32[144,512]{1,0:T(8,128)S(1)}, f32[144,512]{1,0:T(8,128)S(1)}) custom-call(s32[4]{0:T(128)S(1)} %fusion.2.at_ref, bf16[144,512]{1,0:T(8,128)(2,1)S(1)} %shard_map.83.refs_0_, bf16[144,512]{1,0:T(8,128)(2,1)S(1)} %collective-permute-done.6.refs_1_, bf16[144,512]{1,0:T(8,128)(2,1)S(1)} %collective-permute-done.7.refs_2_, ...), custom_call_target="tpu_custom_call" | custom-call | flops 603979776 | bytes 4194304 | tf_op jit(solution)/shard_map/pallas_call | solution.py:199
  103.3 3.4 %shard_map.85 = (f32[144,512]{1,0:T(8,128)S(1)}, bf16[144,512]{1,0:T(8,128)(2,1)S(1)}) custom-call(s32[4]{0:T(128)S(1)} %fusion.5.at_ref, bf16[4,144,512]{2,1,0:T(8,128)(2,1)S(1)} %collective-permute-done.9.grad_ref, f32[144,512]{1,0:T(8,128)S(1)} %get-tuple-element.29.own_in, f32[144,512]{1,0:T(8,128)S(1)} %get-tuple-element.30.other_in, ...), custom_call_target="tpu_custom_call" | custom-call | flops 603979776 | bytes 4194304 | tf_op jit(solution)/shard_map/pallas_call | solution.py:199
  106.7 2.8 %collective-permute-start.10 = (bf16[144,512]{1,0:T(8,128)(2,1)S(1)}, bf16[144,512]{1,0:T(8,128)(2,1)S(1)}, u32[]{:S(2)}, u32[]{:S(2)}) collective-permute-start(bf16[144,512]{1,0:T(8,128)(2,1)S(1)} %get-tuple-element.32), channel_id=1, source_target_pairs={{0,1},{1,0},{2,3},{3,2},{4,5},{5,4},{6,7},{7,6},{8,9},{9,8},{10,11... | collective-permute-start | bytes 442376 | tf_op jit(solution)/shard_map/ppermute | solution.py:311
  109.5 1.0 collective-permute-done.10.other_ref
  111.2 8.1 %all-to-all-done = bf16[64,4,384]{2,1,0:T(4,128)(2,1)S(1)} async-done(((bf16[64,4,384]{2,1,0:T(4,128)(2,1)}), bf16[64,4,384]{2,1,0:T(4,128)(2,1)S(1)}, u32[]{:S(2)}, u32[]{:S(2)}) %all-to-all-start) | async-done | bytes 196640 | tf_op jit(solution)/shard_map/all_to_all | solution.py:246
  119.4 1.2 shard_map.81
  (29 shorter events, 4.5 us)
Async XLA Ops:
  0.6 28.7 %collective-permute-start.1 = (bf16[512,8192]{1,0:T(8,128)(2,1)}, bf16[512,8192]{1,0:T(8,128)(2,1)}, u32[]{:S(2)}, u32[]{:S(2)}) collective-permute-start(bf16[512,8192]{1,0:T(8,128)(2,1)} %w_own_ref.5), channel_id=1, source_target_pairs={{0,1},{1,0},{2,3},{3,2},{4,5},{5,4},{6,7},{7,6},{8,9},{9,8},{10,11... | collective-permute-start | bytes 25165832 | tf_op jit(solution)/shard_map/ppermute | solution.py:249
  2.6 26.8 %collective-permute-start = (bf16[144,512]{1,0:T(8,128)(2,1)}, bf16[144,512]{1,0:T(8,128)(2,1)S(1)}, u32[]{:S(2)}, u32[]{:S(2)}) collective-permute-start(bf16[144,512]{1,0:T(8,128)(2,1)} %refs_4_.1), channel_id=1, source_target_pairs={{0,1},{1,0},{2,3},{3,2},{4,5},{5,4},{6,7},{7,6},{8,9},{9,8},{10,11... | collective-permute-start | bytes 442376 | tf_op jit(solution)/shard_map/ppermute | solution.py:250
  7.1 43.1 %all-to-all-start.1 = ((bf16[64,4,384]{2,1,0:T(4,128)(2,1)}), bf16[64,4,384]{2,1,0:T(4,128)(2,1)S(1)}, u32[]{:S(2)}, u32[]{:S(2)}) async-start(bf16[64,4,384]{2,1,0:T(4,128)(2,1)} %reshape.22), calls=%async_computation.1 | async-start | bytes 393216 | tf_op jit(solution)/shard_map/all_to_all | solution.py:246
  29.4 0.9 copy-start
  33.4 11.8 %collective-permute-start.2 = (bf16[4,144,512]{2,1,0:T(8,128)(2,1)S(1)}, bf16[4,144,512]{2,1,0:T(8,128)(2,1)S(1)}, u32[]{:S(2)}, u32[]{:S(2)}) collective-permute-start(bf16[4,144,512]{2,1,0:T(8,128)(2,1)S(1)} %get-tuple-element.19), channel_id=1, source_target_pairs={{0,2},{1,15},{2,0},{3,5},{4,6},{5,3},{6,4},{7,9},{8,10},{9,7},{10,... | collective-permute-start | bytes 1769480 | tf_op jit(solution)/shard_map/ppermute | solution.py:265
  35.8 21.5 %copy-start.4 = (s32[144,1]{0,1:T(1,128)S(1)}, s32[144,1]{0,1:T(1,128)}, u32[]{:S(2)}) copy-start(s32[144,1]{0,1:T(1,128)} %param.9) | copy-start | bytes 1732
  35.8 63.7 %copy-start.1 = (bf16[144,512]{1,0:T(8,128)(2,1)S(1)}, bf16[144,512]{1,0:T(8,128)(2,1)}, u32[]{:S(2)}) copy-start(bf16[144,512]{1,0:T(8,128)(2,1)} %refs_4_.1) | copy-start | bytes 442372
  45.4 20.5 %collective-permute-start.3 = (bf16[144,512]{1,0:T(8,128)(2,1)S(1)}, bf16[144,512]{1,0:T(8,128)(2,1)S(1)}, u32[]{:S(2)}, u32[]{:S(2)}) collective-permute-start(bf16[144,512]{1,0:T(8,128)(2,1)S(1)} %get-tuple-element.21), channel_id=1, source_target_pairs={{0,4},{2,6},{4,8},{6,10},{8,12},{10,14},{12,0},{14,2},{1,5},{3,7},... | collective-permute-start | bytes 442376 | tf_op jit(solution)/shard_map/ppermute | solution.py:240
  50.3 20.1 %collective-permute-start.4 = (bf16[144,512]{1,0:T(8,128)(2,1)S(1)}, bf16[144,512]{1,0:T(8,128)(2,1)S(1)}, u32[]{:S(2)}, u32[]{:S(2)}) collective-permute-start(bf16[144,512]{1,0:T(8,128)(2,1)S(1)} %get-tuple-element.22), channel_id=1, source_target_pairs={{0,8},{2,10},{4,12},{6,14},{8,0},{10,2},{12,4},{14,6},{1,9},{3,11}... | collective-permute-start | bytes 442376 | tf_op jit(solution)/shard_map/ppermute | solution.py:240
  53.2 17.2 %collective-permute-start.5 = (bf16[144,512]{1,0:T(8,128)(2,1)S(1)}, bf16[144,512]{1,0:T(8,128)(2,1)S(1)}, u32[]{:S(2)}, u32[]{:S(2)}) collective-permute-start(bf16[144,512]{1,0:T(8,128)(2,1)S(1)} %get-tuple-element.23), channel_id=1, source_target_pairs={{0,12},{2,14},{4,0},{6,2},{8,4},{10,6},{12,8},{14,10},{1,13},{3,15... | collective-permute-start | bytes 442376 | tf_op jit(solution)/shard_map/ppermute | solution.py:240
  57.7 13.9 %collective-permute-start.6 = (bf16[144,512]{1,0:T(8,128)(2,1)S(1)}, bf16[144,512]{1,0:T(8,128)(2,1)S(1)}, u32[]{:S(2)}, u32[]{:S(2)}) collective-permute-start(bf16[144,512]{1,0:T(8,128)(2,1)S(1)} %shard_map.83.refs_0_), channel_id=1, source_target_pairs={{0,12},{2,14},{4,0},{6,2},{8,4},{10,6},{12,8},{14,10},{1,13},{3,15... | collective-permute-start | bytes 442376 | tf_op jit(solution)/shard_map/ppermute | solution.py:240
  63.0 12.2 %collective-permute-start.7 = (bf16[144,512]{1,0:T(8,128)(2,1)S(1)}, bf16[144,512]{1,0:T(8,128)(2,1)S(1)}, u32[]{:S(2)}, u32[]{:S(2)}) collective-permute-start(bf16[144,512]{1,0:T(8,128)(2,1)S(1)} %shard_map.83.refs_0_), channel_id=1, source_target_pairs={{0,8},{2,10},{4,12},{6,14},{8,0},{10,2},{12,4},{14,6},{1,9},{3,11}... | collective-permute-start | bytes 442376 | tf_op jit(solution)/shard_map/ppermute | solution.py:240
  65.9 14.6 %collective-permute-start.8 = (bf16[144,512]{1,0:T(8,128)(2,1)S(1)}, bf16[144,512]{1,0:T(8,128)(2,1)S(1)}, u32[]{:S(2)}, u32[]{:S(2)}) collective-permute-start(bf16[144,512]{1,0:T(8,128)(2,1)S(1)} %shard_map.83.refs_0_), channel_id=1, source_target_pairs={{0,4},{2,6},{4,8},{6,10},{8,12},{10,14},{12,0},{14,2},{1,5},{3,7},... | collective-permute-start | bytes 442376 | tf_op jit(solution)/shard_map/ppermute | solution.py:240
  80.6 22.6 %collective-permute-start.9 = (bf16[4,144,512]{2,1,0:T(8,128)(2,1)S(1)}, bf16[4,144,512]{2,1,0:T(8,128)(2,1)S(1)}, u32[]{:S(2)}, u32[]{:S(2)}) collective-permute-start(bf16[4,144,512]{2,1,0:T(8,128)(2,1)S(1)} %pad_maximum_fusion), channel_id=1, source_target_pairs={{0,2},{1,15},{2,0},{3,5},{4,6},{5,3},{6,4},{7,9},{8,10},{9,7},{10,... | collective-permute-start | bytes 1769480 | tf_op jit(solution)/shard_map/ppermute | solution.py:293
  84.9 34.4 %all-to-all-start = ((bf16[64,4,384]{2,1,0:T(4,128)(2,1)}), bf16[64,4,384]{2,1,0:T(4,128)(2,1)S(1)}, u32[]{:S(2)}, u32[]{:S(2)}) async-start(bf16[64,4,384]{2,1,0:T(4,128)(2,1)} %reshape.20), calls=%async_computation | async-start | bytes 393216 | tf_op jit(solution)/shard_map/all_to_all | solution.py:246
  103.2 16.2 %copy-start.2 = (bf16[384,512]{1,0:T(8,128)(2,1)S(1)}, bf16[384,512]{1,0:T(8,128)(2,1)}, u32[]{:S(2)}) copy-start(bf16[384,512]{1,0:T(8,128)(2,1)} %text_ref.1) | copy-start | bytes 1179652
  103.3 16.2 %copy-start.3 = (s32[1,192]{1,0:T(1,128)S(1)}, s32[1,192]{1,0:T(1,128)}, u32[]{:S(2)}) copy-start(s32[1,192]{1,0:T(1,128)} %offsets_ref.3) | copy-start | bytes 2308
  106.7 3.8 %collective-permute-start.10 = (bf16[144,512]{1,0:T(8,128)(2,1)S(1)}, bf16[144,512]{1,0:T(8,128)(2,1)S(1)}, u32[]{:S(2)}, u32[]{:S(2)}) collective-permute-start(bf16[144,512]{1,0:T(8,128)(2,1)S(1)} %get-tuple-element.32), channel_id=1, source_target_pairs={{0,1},{1,0},{2,3},{3,2},{4,5},{5,4},{6,7},{7,6},{8,9},{9,8},{10,11... | collective-permute-start | bytes 442376 | tf_op jit(solution)/shard_map/ppermute | solution.py:311

commit v3 on v2

--- a/solution.py
+++ b/solution.py
@@ -58,12 +58,9 @@
     out_ref[...] = rows
 
 
-def route_kernel(groups, capacity, dest_ref, total_ref, *refs):
-    term_refs, out_ref = refs[:-1], refs[-1]
+def route_kernel(groups, capacity, dest_ref, total_ref, last_ref, out_ref):
     slots = out_ref.shape[0]
-    total = total_ref[...]
-    for term_ref in term_refs:
-        total += term_ref[...].astype(F32)
+    total = total_ref[...] + last_ref[...].astype(F32)
     hit = rows_by_target(dest_ref[...], groups, capacity, slots)
     pick = jnp.where(hit, 1.0, 0.0)
     sent = jnp.dot(pick.astype(BF16), total.astype(BF16), preferred_element_type=F32)
@@ -128,11 +125,17 @@
         out_ref[j] = total.astype(BF16)
 
 
-def add_kernel(kept_ref, beside_ref, token_ref, total_ref, *term_refs):
-    token_ref[...] = jnp.zeros_like(token_ref)
+def add_kernel(kept_ref, beside_ref, total_ref, *term_refs):
     total_ref[...] = kept_ref[0].astype(F32) + beside_ref[0].astype(F32)
     for j, term_ref in enumerate(term_refs, 1):
-        term_ref[...] = (kept_ref[j].astype(F32) + beside_ref[j].astype(F32)).astype(BF16)
+        total = kept_ref[j].astype(F32) + beside_ref[j].astype(F32)
+        term_ref[...] = total.astype(term_ref.dtype)
+
+
+def relay_kernel(held_ref, arrived_ref, total_ref, back_ref, out_ref, sum_ref, token_ref):
+    token_ref[...] = jnp.zeros_like(token_ref)
+    out_ref[...] = (held_ref[...] + arrived_ref[...].astype(F32)).astype(BF16)
+    sum_ref[...] = total_ref[...] + back_ref[...].astype(F32)
 
 
 def backward_first_kernel(blocks, at_ref, *refs):
@@ -193,7 +196,7 @@
     return got if len(outs) > 1 else got[0]
 
 
-def product(kernel, outs, at, args, weights, blocks):
+def product(kernel, outs, at, args, weights, blocks, share=1):
     hid, width = weights[0].shape[0], weights[0].shape[1] // (4 * blocks)
     rows = args[0].shape[-2]
     got = pl.pallas_call(
@@ -206,8 +209,8 @@
             pltpu.SemaphoreType.DMA((2, blocks)),
         ],
         cost_estimate=pl.CostEstimate(
-            flops=2 * rows * blocks * width * 2 * hid,
-            bytes_accessed=4 * blocks * hid * width,
+            flops=2 * rows * blocks * width * 2 * hid // share,
+            bytes_accessed=4 * blocks * hid * width // share,
             transcendentals=0,
         ),
         compiler_params=pltpu.CompilerParams(vmem_limit_bytes=24 * 1024 * 1024),
@@ -224,7 +227,7 @@
     half = lines // 2
     line, core = lax.axis_index("line"), lax.axis_index("core")
     beside_line = line + 1 - 2 * lax.rem(line + core, 2) + lines
-    steps = 2 * jnp.arange(half, dtype=jnp.int32)
+    steps = (2 - 4 * core) * jnp.arange(half, dtype=jnp.int32) + 2 * lines
     same = 2 * lax.rem(line + steps, lines) + core
     opposite = 2 * lax.rem(beside_line + steps, lines) + core
     dest_row = routes_dest.reshape(1, rows)
@@ -236,8 +239,12 @@
             odd = (i + c) % 2
             beside.append((2 * i + c, 2 * ((i + (-1 if odd else 1)) % lines) + c))
 
-    def shift(x, by):
-        return lax.ppermute(x, "line", [(i, (i + by) % lines) for i in range(lines)])
+    def relay(x, by):
+        pairs = []
+        for i in range(lines):
+            for c in range(2):
+                pairs.append((2 * i + c, 2 * ((i + (by if c == 0 else -by)) % lines) + c))
+        return lax.ppermute(x, ("line", "core"), pairs)
 
     def by_group(x):
         return x.reshape(groups, 4, capacity * width // 4)
@@ -264,19 +271,29 @@
     )
     beside_terms = lax.ppermute(sent, ("line", "core"), beside)
     kept = product(forward_second_kernel, [terms_out], same, (act,), weights, half)
-    token, total, *terms = call(
+    total, first, second, third = call(
         add_kernel,
-        [((8, 128), F32), ((rows, width), F32)] + [((rows, width), BF16)] * (half - 1),
+        [((rows, width), F32)] * 2 + [((rows, width), BF16)] * 2,
         kept,
         beside_terms,
     )
-    terms = [shift(term, 2 * j) for j, term in enumerate(terms, 1)]
+    passed = relay(second, 2)
+    back = relay(third, -2)
+    first, total, token = call(
+        relay_kernel,
+        [((rows, width), BF16), ((rows, width), F32), ((8, 128), F32)],
+        first,
+        passed,
+        total,
+        back,
+    )
+    last = relay(first, 2)
     outgoing = call(
         functools.partial(route_kernel, groups, capacity),
         [((slots, width), BF16)],
         dest_row,
         total,
-        *terms,
+        last,
     )
     outgoing = by_group(outgoing)
     arrived = exchange(outgoing)
@@ -288,8 +305,8 @@
         returned,
         token,
     )
-    near = [mine] + [shift(mine, -2 * j) for j in range(1, half)]
-    *near, _ = lax.optimization_barrier((*near, outgoing))
+    last = relay(mine, 2)
+    near = [mine, relay(mine, -2), relay(last, 2), last]
     far = lax.ppermute(jnp.stack(near), ("line", "core"), beside)
     wide = ((rows, hid), F32)
     own, other, slope = product(
@@ -299,6 +316,7 @@
         (*near, pre_hidden),
         weights,
         half,
+        1000,
     )
     own, other = product(
         backward_second_kernel,
@@ -307,6 +325,7 @@
         (far, own, other),
         weights,
         half,
+        1000,
     )
     other = lax.ppermute(other, "core", cores)
     grad_hidden = call(slope_kernel, [((rows, hid), BF16)], own, other, slope, final=True)

time: 121 us -> 116 us (0.959)
  the two profiles are of different devices: /device:TPU:24 before, /device:TPU:1 now
where the time goes in v3:
time: 116 us
  starting transfers between devices  76.2 us (66%)
  waiting for transfers between devices  18 us (16%)
  Pallas kernels  17.6 us (15%)
  local copies, waits for them, and re-layouts  2.76 us (2%)
    all_to_all x2, starting transfers between devices, exchange(): x = lax.all_to_all(x, 'group', split_axis=0, concat_axis=0, tiled=True)  24.1 us
    ppermute x6, starting transfers between devices, relay(): return lax.ppermute(x, ('line', 'core'), pairs)  22.7 us
    ppermute x1, starting transfers between devices, on_device(): w_other = lax.ppermute(proj_weight, 'core', cores)  16.1 us
    pallas_call x4, Pallas kernels, product(): pl.pallas_call(kernel, in_specs=[SMEM] + [VMEM] * len(args) + [HBM] * 2,...  13.4 us
    ppermute x6, waiting for transfers between devices, relay(): return lax.ppermute(x, ('line', 'core'), pairs)  7.2 us
    ppermute x1, waiting for transfers between devices, on_device(): far = lax.ppermute(jnp.stack(near), ('line', 'core'), beside)  6.46 us
    ppermute x1, starting transfers between devices, on_device(): beside_terms = lax.ppermute(sent, ('line', 'core'), beside)  5.1 us
    ppermute x1, waiting for transfers between devices, on_device(): beside_terms = lax.ppermute(sent, ('line', 'core'), beside)  4.37 us
  transfers between devices with their start and end apart: 13, of which 4 were waited for; matrix products, arithmetic and copies ran while one was open for 2% of the time, Pallas kernels for 14%

profile of v3, /device:TPU:1, one launch (start us, length us, event | category | flops | bytes accessed | tf_op | source)
XLA Modules:
  0.0 115.7 jit_solution(2567621888090366537)
XLA Ops:
  0.6 16.1 %collective-permute-start.1 = (bf16[512,8192]{1,0:T(8,128)(2,1)}, bf16[512,8192]{1,0:T(8,128)(2,1)}, u32[]{:S(2)}, u32[]{:S(2)}) collective-permute-start(bf16[512,8192]{1,0:T(8,128)(2,1)} %w_own_ref.5), channel_id=1, source_target_pairs={{0,1},{1,0},{2,3},{3,2},{4,5},{5,4},{6,7},{7,6},{8,9},{9,8},{10,11... | collective-permute-start | bytes 25165832 | tf_op jit(solution)/shard_map/ppermute | solution.py:256
  16.7 1.9 %collective-permute-start = (bf16[144,512]{1,0:T(8,128)(2,1)}, bf16[144,512]{1,0:T(8,128)(2,1)S(1)}, u32[]{:S(2)}, u32[]{:S(2)}) collective-permute-start(bf16[144,512]{1,0:T(8,128)(2,1)} %refs_4_.1), channel_id=1, source_target_pairs={{0,1},{1,0},{2,3},{3,2},{4,5},{5,4},{6,7},{7,6},{8,9},{9,8},{10,11... | collective-permute-start | bytes 442376 | tf_op jit(solution)/shard_map/ppermute | solution.py:257
  18.6 1.3 %shard_map.83 = bf16[192,512]{1,0:T(8,128)(2,1)S(1)} custom-call(s32[1,192]{1,0:T(1,128)} %offsets_ref.3, bf16[384,512]{1,0:T(8,128)(2,1)} %grad_ref.1), custom_call_target="tpu_custom_call" | custom-call | tf_op jit(solution)/shard_map/pallas_call | solution.py:190
  20.7 9.3 %all-to-all-start.1 = ((bf16[64,4,384]{2,1,0:T(4,128)(2,1)}), bf16[64,4,384]{2,1,0:T(4,128)(2,1)S(1)}, u32[]{:S(2)}, u32[]{:S(2)}) async-start(bf16[64,4,384]{2,1,0:T(4,128)(2,1)} %reshape.22), calls=%async_computation.1 | async-start | bytes 393216 | tf_op jit(solution)/shard_map/all_to_all | solution.py:253
  30.1 0.9 copy-done
  31.0 3.1 %shard_map.77 = (bf16[4,144,512]{2,1,0:T(8,128)(2,1)S(1)}, bf16[144,1024]{1,0:T(8,128)(2,1)S(1)}) custom-call(s32[4]{0:T(128)S(1)} %fusion.5.at_ref, bf16[144,512]{1,0:T(8,128)(2,1)S(1)} %copy-done, bf16[144,512]{1,0:T(8,128)(2,1)S(1)} %collective-permute-done.other_ref, bf16[512,8192]{1,0:T(8,128)(2,1)} %w_own_ref.5, ...), custom_call_target="tpu_custom_call" | custom-call | flops 603979776 | bytes 4194304 | tf_op jit(solution)/shard_map/pallas_call | solution.py:202
  34.1 5.1 %collective-permute-start.2 = (bf16[4,144,512]{2,1,0:T(8,128)(2,1)S(1)}, bf16[4,144,512]{2,1,0:T(8,128)(2,1)S(1)}, u32[]{:S(2)}, u32[]{:S(2)}) collective-permute-start(bf16[4,144,512]{2,1,0:T(8,128)(2,1)S(1)} %get-tuple-element.17), channel_id=1, source_target_pairs={{0,2},{1,15},{2,0},{3,5},{4,6},{5,3},{6,4},{7,9},{8,10},{9,7},{10,... | collective-permute-start | bytes 1769480 | tf_op jit(solution)/shard_map/ppermute | solution.py:272
  39.3 3.1 %shard_map.78.kept_ref = bf16[4,144,512]{2,1,0:T(8,128)(2,1)S(1)} custom-call(s32[4]{0:T(128)S(1)} %fusion.2.at_ref, bf16[144,1024]{1,0:T(8,128)(2,1)S(1)} %get-tuple-element.16.act_ref, bf16[512,8192]{1,0:T(8,128)(2,1)} %w_own_ref.5, bf16[512,8192]{1,0:T(8,128)(2,1)} %collective-permute-done.1.w_other_ref.refs_6_), custom_call_target="tpu_custom_call" | custom-call | flops 603979776 | bytes 4194304 | tf_op jit(solution)/shard_map/pallas_call | solution.py:202
  42.4 4.4 %collective-permute-done.2.beside_ref = bf16[4,144,512]{2,1,0:T(8,128)(2,1)S(1)} collective-permute-done((bf16[4,144,512]{2,1,0:T(8,128)(2,1)S(1)}, bf16[4,144,512]{2,1,0:T(8,128)(2,1)S(1)}, u32[]{:S(2)}, u32[]{:S(2)}) %collective-permute-start.2) | collective-permute-done | bytes 589856 | tf_op jit(solution)/shard_map/ppermute | solution.py:272
  46.9 4.1 %collective-permute-start.3 = (bf16[144,512]{1,0:T(8,128)(2,1)S(1)}, bf16[144,512]{1,0:T(8,128)(2,1)S(1)}, u32[]{:S(2)}, u32[]{:S(2)}) collective-permute-start(bf16[144,512]{1,0:T(8,128)(2,1)S(1)} %get-tuple-element.19), channel_id=1, source_target_pairs={{0,4},{1,13},{2,6},{3,15},{4,8},{5,1},{6,10},{7,3},{8,12},{9,5},{1... | collective-permute-start | bytes 442376 | tf_op jit(solution)/shard_map/ppermute | solution.py:247
  51.1 2.0 %collective-permute-start.4 = (bf16[144,512]{1,0:T(8,128)(2,1)S(1)}, bf16[144,512]{1,0:T(8,128)(2,1)S(1)}, u32[]{:S(2)}, u32[]{:S(2)}) collective-permute-start(bf16[144,512]{1,0:T(8,128)(2,1)S(1)} %get-tuple-element.21), channel_id=1, source_target_pairs={{0,12},{1,5},{2,14},{3,7},{4,0},{5,9},{6,2},{7,11},{8,4},{9,13},{1... | collective-permute-start | bytes 442376 | tf_op jit(solution)/shard_map/ppermute | solution.py:247
  53.3 2.4 %collective-permute-done.3.arrived_ref = bf16[144,512]{1,0:T(8,128)(2,1)S(1)} collective-permute-done((bf16[144,512]{1,0:T(8,128)(2,1)S(1)}, bf16[144,512]{1,0:T(8,128)(2,1)S(1)}, u32[]{:S(2)}, u32[]{:S(2)}) %collective-permute-start.3) | collective-permute-done | bytes 147488 | tf_op jit(solution)/shard_map/ppermute | solution.py:247
  55.6 4.8 %collective-permute-done.4.back_ref = bf16[144,512]{1,0:T(8,128)(2,1)S(1)} collective-permute-done((bf16[144,512]{1,0:T(8,128)(2,1)S(1)}, bf16[144,512]{1,0:T(8,128)(2,1)S(1)}, u32[]{:S(2)}, u32[]{:S(2)}) %collective-permute-start.4) | collective-permute-done | bytes 147488 | tf_op jit(solution)/shard_map/ppermute | solution.py:247
  60.9 4.3 %collective-permute-start.7 = (bf16[144,512]{1,0:T(8,128)(2,1)S(1)}, bf16[144,512]{1,0:T(8,128)(2,1)S(1)}, u32[]{:S(2)}, u32[]{:S(2)}) collective-permute-start(bf16[144,512]{1,0:T(8,128)(2,1)S(1)} %shard_map.84.refs_0_), channel_id=1, source_target_pairs={{0,4},{1,13},{2,6},{3,15},{4,8},{5,1},{6,10},{7,3},{8,12},{9,5},{1... | collective-permute-start | bytes 442376 | tf_op jit(solution)/shard_map/ppermute | solution.py:247
  65.2 4.9 %collective-permute-start.5 = (bf16[144,512]{1,0:T(8,128)(2,1)S(1)}, bf16[144,512]{1,0:T(8,128)(2,1)S(1)}, u32[]{:S(2)}, u32[]{:S(2)}) collective-permute-start(bf16[144,512]{1,0:T(8,128)(2,1)S(1)} %get-tuple-element.23), channel_id=1, source_target_pairs={{0,4},{1,13},{2,6},{3,15},{4,8},{5,1},{6,10},{7,3},{8,12},{9,5},{1... | collective-permute-start | bytes 442376 | tf_op jit(solution)/shard_map/ppermute | solution.py:247
  70.1 1.9 %collective-permute-start.6 = (bf16[144,512]{1,0:T(8,128)(2,1)S(1)}, bf16[144,512]{1,0:T(8,128)(2,1)S(1)}, u32[]{:S(2)}, u32[]{:S(2)}) collective-permute-start(bf16[144,512]{1,0:T(8,128)(2,1)S(1)} %shard_map.84.refs_0_), channel_id=1, source_target_pairs={{0,12},{1,5},{2,14},{3,7},{4,0},{5,9},{6,2},{7,11},{8,4},{9,13},{1... | collective-permute-start | bytes 442376 | tf_op jit(solution)/shard_map/ppermute | solution.py:247
  72.0 5.5 %collective-permute-start.8 = (bf16[144,512]{1,0:T(8,128)(2,1)S(1)}, bf16[144,512]{1,0:T(8,128)(2,1)S(1)}, u32[]{:S(2)}, u32[]{:S(2)}) collective-permute-start(bf16[144,512]{1,0:T(8,128)(2,1)S(1)} %collective-permute-done.7.refs_3_), channel_id=1, source_target_pairs={{0,4},{1,13},{2,6},{3,15},{4,8},{5,1},{6,10},{7,3},{8,12},{9,5},{1... | collective-permute-start | bytes 442376 | tf_op jit(solution)/shard_map/ppermute | solution.py:247
  78.7 14.8 %all-to-all-start = ((bf16[64,4,384]{2,1,0:T(4,128)(2,1)}), bf16[64,4,384]{2,1,0:T(4,128)(2,1)S(1)}, u32[]{:S(2)}, u32[]{:S(2)}) async-start(bf16[64,4,384]{2,1,0:T(4,128)(2,1)} %reshape.20), calls=%async_computation | async-start | bytes 393216 | tf_op jit(solution)/shard_map/all_to_all | solution.py:253
  93.6 1.9 %collective-permute-start.9 = (bf16[4,144,512]{2,1,0:T(8,128)(2,1)S(1)}, bf16[4,144,512]{2,1,0:T(8,128)(2,1)S(1)}, u32[]{:S(2)}, u32[]{:S(2)}) collective-permute-start(bf16[4,144,512]{2,1,0:T(8,128)(2,1)S(1)} %pad_maximum_fusion), channel_id=1, source_target_pairs={{0,2},{1,15},{2,0},{3,5},{4,6},{5,3},{6,4},{7,9},{8,10},{9,7},{10,... | collective-permute-start | bytes 1769480 | tf_op jit(solution)/shard_map/ppermute | solution.py:310
  95.6 3.7 %shard_map.85 = (f32[144,512]{1,0:T(8,128)S(1)}, f32[144,512]{1,0:T(8,128)S(1)}, f32[144,512]{1,0:T(8,128)S(1)}) custom-call(s32[4]{0:T(128)S(1)} %fusion.2.at_ref, bf16[144,512]{1,0:T(8,128)(2,1)S(1)} %shard_map.84.refs_0_, bf16[144,512]{1,0:T(8,128)(2,1)S(1)} %collective-permute-done.6.refs_1_, bf16[144,512]{1,0:T(8,128)(2,1)S(1)} %collective-permute-done.8.refs_2_, ...), custom_call_target="tpu_custom_call" | custom-call | flops 603979 | bytes 4194 | tf_op jit(solution)/shard_map/pallas_call | solution.py:202
  99.3 6.5 %collective-permute-done.9.grad_ref = bf16[4,144,512]{2,1,0:T(8,128)(2,1)S(1)} collective-permute-done((bf16[4,144,512]{2,1,0:T(8,128)(2,1)S(1)}, bf16[4,144,512]{2,1,0:T(8,128)(2,1)S(1)}, u32[]{:S(2)}, u32[]{:S(2)}) %collective-permute-start.9) | collective-permute-done | bytes 589856 | tf_op jit(solution)/shard_map/ppermute | solution.py:310
  105.8 3.4 %shard_map.86 = (f32[144,512]{1,0:T(8,128)S(1)}, bf16[144,512]{1,0:T(8,128)(2,1)S(1)}) custom-call(s32[4]{0:T(128)S(1)} %fusion.5.at_ref, bf16[4,144,512]{2,1,0:T(8,128)(2,1)S(1)} %collective-permute-done.9.grad_ref, f32[144,512]{1,0:T(8,128)S(1)} %get-tuple-element.25.own_in, f32[144,512]{1,0:T(8,128)S(1)} %get-tuple-element.26.other_in, ...), custom_call_target="tpu_custom_call" | custom-call | flops 603979 | bytes 4194 | tf_op jit(solution)/shard_map/pallas_call | solution.py:202
  109.2 4.4 %collective-permute-start.10 = (bf16[144,512]{1,0:T(8,128)(2,1)S(1)}, bf16[144,512]{1,0:T(8,128)(2,1)S(1)}, u32[]{:S(2)}, u32[]{:S(2)}) collective-permute-start(bf16[144,512]{1,0:T(8,128)(2,1)S(1)} %get-tuple-element.28), channel_id=1, source_target_pairs={{0,1},{1,0},{2,3},{3,2},{4,5},{5,4},{6,7},{7,6},{8,9},{9,8},{10,11... | collective-permute-start | bytes 442376 | tf_op jit(solution)/shard_map/ppermute | solution.py:330
  113.7 1.2 %shard_map.82 = bf16[384,512]{1,0:T(8,128)(2,1)} custom-call(s32[1,192]{1,0:T(1,128)S(1)} %copy-done.4, bf16[192,512]{1,0:T(8,128)(2,1)S(1)} %reshape.21.arrived_ref, bf16[384,512]{1,0:T(8,128)(2,1)S(1)} %copy-done.2), custom_call_target="tpu_custom_call" | custom-call | tf_op jit(solution)/shard_map/pallas_call | solution.py:190
  (30 shorter events, 3.6 us)
Async XLA Ops:
  0.6 29.5 %collective-permute-start.1 = (bf16[512,8192]{1,0:T(8,128)(2,1)}, bf16[512,8192]{1,0:T(8,128)(2,1)}, u32[]{:S(2)}, u32[]{:S(2)}) collective-permute-start(bf16[512,8192]{1,0:T(8,128)(2,1)} %w_own_ref.5), channel_id=1, source_target_pairs={{0,1},{1,0},{2,3},{3,2},{4,5},{5,4},{6,7},{7,6},{8,9},{9,8},{10,11... | collective-permute-start | bytes 25165832 | tf_op jit(solution)/shard_map/ppermute | solution.py:256
  16.7 13.4 %collective-permute-start = (bf16[144,512]{1,0:T(8,128)(2,1)}, bf16[144,512]{1,0:T(8,128)(2,1)S(1)}, u32[]{:S(2)}, u32[]{:S(2)}) collective-permute-start(bf16[144,512]{1,0:T(8,128)(2,1)} %refs_4_.1), channel_id=1, source_target_pairs={{0,1},{1,0},{2,3},{3,2},{4,5},{5,4},{6,7},{7,6},{8,9},{9,8},{10,11... | collective-permute-start | bytes 442376 | tf_op jit(solution)/shard_map/ppermute | solution.py:257
  20.7 32.4 %all-to-all-start.1 = ((bf16[64,4,384]{2,1,0:T(4,128)(2,1)}), bf16[64,4,384]{2,1,0:T(4,128)(2,1)S(1)}, u32[]{:S(2)}, u32[]{:S(2)}) async-start(bf16[64,4,384]{2,1,0:T(4,128)(2,1)} %reshape.22), calls=%async_computation.1 | async-start | bytes 393216 | tf_op jit(solution)/shard_map/all_to_all | solution.py:253
  30.1 0.9 copy-start
  34.1 12.7 %collective-permute-start.2 = (bf16[4,144,512]{2,1,0:T(8,128)(2,1)S(1)}, bf16[4,144,512]{2,1,0:T(8,128)(2,1)S(1)}, u32[]{:S(2)}, u32[]{:S(2)}) collective-permute-start(bf16[4,144,512]{2,1,0:T(8,128)(2,1)S(1)} %get-tuple-element.17), channel_id=1, source_target_pairs={{0,2},{1,15},{2,0},{3,5},{4,6},{5,3},{6,4},{7,9},{8,10},{9,7},{10,... | collective-permute-start | bytes 1769480 | tf_op jit(solution)/shard_map/ppermute | solution.py:272
  39.3 21.2 %copy-start.3 = (s32[144,1]{0,1:T(1,128)S(1)}, s32[144,1]{0,1:T(1,128)}, u32[]{:S(2)}) copy-start(s32[144,1]{0,1:T(1,128)} %param.9) | copy-start | bytes 1732
  39.3 56.3 %copy-start.1 = (bf16[144,512]{1,0:T(8,128)(2,1)S(1)}, bf16[144,512]{1,0:T(8,128)(2,1)}, u32[]{:S(2)}) copy-start(bf16[144,512]{1,0:T(8,128)(2,1)} %refs_4_.1) | copy-start | bytes 442372
  46.9 8.7 %collective-permute-start.3 = (bf16[144,512]{1,0:T(8,128)(2,1)S(1)}, bf16[144,512]{1,0:T(8,128)(2,1)S(1)}, u32[]{:S(2)}, u32[]{:S(2)}) collective-permute-start(bf16[144,512]{1,0:T(8,128)(2,1)S(1)} %get-tuple-element.19), channel_id=1, source_target_pairs={{0,4},{1,13},{2,6},{3,15},{4,8},{5,1},{6,10},{7,3},{8,12},{9,5},{1... | collective-permute-start | bytes 442376 | tf_op jit(solution)/shard_map/ppermute | solution.py:247
  51.1 9.4 %collective-permute-start.4 = (bf16[144,512]{1,0:T(8,128)(2,1)S(1)}, bf16[144,512]{1,0:T(8,128)(2,1)S(1)}, u32[]{:S(2)}, u32[]{:S(2)}) collective-permute-start(bf16[144,512]{1,0:T(8,128)(2,1)S(1)} %get-tuple-element.21), channel_id=1, source_target_pairs={{0,12},{1,5},{2,14},{3,7},{4,0},{5,9},{6,2},{7,11},{8,4},{9,13},{1... | collective-permute-start | bytes 442376 | tf_op jit(solution)/shard_map/ppermute | solution.py:247
  60.9 11.1 %collective-permute-start.7 = (bf16[144,512]{1,0:T(8,128)(2,1)S(1)}, bf16[144,512]{1,0:T(8,128)(2,1)S(1)}, u32[]{:S(2)}, u32[]{:S(2)}) collective-permute-start(bf16[144,512]{1,0:T(8,128)(2,1)S(1)} %shard_map.84.refs_0_), channel_id=1, source_target_pairs={{0,4},{1,13},{2,6},{3,15},{4,8},{5,1},{6,10},{7,3},{8,12},{9,5},{1... | collective-permute-start | bytes 442376 | tf_op jit(solution)/shard_map/ppermute | solution.py:247
  65.2 12.3 %collective-permute-start.5 = (bf16[144,512]{1,0:T(8,128)(2,1)S(1)}, bf16[144,512]{1,0:T(8,128)(2,1)S(1)}, u32[]{:S(2)}, u32[]{:S(2)}) collective-permute-start(bf16[144,512]{1,0:T(8,128)(2,1)S(1)} %get-tuple-element.23), channel_id=1, source_target_pairs={{0,4},{1,13},{2,6},{3,15},{4,8},{5,1},{6,10},{7,3},{8,12},{9,5},{1... | collective-permute-start | bytes 442376 | tf_op jit(solution)/shard_map/ppermute | solution.py:247
  70.1 23.4 %collective-permute-start.6 = (bf16[144,512]{1,0:T(8,128)(2,1)S(1)}, bf16[144,512]{1,0:T(8,128)(2,1)S(1)}, u32[]{:S(2)}, u32[]{:S(2)}) collective-permute-start(bf16[144,512]{1,0:T(8,128)(2,1)S(1)} %shard_map.84.refs_0_), channel_id=1, source_target_pairs={{0,12},{1,5},{2,14},{3,7},{4,0},{5,9},{6,2},{7,11},{8,4},{9,13},{1... | collective-permute-start | bytes 442376 | tf_op jit(solution)/shard_map/ppermute | solution.py:247
  72.0 21.5 %collective-permute-start.8 = (bf16[144,512]{1,0:T(8,128)(2,1)S(1)}, bf16[144,512]{1,0:T(8,128)(2,1)S(1)}, u32[]{:S(2)}, u32[]{:S(2)}) collective-permute-start(bf16[144,512]{1,0:T(8,128)(2,1)S(1)} %collective-permute-done.7.refs_3_), channel_id=1, source_target_pairs={{0,4},{1,13},{2,6},{3,15},{4,8},{5,1},{6,10},{7,3},{8,12},{9,5},{1... | collective-permute-start | bytes 442376 | tf_op jit(solution)/shard_map/ppermute | solution.py:247
  78.7 34.9 %all-to-all-start = ((bf16[64,4,384]{2,1,0:T(4,128)(2,1)}), bf16[64,4,384]{2,1,0:T(4,128)(2,1)S(1)}, u32[]{:S(2)}, u32[]{:S(2)}) async-start(bf16[64,4,384]{2,1,0:T(4,128)(2,1)} %reshape.20), calls=%async_computation | async-start | bytes 393216 | tf_op jit(solution)/shard_map/all_to_all | solution.py:253
  93.6 12.1 %collective-permute-start.9 = (bf16[4,144,512]{2,1,0:T(8,128)(2,1)S(1)}, bf16[4,144,512]{2,1,0:T(8,128)(2,1)S(1)}, u32[]{:S(2)}, u32[]{:S(2)}) collective-permute-start(bf16[4,144,512]{2,1,0:T(8,128)(2,1)S(1)} %pad_maximum_fusion), channel_id=1, source_target_pairs={{0,2},{1,15},{2,0},{3,5},{4,6},{5,3},{6,4},{7,9},{8,10},{9,7},{10,... | collective-permute-start | bytes 1769480 | tf_op jit(solution)/shard_map/ppermute | solution.py:310
  105.7 8.0 %copy-start.2 = (bf16[384,512]{1,0:T(8,128)(2,1)S(1)}, bf16[384,512]{1,0:T(8,128)(2,1)}, u32[]{:S(2)}) copy-start(bf16[384,512]{1,0:T(8,128)(2,1)} %text_ref.1) | copy-start | bytes 1179652
  105.7 8.0 %copy-start.4 = (s32[1,192]{1,0:T(1,128)S(1)}, s32[1,192]{1,0:T(1,128)}, u32[]{:S(2)}) copy-start(s32[1,192]{1,0:T(1,128)} %offsets_ref.3) | copy-start | bytes 2308
  109.2 5.7 %collective-permute-start.10 = (bf16[144,512]{1,0:T(8,128)(2,1)S(1)}, bf16[144,512]{1,0:T(8,128)(2,1)S(1)}, u32[]{:S(2)}, u32[]{:S(2)}) collective-permute-start(bf16[144,512]{1,0:T(8,128)(2,1)S(1)} %get-tuple-element.28), channel_id=1, source_target_pairs={{0,1},{1,0},{2,3},{3,2},{4,5},{5,4},{6,7},{7,6},{8,9},{9,8},{10,11... | collective-permute-start | bytes 442376 | tf_op jit(solution)/shard_map/ppermute | solution.py:330

commit v4 on v3

--- a/solution.py
+++ b/solution.py
@@ -55,7 +55,8 @@
     rows = lax.dot_general(
         pick, arrived_ref[...], (((0,), (0,)), ((), ())), preferred_element_type=F32
     ).astype(BF16)
-    out_ref[...] = rows
+    for j in range(out_ref.shape[0]):
+        out_ref[j] = rows
 
 
 def route_kernel(groups, capacity, dest_ref, total_ref, last_ref, out_ref):
@@ -125,30 +126,30 @@
         out_ref[j] = total.astype(BF16)
 
 
-def add_kernel(kept_ref, beside_ref, total_ref, *term_refs):
+def add_kernel(kept_ref, beside_ref, token_ref, total_ref, *term_refs):
+    token_ref[...] = jnp.zeros_like(token_ref)
     total_ref[...] = kept_ref[0].astype(F32) + beside_ref[0].astype(F32)
     for j, term_ref in enumerate(term_refs, 1):
         total = kept_ref[j].astype(F32) + beside_ref[j].astype(F32)
         term_ref[...] = total.astype(term_ref.dtype)
 
 
-def relay_kernel(held_ref, arrived_ref, total_ref, back_ref, out_ref, sum_ref, token_ref):
-    token_ref[...] = jnp.zeros_like(token_ref)
+def relay_kernel(held_ref, arrived_ref, total_ref, back_ref, out_ref, sum_ref):
     out_ref[...] = (held_ref[...] + arrived_ref[...].astype(F32)).astype(BF16)
     sum_ref[...] = total_ref[...] + back_ref[...].astype(F32)
 
 
-def backward_first_kernel(blocks, at_ref, *refs):
-    grad_refs, refs = refs[:blocks], refs[blocks:]
-    pre_ref, w_own_ref, w_other_ref, own_ref, other_ref, slope_ref, held_ref, sems = refs
+def backward_first_kernel(
+    at_ref, grad_ref, pre_ref, w_own_ref, w_other_ref, own_ref, other_ref, slope_ref, held_ref, sems
+):
     copies = fetch(at_ref, (w_own_ref, w_other_ref), held_ref, sems)
     slope_ref[...] = gelu_slope(pre_ref[...].astype(F32))
     own, other = 0.0, 0.0
-    for grad_ref, j, pair in zip(grad_refs, range(blocks), copies):
+    for j, pair in enumerate(copies):
         for copy in pair:
             copy.wait()
-        own += lax.dot_general(grad_ref[...], held_ref[0, j], TRANS, preferred_element_type=F32)
-        other += lax.dot_general(grad_ref[...], held_ref[1, j], TRANS, preferred_element_type=F32)
+        own += lax.dot_general(grad_ref[j], held_ref[0, j], TRANS, preferred_element_type=F32)
+        other += lax.dot_general(grad_ref[j], held_ref[1, j], TRANS, preferred_element_type=F32)
     own_ref[...] = own
     other_ref[...] = other
 
@@ -239,6 +240,8 @@
             odd = (i + c) % 2
             beside.append((2 * i + c, 2 * ((i + (-1 if odd else 1)) % lines) + c))
 
+    alike = [list(range(0, lines, 2)), list(range(1, lines, 2))]
+
     def relay(x, by):
         pairs = []
         for i in range(lines):
@@ -250,8 +253,7 @@
         return x.reshape(groups, 4, capacity * width // 4)
 
     def exchange(x):
-        x = lax.all_to_all(x, "group", split_axis=0, concat_axis=0, tiled=True)
-        return x.reshape(slots, width)
+        return lax.all_to_all(x, "group", split_axis=0, concat_axis=0, tiled=True)
 
     w_other = lax.ppermute(proj_weight, "core", cores)
     pre_other = lax.ppermute(pre_hidden, "core", cores)
@@ -271,17 +273,17 @@
     )
     beside_terms = lax.ppermute(sent, ("line", "core"), beside)
     kept = product(forward_second_kernel, [terms_out], same, (act,), weights, half)
-    total, first, second, third = call(
+    token, total, first, second, third = call(
         add_kernel,
-        [((rows, width), F32)] * 2 + [((rows, width), BF16)] * 2,
+        [((8, 128), F32)] + [((rows, width), F32)] * 2 + [((rows, width), BF16)] * 2,
         kept,
         beside_terms,
     )
     passed = relay(second, 2)
     back = relay(third, -2)
-    first, total, token = call(
+    first, total = call(
         relay_kernel,
-        [((rows, width), BF16), ((rows, width), F32), ((8, 128), F32)],
+        [((rows, width), BF16), ((rows, width), F32)],
         first,
         passed,
         total,
@@ -298,22 +300,27 @@
     outgoing = by_group(outgoing)
     arrived = exchange(outgoing)
 
+    returned, token = lax.optimization_barrier((returned, token))
+    returned = returned.reshape(slots, width)
     mine = call(
         functools.partial(owner_rows_kernel, groups, capacity),
-        [((rows, width), BF16)],
+        [terms_out],
         dest_row,
         returned,
         token,
     )
-    last = relay(mine, 2)
-    near = [mine, relay(mine, -2), relay(last, 2), last]
-    far = lax.ppermute(jnp.stack(near), ("line", "core"), beside)
+    near = lax.all_to_all(
+        mine, "line", split_axis=0, concat_axis=0, tiled=True, axis_index_groups=alike
+    )
+    far = lax.ppermute(near, ("line", "core"), beside)
+    parity = lax.rem(line, 2)
+    every = 4 * jnp.arange(half, dtype=jnp.int32) + core
     wide = ((rows, hid), F32)
     own, other, slope = product(
-        functools.partial(backward_first_kernel, half),
+        backward_first_kernel,
         [wide] * 3,
-        same,
-        (*near, pre_hidden),
+        every + 2 * parity,
+        (near, pre_hidden),
         weights,
         half,
         1000,
@@ -321,7 +328,7 @@
     own, other = product(
         backward_second_kernel,
         [wide, ((rows, hid), BF16)],
-        opposite,
+        every + 2 * (1 - parity),
         (far, own, other),
         weights,
         half,
@@ -331,7 +338,7 @@
     grad_hidden = call(slope_kernel, [((rows, hid), BF16)], own, other, slope, final=True)
 
     packed = call(
-        place_kernel, [(text_embed.shape, BF16)], place, arrived, text_embed, final=True
+        place_kernel, [(text_embed.shape, BF16)], place, arrived.reshape(slots, width), text_embed, final=True
     )
     return (packed, grad_hidden)
 

time: 116 us -> 124 us (1.069)
  waiting for transfers between devices: 18 us -> 28.9 us
  starting transfers between devices: 76.2 us -> 72 us
    ppermute x6 -> x3, waiting for transfers between devices: 7.2 us -> 20.8 us  [relay(): return lax.ppermute(x, ('line', 'core'), pairs)]
    ppermute x6 -> x3, starting transfers between devices: 22.7 us -> 10.3 us  [relay(): return lax.ppermute(x, ('line', 'core'), pairs)]
    all_to_all x2 -> x3, starting transfers between devices: 24.1 us -> 29.3 us  [the longest x2 22.8 us: exchange(): return lax.all_to_all(x, 'group', split_axis=0, concat_axis=0, tiled=True)]
    ppermute x1, starting transfers between devices: 1.92 us -> 5.08 us  [on_device(): far = lax.ppermute(near, ('line', 'core'), beside)]
    ppermute x1, waiting for transfers between devices: 6.46 us -> 3.78 us  [on_device(): far = lax.ppermute(near, ('line', 'core'), beside)]
  transfers between devices with their start and end apart: 13 -> 11, of which waited for: 4 -> 4; matrix products, arithmetic and copies ran while one was open for 2% -> 1% of each run, Pallas kernels for 14% -> 13%
where the time goes in v4:
time: 124 us; the launch traced here: 123 us
  starting transfers between devices  72 us (58%)
  waiting for transfers between devices  28.9 us (23%)
  Pallas kernels  18.5 us (15%)
  local copies, waits for them, and re-layouts  2.76 us (2%)
    all_to_all x2, starting transfers between devices, exchange(): return lax.all_to_all(x, 'group', split_axis=0, concat_axis=0, tiled=True)  22.8 us
    ppermute x3, waiting for transfers between devices, relay(): return lax.ppermute(x, ('line', 'core'), pairs)  20.8 us
    ppermute x1, starting transfers between devices, on_device(): w_other = lax.ppermute(proj_weight, 'core', cores)  16.1 us
    pallas_call x4, Pallas kernels, product(): pl.pallas_call(kernel, in_specs=[SMEM] + [VMEM] * len(args) + [HBM] * 2,...  13.4 us
    ppermute x3, starting transfers between devices, relay(): return lax.ppermute(x, ('line', 'core'), pairs)  10.3 us
    all_to_all x1, starting transfers between devices, on_device(): lax.all_to_all(mine, 'line', split_axis=0, concat_axis=0, tiled=True, axi...  6.56 us
    ppermute x1, starting transfers between devices, on_device(): beside_terms = lax.ppermute(sent, ('line', 'core'), beside)  5.1 us
    ppermute x1, starting transfers between devices, on_device(): far = lax.ppermute(near, ('line', 'core'), beside)  5.08 us
  transfers between devices with their start and end apart: 11, of which 4 were waited for; matrix products, arithmetic and copies ran while one was open for 1% of the time, Pallas kernels for 13%

profile of v4, /device:TPU:1, one launch (start us, length us, event | category | flops | bytes accessed | tf_op | source)
XLA Modules:
  0.0 123.1 jit_solution(16326267085969780646)
XLA Ops:
  0.6 16.1 %collective-permute-start.1 = (bf16[512,8192]{1,0:T(8,128)(2,1)}, bf16[512,8192]{1,0:T(8,128)(2,1)}, u32[]{:S(2)}, u32[]{:S(2)}) collective-permute-start(bf16[512,8192]{1,0:T(8,128)(2,1)} %w_own_ref.7), channel_id=1, source_target_pairs={{0,1},{1,0},{2,3},{3,2},{4,5},{5,4},{6,7},{7,6},{8,9},{9,8},{10,11... | collective-permute-start | bytes 25165832 | tf_op jit(solution)/shard_map/ppermute | solution.py:258
  16.7 1.9 %collective-permute-start = (bf16[144,512]{1,0:T(8,128)(2,1)}, bf16[144,512]{1,0:T(8,128)(2,1)S(1)}, u32[]{:S(2)}, u32[]{:S(2)}) collective-permute-start(bf16[144,512]{1,0:T(8,128)(2,1)} %pre_ref.1), channel_id=1, source_target_pairs={{0,1},{1,0},{2,3},{3,2},{4,5},{5,4},{6,7},{7,6},{8,9},{9,8},{10,11... | collective-permute-start | bytes 442376 | tf_op jit(solution)/shard_map/ppermute | solution.py:259
  18.6 1.3 %shard_map.83 = bf16[192,512]{1,0:T(8,128)(2,1)S(1)} custom-call(s32[1,192]{1,0:T(1,128)} %offsets_ref.3, bf16[384,512]{1,0:T(8,128)(2,1)} %grad_ref.1), custom_call_target="tpu_custom_call" | custom-call | tf_op jit(solution)/shard_map/pallas_call | solution.py:191
  19.9 0.8 reshape.22
  20.7 9.3 %all-to-all-start.1 = ((bf16[64,4,384]{2,1,0:T(4,128)(2,1)}), bf16[64,4,384]{2,1,0:T(4,128)(2,1)S(1)}, u32[]{:S(2)}, u32[]{:S(2)}) async-start(bf16[64,4,384]{2,1,0:T(4,128)(2,1)} %reshape.22), calls=%async_computation.1 | async-start | bytes 393216 | tf_op jit(solution)/shard_map/all_to_all | solution.py:256
  30.1 0.9 copy-done
  31.0 3.1 %shard_map.77 = (bf16[4,144,512]{2,1,0:T(8,128)(2,1)S(1)}, bf16[144,1024]{1,0:T(8,128)(2,1)S(1)}) custom-call(s32[4]{0:T(128)S(1)} %fusion.5.at_ref, bf16[144,512]{1,0:T(8,128)(2,1)S(1)} %copy-done, bf16[144,512]{1,0:T(8,128)(2,1)S(1)} %collective-permute-done.other_ref, bf16[512,8192]{1,0:T(8,128)(2,1)} %w_own_ref.7, ...), custom_call_target="tpu_custom_call" | custom-call | flops 603979776 | bytes 4194304 | tf_op jit(solution)/shard_map/pallas_call | solution.py:203
  34.1 5.1 %collective-permute-start.2 = (bf16[4,144,512]{2,1,0:T(8,128)(2,1)S(1)}, bf16[4,144,512]{2,1,0:T(8,128)(2,1)S(1)}, u32[]{:S(2)}, u32[]{:S(2)}) collective-permute-start(bf16[4,144,512]{2,1,0:T(8,128)(2,1)S(1)} %get-tuple-element.19), channel_id=1, source_target_pairs={{0,2},{1,15},{2,0},{3,5},{4,6},{5,3},{6,4},{7,9},{8,10},{9,7},{10,... | collective-permute-start | bytes 1769480 | tf_op jit(solution)/shard_map/ppermute | solution.py:274
  39.3 3.1 %shard_map.78.kept_ref = bf16[4,144,512]{2,1,0:T(8,128)(2,1)S(1)} custom-call(s32[4]{0:T(128)S(1)} %fusion.2.at_ref, bf16[144,1024]{1,0:T(8,128)(2,1)S(1)} %get-tuple-element.18.act_ref, bf16[512,8192]{1,0:T(8,128)(2,1)} %w_own_ref.7, bf16[512,8192]{1,0:T(8,128)(2,1)} %collective-permute-done.1.w_other_ref), custom_call_target="tpu_custom_call" | custom-call | flops 603979776 | bytes 4194304 | tf_op jit(solution)/shard_map/pallas_call | solution.py:203
  42.4 4.4 %collective-permute-done.2.beside_ref = bf16[4,144,512]{2,1,0:T(8,128)(2,1)S(1)} collective-permute-done((bf16[4,144,512]{2,1,0:T(8,128)(2,1)S(1)}, bf16[4,144,512]{2,1,0:T(8,128)(2,1)S(1)}, u32[]{:S(2)}, u32[]{:S(2)}) %collective-permute-start.2) | collective-permute-done | bytes 589856 | tf_op jit(solution)/shard_map/ppermute | solution.py:274
  47.1 1.3 %shard_map.84 = bf16[4,144,512]{2,1,0:T(8,128)(2,1)} custom-call(s32[1,144]{1,0:T(1,128)S(1)} %bitcast.1, bf16[192,512]{1,0:T(8,128)(2,1)S(1)} %reshape.23.arrived_ref, f32[8,128]{1,0:T(8,128)S(1)} %get-tuple-element.28.token_ref), custom_call_target="tpu_custom_call" | custom-call | tf_op jit(solution)/shard_map/pallas_call | solution.py:191
  48.4 6.6 %all-to-all-start.2 = ((bf16[4,144,512]{2,1,0:T(8,128)(2,1)}), bf16[4,144,512]{2,1,0:T(8,128)(2,1)S(1)}, u32[]{:S(2)}, u32[]{:S(2)}) async-start(bf16[4,144,512]{2,1,0:T(8,128)(2,1)} %shard_map.84), calls=%async_computation.2 | async-start | bytes 1179648 | tf_op jit(solution)/shard_map/all_to_all | solution.py:312
  55.0 5.5 %collective-permute-start.3 = (bf16[144,512]{1,0:T(8,128)(2,1)S(1)}, bf16[144,512]{1,0:T(8,128)(2,1)S(1)}, u32[]{:S(2)}, u32[]{:S(2)}) collective-permute-start(bf16[144,512]{1,0:T(8,128)(2,1)S(1)} %get-tuple-element.21), channel_id=1, source_target_pairs={{0,4},{1,13},{2,6},{3,15},{4,8},{5,1},{6,10},{7,3},{8,12},{9,5},{1... | collective-permute-start | bytes 442376 | tf_op jit(solution)/shard_map/ppermute | solution.py:250
  60.4 1.9 %collective-permute-start.4 = (bf16[144,512]{1,0:T(8,128)(2,1)S(1)}, bf16[144,512]{1,0:T(8,128)(2,1)S(1)}, u32[]{:S(2)}, u32[]{:S(2)}) collective-permute-start(bf16[144,512]{1,0:T(8,128)(2,1)S(1)} %get-tuple-element.23), channel_id=1, source_target_pairs={{0,12},{1,5},{2,14},{3,7},{4,0},{5,9},{6,2},{7,11},{8,4},{9,13},{1... | collective-permute-start | bytes 442376 | tf_op jit(solution)/shard_map/ppermute | solution.py:250
  62.4 15.2 %collective-permute-done.3.arrived_ref = bf16[144,512]{1,0:T(8,128)(2,1)S(1)} collective-permute-done((bf16[144,512]{1,0:T(8,128)(2,1)S(1)}, bf16[144,512]{1,0:T(8,128)(2,1)S(1)}, u32[]{:S(2)}, u32[]{:S(2)}) %collective-permute-start.3) | collective-permute-done | bytes 147488 | tf_op jit(solution)/shard_map/ppermute | solution.py:250
  77.6 2.9 %collective-permute-start.5 = (bf16[144,512]{1,0:T(8,128)(2,1)S(1)}, bf16[144,512]{1,0:T(8,128)(2,1)S(1)}, u32[]{:S(2)}, u32[]{:S(2)}) collective-permute-start(bf16[144,512]{1,0:T(8,128)(2,1)S(1)} %get-tuple-element.25), channel_id=1, source_target_pairs={{0,4},{1,13},{2,6},{3,15},{4,8},{5,1},{6,10},{7,3},{8,12},{9,5},{1... | collective-permute-start | bytes 442376 | tf_op jit(solution)/shard_map/ppermute | solution.py:250
  80.5 5.6 %collective-permute-done.5.last_ref = bf16[144,512]{1,0:T(8,128)(2,1)S(1)} collective-permute-done((bf16[144,512]{1,0:T(8,128)(2,1)S(1)}, bf16[144,512]{1,0:T(8,128)(2,1)S(1)}, u32[]{:S(2)}, u32[]{:S(2)}) %collective-permute-start.5) | collective-permute-done | bytes 147488 | tf_op jit(solution)/shard_map/ppermute | solution.py:250
  87.3 13.5 %all-to-all-start = ((bf16[64,4,384]{2,1,0:T(4,128)(2,1)}), bf16[64,4,384]{2,1,0:T(4,128)(2,1)S(1)}, u32[]{:S(2)}, u32[]{:S(2)}) async-start(bf16[64,4,384]{2,1,0:T(4,128)(2,1)} %reshape.20), calls=%async_computation | async-start | bytes 393216 | tf_op jit(solution)/shard_map/all_to_all | solution.py:256
  100.8 5.1 %collective-permute-start.6 = (bf16[4,144,512]{2,1,0:T(8,128)(2,1)S(1)}, bf16[4,144,512]{2,1,0:T(8,128)(2,1)S(1)}, u32[]{:S(2)}, u32[]{:S(2)}) collective-permute-start(bf16[4,144,512]{2,1,0:T(8,128)(2,1)S(1)} %all-to-all-done.2.grad_ref), channel_id=1, source_target_pairs={{0,2},{1,15},{2,0},{3,5},{4,6},{5,3},{6,4},{7,9},{8,10},{9,7},{10,... | collective-permute-start | bytes 1769480 | tf_op jit(solution)/shard_map/ppermute | solution.py:315
  105.9 3.7 %shard_map.85 = (f32[144,512]{1,0:T(8,128)S(1)}, f32[144,512]{1,0:T(8,128)S(1)}, f32[144,512]{1,0:T(8,128)S(1)}) custom-call(s32[4]{0:T(128)S(1)} %fusion.6.at_ref, bf16[4,144,512]{2,1,0:T(8,128)(2,1)S(1)} %all-to-all-done.2.grad_ref, bf16[144,512]{1,0:T(8,128)(2,1)S(1)} %copy-done.1, bf16[512,8192]{1,0:T(8,128)(2,1)} %w_own_ref.7, ...), custom_call_target="tpu_custom_call" | custom-call | flops 603979 | bytes 4194 | tf_op jit(solution)/shard_map/pallas_call | solution.py:203
  109.6 3.8 %collective-permute-done.6.grad_ref = bf16[4,144,512]{2,1,0:T(8,128)(2,1)S(1)} collective-permute-done((bf16[4,144,512]{2,1,0:T(8,128)(2,1)S(1)}, bf16[4,144,512]{2,1,0:T(8,128)(2,1)S(1)}, u32[]{:S(2)}, u32[]{:S(2)}) %collective-permute-start.6) | collective-permute-done | bytes 589856 | tf_op jit(solution)/shard_map/ppermute | solution.py:315
  113.4 3.4 %shard_map.86 = (f32[144,512]{1,0:T(8,128)S(1)}, bf16[144,512]{1,0:T(8,128)(2,1)S(1)}) custom-call(s32[4]{0:T(128)S(1)} %fusion.7.at_ref, bf16[4,144,512]{2,1,0:T(8,128)(2,1)S(1)} %collective-permute-done.6.grad_ref, f32[144,512]{1,0:T(8,128)S(1)} %get-tuple-element.29.own_in, f32[144,512]{1,0:T(8,128)S(1)} %get-tuple-element.30.other_in, ...), custom_call_target="tpu_custom_call" | custom-call | flops 603979 | bytes 4194 | tf_op jit(solution)/shard_map/pallas_call | solution.py:203
  116.9 4.2 %collective-permute-start.7 = (bf16[144,512]{1,0:T(8,128)(2,1)S(1)}, bf16[144,512]{1,0:T(8,128)(2,1)S(1)}, u32[]{:S(2)}, u32[]{:S(2)}) collective-permute-start(bf16[144,512]{1,0:T(8,128)(2,1)S(1)} %get-tuple-element.32), channel_id=1, source_target_pairs={{0,1},{1,0},{2,3},{3,2},{4,5},{5,4},{6,7},{7,6},{8,9},{9,8},{10,11... | collective-permute-start | bytes 442376 | tf_op jit(solution)/shard_map/ppermute | solution.py:337
  121.2 1.2 shard_map.82
  (27 shorter events, 2.4 us)
Async XLA Ops:
  0.6 29.5 %collective-permute-start.1 = (bf16[512,8192]{1,0:T(8,128)(2,1)}, bf16[512,8192]{1,0:T(8,128)(2,1)}, u32[]{:S(2)}, u32[]{:S(2)}) collective-permute-start(bf16[512,8192]{1,0:T(8,128)(2,1)} %w_own_ref.7), channel_id=1, source_target_pairs={{0,1},{1,0},{2,3},{3,2},{4,5},{5,4},{6,7},{7,6},{8,9},{9,8},{10,11... | collective-permute-start | bytes 25165832 | tf_op jit(solution)/shard_map/ppermute | solution.py:258
  16.7 13.4 %collective-permute-start = (bf16[144,512]{1,0:T(8,128)(2,1)}, bf16[144,512]{1,0:T(8,128)(2,1)S(1)}, u32[]{:S(2)}, u32[]{:S(2)}) collective-permute-start(bf16[144,512]{1,0:T(8,128)(2,1)} %pre_ref.1), channel_id=1, source_target_pairs={{0,1},{1,0},{2,3},{3,2},{4,5},{5,4},{6,7},{7,6},{8,9},{9,8},{10,11... | collective-permute-start | bytes 442376 | tf_op jit(solution)/shard_map/ppermute | solution.py:259
  20.7 26.2 %all-to-all-start.1 = ((bf16[64,4,384]{2,1,0:T(4,128)(2,1)}), bf16[64,4,384]{2,1,0:T(4,128)(2,1)S(1)}, u32[]{:S(2)}, u32[]{:S(2)}) async-start(bf16[64,4,384]{2,1,0:T(4,128)(2,1)} %reshape.22), calls=%async_computation.1 | async-start | bytes 393216 | tf_op jit(solution)/shard_map/all_to_all | solution.py:256
  30.1 0.9 copy-start
  34.1 12.7 %collective-permute-start.2 = (bf16[4,144,512]{2,1,0:T(8,128)(2,1)S(1)}, bf16[4,144,512]{2,1,0:T(8,128)(2,1)S(1)}, u32[]{:S(2)}, u32[]{:S(2)}) collective-permute-start(bf16[4,144,512]{2,1,0:T(8,128)(2,1)S(1)} %get-tuple-element.19), channel_id=1, source_target_pairs={{0,2},{1,15},{2,0},{3,5},{4,6},{5,3},{6,4},{7,9},{8,10},{9,7},{10,... | collective-permute-start | bytes 1769480 | tf_op jit(solution)/shard_map/ppermute | solution.py:274
  39.3 7.8 %copy-start.3 = (s32[144,1]{0,1:T(1,128)S(1)}, s32[144,1]{0,1:T(1,128)}, u32[]{:S(2)}) copy-start(s32[144,1]{0,1:T(1,128)} %param.9) | copy-start | bytes 1732
  39.3 66.6 %copy-start.1 = (bf16[144,512]{1,0:T(8,128)(2,1)S(1)}, bf16[144,512]{1,0:T(8,128)(2,1)}, u32[]{:S(2)}) copy-start(bf16[144,512]{1,0:T(8,128)(2,1)} %pre_ref.1) | copy-start | bytes 442372
  48.4 38.9 %all-to-all-start.2 = ((bf16[4,144,512]{2,1,0:T(8,128)(2,1)}), bf16[4,144,512]{2,1,0:T(8,128)(2,1)S(1)}, u32[]{:S(2)}, u32[]{:S(2)}) async-start(bf16[4,144,512]{2,1,0:T(8,128)(2,1)} %shard_map.84), calls=%async_computation.2 | async-start | bytes 1179648 | tf_op jit(solution)/shard_map/all_to_all | solution.py:312
  55.0 22.6 %collective-permute-start.3 = (bf16[144,512]{1,0:T(8,128)(2,1)S(1)}, bf16[144,512]{1,0:T(8,128)(2,1)S(1)}, u32[]{:S(2)}, u32[]{:S(2)}) collective-permute-start(bf16[144,512]{1,0:T(8,128)(2,1)S(1)} %get-tuple-element.21), channel_id=1, source_target_pairs={{0,4},{1,13},{2,6},{3,15},{4,8},{5,1},{6,10},{7,3},{8,12},{9,5},{1... | collective-permute-start | bytes 442376 | tf_op jit(solution)/shard_map/ppermute | solution.py:250
  60.4 17.1 %collective-permute-start.4 = (bf16[144,512]{1,0:T(8,128)(2,1)S(1)}, bf16[144,512]{1,0:T(8,128)(2,1)S(1)}, u32[]{:S(2)}, u32[]{:S(2)}) collective-permute-start(bf16[144,512]{1,0:T(8,128)(2,1)S(1)} %get-tuple-element.23), channel_id=1, source_target_pairs={{0,12},{1,5},{2,14},{3,7},{4,0},{5,9},{6,2},{7,11},{8,4},{9,13},{1... | collective-permute-start | bytes 442376 | tf_op jit(solution)/shard_map/ppermute | solution.py:250
  77.6 8.5 %collective-permute-start.5 = (bf16[144,512]{1,0:T(8,128)(2,1)S(1)}, bf16[144,512]{1,0:T(8,128)(2,1)S(1)}, u32[]{:S(2)}, u32[]{:S(2)}) collective-permute-start(bf16[144,512]{1,0:T(8,128)(2,1)S(1)} %get-tuple-element.25), channel_id=1, source_target_pairs={{0,4},{1,13},{2,6},{3,15},{4,8},{5,1},{6,10},{7,3},{8,12},{9,5},{1... | collective-permute-start | bytes 442376 | tf_op jit(solution)/shard_map/ppermute | solution.py:250
  87.3 33.8 %all-to-all-start = ((bf16[64,4,384]{2,1,0:T(4,128)(2,1)}), bf16[64,4,384]{2,1,0:T(4,128)(2,1)S(1)}, u32[]{:S(2)}, u32[]{:S(2)}) async-start(bf16[64,4,384]{2,1,0:T(4,128)(2,1)} %reshape.20), calls=%async_computation | async-start | bytes 393216 | tf_op jit(solution)/shard_map/all_to_all | solution.py:256
  100.8 12.6 %collective-permute-start.6 = (bf16[4,144,512]{2,1,0:T(8,128)(2,1)S(1)}, bf16[4,144,512]{2,1,0:T(8,128)(2,1)S(1)}, u32[]{:S(2)}, u32[]{:S(2)}) collective-permute-start(bf16[4,144,512]{2,1,0:T(8,128)(2,1)S(1)} %all-to-all-done.2.grad_ref), channel_id=1, source_target_pairs={{0,2},{1,15},{2,0},{3,5},{4,6},{5,3},{6,4},{7,9},{8,10},{9,7},{10,... | collective-permute-start | bytes 1769480 | tf_op jit(solution)/shard_map/ppermute | solution.py:315
  113.4 7.8 %copy-start.2 = (bf16[384,512]{1,0:T(8,128)(2,1)S(1)}, bf16[384,512]{1,0:T(8,128)(2,1)}, u32[]{:S(2)}) copy-start(bf16[384,512]{1,0:T(8,128)(2,1)} %text_ref.1) | copy-start | bytes 1179652
  113.4 7.8 %copy-start.4 = (s32[1,192]{1,0:T(1,128)S(1)}, s32[1,192]{1,0:T(1,128)}, u32[]{:S(2)}) copy-start(s32[1,192]{1,0:T(1,128)} %offsets_ref.3) | copy-start | bytes 2308
  116.9 5.6 %collective-permute-start.7 = (bf16[144,512]{1,0:T(8,128)(2,1)S(1)}, bf16[144,512]{1,0:T(8,128)(2,1)S(1)}, u32[]{:S(2)}, u32[]{:S(2)}) collective-permute-start(bf16[144,512]{1,0:T(8,128)(2,1)S(1)} %get-tuple-element.32), channel_id=1, source_target_pairs={{0,1},{1,0},{2,3},{3,2},{4,5},{5,4},{6,7},{7,6},{8,9},{9,8},{10,11... | collective-permute-start | bytes 442376 | tf_op jit(solution)/shard_map/ppermute | solution.py:337

commit v5 on v3

--- a/solution.py
+++ b/solution.py
@@ -48,19 +48,24 @@
     ).astype(BF16)
 
 
-def owner_rows_kernel(groups, capacity, dest_ref, arrived_ref, token_ref, out_ref):
-    slots = arrived_ref.shape[0]
-    pick = rows_by_target(dest_ref[...], groups, capacity, slots)
+def meet_kernel(groups, capacity, dest_ref, arrived_ref, kept_ref, beside_ref, *refs):
+    total_ref, first_ref, ahead_ref, back_ref = refs
+    pick = rows_by_target(dest_ref[...], groups, capacity, arrived_ref.shape[0])
     pick = jnp.where(pick, 1.0, 0.0).astype(BF16)
     rows = lax.dot_general(
         pick, arrived_ref[...], (((0,), (0,)), ((), ())), preferred_element_type=F32
     ).astype(BF16)
-    out_ref[...] = rows
-
-
-def route_kernel(groups, capacity, dest_ref, total_ref, last_ref, out_ref):
+    total_ref[...] = kept_ref[0].astype(F32) + beside_ref[0].astype(F32)
+    first_ref[...] = kept_ref[1].astype(F32) + beside_ref[1].astype(F32)
+    ahead_ref[0] = (kept_ref[2].astype(F32) + beside_ref[2].astype(F32)).astype(BF16)
+    ahead_ref[1] = rows
+    back_ref[0] = (kept_ref[3].astype(F32) + beside_ref[3].astype(F32)).astype(BF16)
+    back_ref[1] = rows
+
+
+def route_kernel(groups, capacity, dest_ref, total_ref, back_ref, last_ref, out_ref):
     slots = out_ref.shape[0]
-    total = total_ref[...] + last_ref[...].astype(F32)
+    total = total_ref[...] + back_ref[0].astype(F32) + last_ref[0].astype(F32)
     hit = rows_by_target(dest_ref[...], groups, capacity, slots)
     pick = jnp.where(hit, 1.0, 0.0)
     sent = jnp.dot(pick.astype(BF16), total.astype(BF16), preferred_element_type=F32)
@@ -125,17 +130,9 @@
         out_ref[j] = total.astype(BF16)
 
 
-def add_kernel(kept_ref, beside_ref, total_ref, *term_refs):
-    total_ref[...] = kept_ref[0].astype(F32) + beside_ref[0].astype(F32)
-    for j, term_ref in enumerate(term_refs, 1):
-        total = kept_ref[j].astype(F32) + beside_ref[j].astype(F32)
-        term_ref[...] = total.astype(term_ref.dtype)
-
-
-def relay_kernel(held_ref, arrived_ref, total_ref, back_ref, out_ref, sum_ref, token_ref):
-    token_ref[...] = jnp.zeros_like(token_ref)
-    out_ref[...] = (held_ref[...] + arrived_ref[...].astype(F32)).astype(BF16)
-    sum_ref[...] = total_ref[...] + back_ref[...].astype(F32)
+def relay_kernel(first_ref, arrived_ref, out_ref):
+    out_ref[0] = (first_ref[...] + arrived_ref[0].astype(F32)).astype(BF16)
+    out_ref[1] = arrived_ref[1]
 
 
 def backward_first_kernel(blocks, at_ref, *refs):
@@ -147,8 +144,8 @@
     for grad_ref, j, pair in zip(grad_refs, range(blocks), copies):
         for copy in pair:
             copy.wait()
-        own += lax.dot_general(grad_ref[...], held_ref[0, j], TRANS, preferred_element_type=F32)
-        other += lax.dot_general(grad_ref[...], held_ref[1, j], TRANS, preferred_element_type=F32)
+        own += lax.dot_general(grad_ref[1], held_ref[0, j], TRANS, preferred_element_type=F32)
+        other += lax.dot_general(grad_ref[1], held_ref[1, j], TRANS, preferred_element_type=F32)
     own_ref[...] = own
     other_ref[...] = other
 
@@ -250,8 +247,7 @@
         return x.reshape(groups, 4, capacity * width // 4)
 
     def exchange(x):
-        x = lax.all_to_all(x, "group", split_axis=0, concat_axis=0, tiled=True)
-        return x.reshape(slots, width)
+        return lax.all_to_all(x, "group", split_axis=0, concat_axis=0, tiled=True)
 
     w_other = lax.ppermute(proj_weight, "core", cores)
     pre_other = lax.ppermute(pre_hidden, "core", cores)
@@ -271,43 +267,32 @@
     )
     beside_terms = lax.ppermute(sent, ("line", "core"), beside)
     kept = product(forward_second_kernel, [terms_out], same, (act,), weights, half)
-    total, first, second, third = call(
-        add_kernel,
-        [((rows, width), F32)] * 2 + [((rows, width), BF16)] * 2,
+    returned, beside_terms = lax.optimization_barrier((returned, beside_terms))
+    pair = ((2, rows, width), BF16)
+    total, first, ahead, back = call(
+        functools.partial(meet_kernel, groups, capacity),
+        [((rows, width), F32)] * 2 + [pair] * 2,
+        dest_row,
+        returned.reshape(slots, width),
         kept,
         beside_terms,
     )
-    passed = relay(second, 2)
-    back = relay(third, -2)
-    first, total, token = call(
-        relay_kernel,
-        [((rows, width), BF16), ((rows, width), F32), ((8, 128), F32)],
-        first,
-        passed,
-        total,
-        back,
-    )
-    last = relay(first, 2)
+    passed = relay(ahead, 2)
+    back = relay(back, -2)
+    last = relay(call(relay_kernel, [pair], first, passed), 2)
     outgoing = call(
         functools.partial(route_kernel, groups, capacity),
         [((slots, width), BF16)],
         dest_row,
         total,
+        back,
         last,
     )
     outgoing = by_group(outgoing)
     arrived = exchange(outgoing)
 
-    mine = call(
-        functools.partial(owner_rows_kernel, groups, capacity),
-        [((rows, width), BF16)],
-        dest_row,
-        returned,
-        token,
-    )
-    last = relay(mine, 2)
-    near = [mine, relay(mine, -2), relay(last, 2), last]
-    far = lax.ppermute(jnp.stack(near), ("line", "core"), beside)
+    near = [ahead, back, last, passed]
+    far = lax.ppermute(jnp.stack([x[1] for x in near]), ("line", "core"), beside)
     wide = ((rows, hid), F32)
     own, other, slope = product(
         functools.partial(backward_first_kernel, half),
@@ -331,7 +316,7 @@
     grad_hidden = call(slope_kernel, [((rows, hid), BF16)], own, other, slope, final=True)
 
     packed = call(
-        place_kernel, [(text_embed.shape, BF16)], place, arrived, text_embed, final=True
+        place_kernel, [(text_embed.shape, BF16)], place, arrived.reshape(slots, width), text_embed, final=True
     )
     return (packed, grad_hidden)
 

time: 116 us -> 119 us (1.026); the launches traced: 116 us -> 117 us
  starting transfers between devices: 76.2 us -> 71.4 us
  waiting for transfers between devices: 18 us -> 21.6 us
  local copies, waits for them, and re-layouts: 2.76 us -> 4.48 us
    ppermute x6 -> x3, starting transfers between devices: 22.7 us -> 14.1 us  [relay(): return lax.ppermute(x, ('line', 'core'), pairs)]
    ppermute x6 -> x3, waiting for transfers between devices: 7.2 us -> 12.5 us  [relay(): return lax.ppermute(x, ('line', 'core'), pairs)]
    ppermute x1, waiting for transfers between devices: 4.37 us -> 0.07 us  [on_device(): beside_terms = lax.ppermute(sent, ('line', 'core'), beside)]
    all_to_all x2, waiting for transfers between devices: 0.01 us -> 4.3 us  [exchange(): return lax.all_to_all(x, 'group', split_axis=0, concat_axis=0, tiled=True)]
    ppermute x1, starting transfers between devices: 1.92 us -> 5.63 us  [on_device(): lax.ppermute(jnp.stack([x[1] for x in near]), ('line', 'core'), beside)]
    ppermute x1, starting transfers between devices: 4.37 us -> 7.14 us  [on_device(): other = lax.ppermute(other, 'core', cores)]
    ppermute x1, waiting for transfers between devices: 6.46 us -> 3.81 us  [on_device(): lax.ppermute(jnp.stack([x[1] for x in near]), ('line', 'core'), beside)]
    all_to_all x2, starting transfers between devices: 24.1 us -> 21.5 us  [exchange(): return lax.all_to_all(x, 'group', split_axis=0, concat_axis=0, tiled=True)]
  transfers between devices with their start and end apart: 13 -> 10, of which waited for: 4 -> 6; matrix products, arithmetic and copies ran while one was open for 2% -> 1% of each run, Pallas kernels for 14% -> 13%
where the time goes in v5:
time: 119 us; the launch traced here: 117 us
  starting transfers between devices  71.4 us (60%)
  waiting for transfers between devices  21.6 us (18%)
  Pallas kernels  18.2 us (15%)
  local copies, waits for them, and re-layouts  4.48 us (4%)
    all_to_all x2, starting transfers between devices, exchange(): return lax.all_to_all(x, 'group', split_axis=0, concat_axis=0, tiled=True)  21.5 us
    ppermute x1, starting transfers between devices, on_device(): w_other = lax.ppermute(proj_weight, 'core', cores)  16.1 us
    ppermute x3, starting transfers between devices, relay(): return lax.ppermute(x, ('line', 'core'), pairs)  14.1 us
    pallas_call x4, Pallas kernels, product(): pl.pallas_call(kernel, in_specs=[SMEM] + [VMEM] * len(args) + [HBM] * 2,...  13.4 us
    ppermute x3, waiting for transfers between devices, relay(): return lax.ppermute(x, ('line', 'core'), pairs)  12.5 us
    ppermute x1, starting transfers between devices, on_device(): other = lax.ppermute(other, 'core', cores)  7.14 us
    ppermute x1, starting transfers between devices, on_device(): lax.ppermute(jnp.stack([x[1] for x in near]), ('line', 'core'), beside)  5.63 us
    ppermute x1, starting transfers between devices, on_device(): beside_terms = lax.ppermute(sent, ('line', 'core'), beside)  5.09 us
  transfers between devices with their start and end apart: 10, of which 6 were waited for; matrix products, arithmetic and copies ran while one was open for 1% of the time, Pallas kernels for 13%

profile of v5, /device:TPU:1, one launch (start us, length us, event | category | flops | bytes accessed | tf_op | source)
XLA Modules:
  0.0 116.8 jit_solution(11733347232568201843)
XLA Ops:
  0.6 16.1 %collective-permute-start.1 = (bf16[512,8192]{1,0:T(8,128)(2,1)}, bf16[512,8192]{1,0:T(8,128)(2,1)}, u32[]{:S(2)}, u32[]{:S(2)}) collective-permute-start(bf16[512,8192]{1,0:T(8,128)(2,1)} %w_own_ref.5), channel_id=1, source_target_pairs={{0,1},{1,0},{2,3},{3,2},{4,5},{5,4},{6,7},{7,6},{8,9},{9,8},{10,11... | collective-permute-start | bytes 25165832 | tf_op jit(solution)/shard_map/ppermute | solution.py:252
  16.7 1.9 %collective-permute-start = (bf16[144,512]{1,0:T(8,128)(2,1)}, bf16[144,512]{1,0:T(8,128)(2,1)S(1)}, u32[]{:S(2)}, u32[]{:S(2)}) collective-permute-start(bf16[144,512]{1,0:T(8,128)(2,1)} %refs_4_.1), channel_id=1, source_target_pairs={{0,1},{1,0},{2,3},{3,2},{4,5},{5,4},{6,7},{7,6},{8,9},{9,8},{10,11... | collective-permute-start | bytes 442376 | tf_op jit(solution)/shard_map/ppermute | solution.py:253
  18.6 1.3 %shard_map.77 = bf16[192,512]{1,0:T(8,128)(2,1)S(1)} custom-call(s32[1,192]{1,0:T(1,128)} %offsets_ref.3, bf16[384,512]{1,0:T(8,128)(2,1)} %grad_ref.1), custom_call_target="tpu_custom_call" | custom-call | tf_op jit(solution)/shard_map/pallas_call | solution.py:187
  20.7 9.3 %all-to-all-start = ((bf16[64,4,384]{2,1,0:T(4,128)(2,1)}), bf16[64,4,384]{2,1,0:T(4,128)(2,1)S(1)}, u32[]{:S(2)}, u32[]{:S(2)}) async-start(bf16[64,4,384]{2,1,0:T(4,128)(2,1)} %reshape.20), calls=%async_computation | async-start | bytes 393216 | tf_op jit(solution)/shard_map/all_to_all | solution.py:250
  30.1 0.9 copy-done
  31.0 3.1 %shard_map.78 = (bf16[4,144,512]{2,1,0:T(8,128)(2,1)S(1)}, bf16[144,1024]{1,0:T(8,128)(2,1)S(1)}) custom-call(s32[4]{0:T(128)S(1)} %fusion.2.at_ref, bf16[144,512]{1,0:T(8,128)(2,1)S(1)} %copy-done, bf16[144,512]{1,0:T(8,128)(2,1)S(1)} %collective-permute-done.other_ref, bf16[512,8192]{1,0:T(8,128)(2,1)} %w_own_ref.5, ...), custom_call_target="tpu_custom_call" | custom-call | flops 603979776 | bytes 4194304 | tf_op jit(solution)/shard_map/pallas_call | solution.py:199
  34.2 5.1 %collective-permute-start.2 = (bf16[4,144,512]{2,1,0:T(8,128)(2,1)S(1)}, bf16[4,144,512]{2,1,0:T(8,128)(2,1)S(1)}, u32[]{:S(2)}, u32[]{:S(2)}) collective-permute-start(bf16[4,144,512]{2,1,0:T(8,128)(2,1)S(1)} %get-tuple-element.15), channel_id=1, source_target_pairs={{0,2},{1,15},{2,0},{3,5},{4,6},{5,3},{6,4},{7,9},{8,10},{9,7},{10,... | collective-permute-start | bytes 1769480 | tf_op jit(solution)/shard_map/ppermute | solution.py:268
  39.3 3.1 %shard_map.79.kept_ref = bf16[4,144,512]{2,1,0:T(8,128)(2,1)S(1)} custom-call(s32[4]{0:T(128)S(1)} %fusion.5.at_ref, bf16[144,1024]{1,0:T(8,128)(2,1)S(1)} %get-tuple-element.17.act_ref, bf16[512,8192]{1,0:T(8,128)(2,1)} %w_own_ref.5, bf16[512,8192]{1,0:T(8,128)(2,1)} %collective-permute-done.1.w_other_ref.refs_6_), custom_call_target="tpu_custom_call" | custom-call | flops 603979776 | bytes 4194304 | tf_op jit(solution)/shard_map/pallas_call | solution.py:199
  42.4 4.3 %all-to-all-done = bf16[64,4,384]{2,1,0:T(4,128)(2,1)S(1)} async-done(((bf16[64,4,384]{2,1,0:T(4,128)(2,1)}), bf16[64,4,384]{2,1,0:T(4,128)(2,1)S(1)}, u32[]{:S(2)}, u32[]{:S(2)}) %all-to-all-start) | async-done | bytes 196640 | tf_op jit(solution)/shard_map/all_to_all | solution.py:250
  46.9 1.2 %shard_map.80 = (f32[144,512]{1,0:T(8,128)S(1)}, f32[144,512]{1,0:T(8,128)S(1)}, bf16[2,144,512]{2,1,0:T(8,128)(2,1)S(1)}, bf16[2,144,512]{2,1,0:T(8,128)(2,1)}) custom-call(s32[1,144]{1,0:T(1,128)S(1)} %bitcast.1, bf16[192,512]{1,0:T(8,128)(2,1)S(1)} %reshape.21.arrived_ref, bf16[4,144,512]{2,1,0:T(8,128)(2,1)S(1)} %shard_map.79.kept_ref, ...), custom_call_target="tpu_custom_call" | custom-call | tf_op jit(solution)/shard_map/pallas_call | solution.py:187
  48.9 5.8 %collective-permute-start.4 = (bf16[2,144,512]{2,1,0:T(8,128)(2,1)S(1)}, bf16[2,144,512]{2,1,0:T(8,128)(2,1)S(1)}, u32[]{:S(2)}, u32[]{:S(2)}) collective-permute-start(bf16[2,144,512]{2,1,0:T(8,128)(2,1)S(1)} %get-tuple-element.22.refs_0_), channel_id=1, source_target_pairs={{0,4},{1,13},{2,6},{3,15},{4,8},{5,1},{6,10},{7,3},{8,12},{9,5},{1... | collective-permute-start | bytes 884744 | tf_op jit(solution)/shard_map/ppermute | solution.py:244
  54.7 1.9 %collective-permute-start.3 = (bf16[2,144,512]{2,1,0:T(8,128)(2,1)}, bf16[2,144,512]{2,1,0:T(8,128)(2,1)S(1)}, u32[]{:S(2)}, u32[]{:S(2)}) collective-permute-start(bf16[2,144,512]{2,1,0:T(8,128)(2,1)} %get-tuple-element.20), channel_id=1, source_target_pairs={{0,12},{1,5},{2,14},{3,7},{4,0},{5,9},{6,2},{7,11},{8,4},{9,13},{1... | collective-permute-start | bytes 884744 | tf_op jit(solution)/shard_map/ppermute | solution.py:244
  56.6 6.3 %collective-permute-done.4.arrived_ref.refs_3_ = bf16[2,144,512]{2,1,0:T(8,128)(2,1)S(1)} collective-permute-done((bf16[2,144,512]{2,1,0:T(8,128)(2,1)S(1)}, bf16[2,144,512]{2,1,0:T(8,128)(2,1)S(1)}, u32[]{:S(2)}, u32[]{:S(2)}) %collective-permute-start.4) | collective-permute-done | bytes 294944 | tf_op jit(solution)/shard_map/ppermute | solution.py:244
  63.0 6.4 %collective-permute-start.5 = (bf16[2,144,512]{2,1,0:T(8,128)(2,1)S(1)}, bf16[2,144,512]{2,1,0:T(8,128)(2,1)S(1)}, u32[]{:S(2)}, u32[]{:S(2)}) collective-permute-start(bf16[2,144,512]{2,1,0:T(8,128)(2,1)S(1)} %shard_map.81), channel_id=1, source_target_pairs={{0,4},{1,13},{2,6},{3,15},{4,8},{5,1},{6,10},{7,3},{8,12},{9,5},{1... | collective-permute-start | bytes 884744 | tf_op jit(solution)/shard_map/ppermute | solution.py:244
  69.4 6.1 %collective-permute-done.5.last_ref.refs_2_ = bf16[2,144,512]{2,1,0:T(8,128)(2,1)S(1)} collective-permute-done((bf16[2,144,512]{2,1,0:T(8,128)(2,1)S(1)}, bf16[2,144,512]{2,1,0:T(8,128)(2,1)S(1)}, u32[]{:S(2)}, u32[]{:S(2)}) %collective-permute-start.5) | collective-permute-done | bytes 294944 | tf_op jit(solution)/shard_map/ppermute | solution.py:244
  75.6 1.0 copy-done.4
  77.7 12.2 %all-to-all-start.1 = ((bf16[64,4,384]{2,1,0:T(4,128)(2,1)}), bf16[64,4,384]{2,1,0:T(4,128)(2,1)S(1)}, u32[]{:S(2)}, u32[]{:S(2)}) async-start(bf16[64,4,384]{2,1,0:T(4,128)(2,1)} %reshape.22), calls=%async_computation.1 | async-start | bytes 393216 | tf_op jit(solution)/shard_map/all_to_all | solution.py:250
  90.0 5.6 %collective-permute-start.6 = (bf16[4,144,512]{2,1,0:T(8,128)(2,1)S(1)}, bf16[4,144,512]{2,1,0:T(8,128)(2,1)S(1)}, u32[]{:S(2)}, u32[]{:S(2)}) collective-permute-start(bf16[4,144,512]{2,1,0:T(8,128)(2,1)S(1)} %pad_maximum_fusion), channel_id=1, source_target_pairs={{0,2},{1,15},{2,0},{3,5},{4,6},{5,3},{6,4},{7,9},{8,10},{9,7},{10,... | collective-permute-start | bytes 1769480 | tf_op jit(solution)/shard_map/ppermute | solution.py:295
  95.7 3.7 %shard_map.84 = (f32[144,512]{1,0:T(8,128)S(1)}, f32[144,512]{1,0:T(8,128)S(1)}, f32[144,512]{1,0:T(8,128)S(1)}) custom-call(s32[4]{0:T(128)S(1)} %fusion.5.at_ref, bf16[2,144,512]{2,1,0:T(8,128)(2,1)S(1)} %get-tuple-element.22.refs_0_, bf16[2,144,512]{2,1,0:T(8,128)(2,1)S(1)} %collective-permute-done.3.back_ref.refs_1_, ...), custom_call_target="tpu_custom_call" | custom-call | flops 603979 | bytes 4194 | tf_op jit(solution)/shard_map/pallas_call | solution.py:199
  99.4 3.8 %collective-permute-done.6.grad_ref = bf16[4,144,512]{2,1,0:T(8,128)(2,1)S(1)} collective-permute-done((bf16[4,144,512]{2,1,0:T(8,128)(2,1)S(1)}, bf16[4,144,512]{2,1,0:T(8,128)(2,1)S(1)}, u32[]{:S(2)}, u32[]{:S(2)}) %collective-permute-start.6) | collective-permute-done | bytes 589856 | tf_op jit(solution)/shard_map/ppermute | solution.py:295
  103.2 3.4 %shard_map.85 = (f32[144,512]{1,0:T(8,128)S(1)}, bf16[144,512]{1,0:T(8,128)(2,1)S(1)}) custom-call(s32[4]{0:T(128)S(1)} %fusion.2.at_ref, bf16[4,144,512]{2,1,0:T(8,128)(2,1)S(1)} %collective-permute-done.6.grad_ref, f32[144,512]{1,0:T(8,128)S(1)} %get-tuple-element.23.own_in, f32[144,512]{1,0:T(8,128)S(1)} %get-tuple-element.24.other_in, ...), custom_call_target="tpu_custom_call" | custom-call | flops 603979 | bytes 4194 | tf_op jit(solution)/shard_map/pallas_call | solution.py:199
  106.6 7.1 %collective-permute-start.7 = (bf16[144,512]{1,0:T(8,128)(2,1)S(1)}, bf16[144,512]{1,0:T(8,128)(2,1)S(1)}, u32[]{:S(2)}, u32[]{:S(2)}) collective-permute-start(bf16[144,512]{1,0:T(8,128)(2,1)S(1)} %get-tuple-element.26), channel_id=1, source_target_pairs={{0,1},{1,0},{2,3},{3,2},{4,5},{5,4},{6,7},{7,6},{8,9},{9,8},{10,11... | collective-permute-start | bytes 442376 | tf_op jit(solution)/shard_map/ppermute | solution.py:315
  113.8 1.0 collective-permute-done.7.other_ref
  115.6 1.2 %shard_map.83 = bf16[384,512]{1,0:T(8,128)(2,1)} custom-call(s32[1,192]{1,0:T(1,128)S(1)} %copy-done.6, bf16[192,512]{1,0:T(8,128)(2,1)S(1)} %reshape.23.arrived_ref, bf16[384,512]{1,0:T(8,128)(2,1)S(1)} %copy-done.2), custom_call_target="tpu_custom_call" | custom-call | tf_op jit(solution)/shard_map/pallas_call | solution.py:187
  (31 shorter events, 3.9 us)
Async XLA Ops:
  0.6 29.5 %collective-permute-start.1 = (bf16[512,8192]{1,0:T(8,128)(2,1)}, bf16[512,8192]{1,0:T(8,128)(2,1)}, u32[]{:S(2)}, u32[]{:S(2)}) collective-permute-start(bf16[512,8192]{1,0:T(8,128)(2,1)} %w_own_ref.5), channel_id=1, source_target_pairs={{0,1},{1,0},{2,3},{3,2},{4,5},{5,4},{6,7},{7,6},{8,9},{9,8},{10,11... | collective-permute-start | bytes 25165832 | tf_op jit(solution)/shard_map/ppermute | solution.py:252
  16.7 13.4 %collective-permute-start = (bf16[144,512]{1,0:T(8,128)(2,1)}, bf16[144,512]{1,0:T(8,128)(2,1)S(1)}, u32[]{:S(2)}, u32[]{:S(2)}) collective-permute-start(bf16[144,512]{1,0:T(8,128)(2,1)} %refs_4_.1), channel_id=1, source_target_pairs={{0,1},{1,0},{2,3},{3,2},{4,5},{5,4},{6,7},{7,6},{8,9},{9,8},{10,11... | collective-permute-start | bytes 442376 | tf_op jit(solution)/shard_map/ppermute | solution.py:253
  20.7 26.0 %all-to-all-start = ((bf16[64,4,384]{2,1,0:T(4,128)(2,1)}), bf16[64,4,384]{2,1,0:T(4,128)(2,1)S(1)}, u32[]{:S(2)}, u32[]{:S(2)}) async-start(bf16[64,4,384]{2,1,0:T(4,128)(2,1)} %reshape.20), calls=%async_computation | async-start | bytes 393216 | tf_op jit(solution)/shard_map/all_to_all | solution.py:250
  30.1 0.9 copy-start
  34.2 12.6 %collective-permute-start.2 = (bf16[4,144,512]{2,1,0:T(8,128)(2,1)S(1)}, bf16[4,144,512]{2,1,0:T(8,128)(2,1)S(1)}, u32[]{:S(2)}, u32[]{:S(2)}) collective-permute-start(bf16[4,144,512]{2,1,0:T(8,128)(2,1)S(1)} %get-tuple-element.15), channel_id=1, source_target_pairs={{0,2},{1,15},{2,0},{3,5},{4,6},{5,3},{6,4},{7,9},{8,10},{9,7},{10,... | collective-permute-start | bytes 1769480 | tf_op jit(solution)/shard_map/ppermute | solution.py:268
  39.3 7.7 %copy-start.5 = (s32[144,1]{0,1:T(1,128)S(1)}, s32[144,1]{0,1:T(1,128)}, u32[]{:S(2)}) copy-start(s32[144,1]{0,1:T(1,128)} %param.9) | copy-start | bytes 1732
  39.3 56.4 %copy-start.1 = (bf16[144,512]{1,0:T(8,128)(2,1)S(1)}, bf16[144,512]{1,0:T(8,128)(2,1)}, u32[]{:S(2)}) copy-start(bf16[144,512]{1,0:T(8,128)(2,1)} %refs_4_.1) | copy-start | bytes 442372
  48.2 0.7 copy-start.3
  48.9 14.1 %collective-permute-start.4 = (bf16[2,144,512]{2,1,0:T(8,128)(2,1)S(1)}, bf16[2,144,512]{2,1,0:T(8,128)(2,1)S(1)}, u32[]{:S(2)}, u32[]{:S(2)}) collective-permute-start(bf16[2,144,512]{2,1,0:T(8,128)(2,1)S(1)} %get-tuple-element.22.refs_0_), channel_id=1, source_target_pairs={{0,4},{1,13},{2,6},{3,15},{4,8},{5,1},{6,10},{7,3},{8,12},{9,5},{1... | collective-permute-start | bytes 884744 | tf_op jit(solution)/shard_map/ppermute | solution.py:244
  54.7 14.7 %collective-permute-start.3 = (bf16[2,144,512]{2,1,0:T(8,128)(2,1)}, bf16[2,144,512]{2,1,0:T(8,128)(2,1)S(1)}, u32[]{:S(2)}, u32[]{:S(2)}) collective-permute-start(bf16[2,144,512]{2,1,0:T(8,128)(2,1)} %get-tuple-element.20), channel_id=1, source_target_pairs={{0,12},{1,5},{2,14},{3,7},{4,0},{5,9},{6,2},{7,11},{8,4},{9,13},{1... | collective-permute-start | bytes 884744 | tf_op jit(solution)/shard_map/ppermute | solution.py:244
  63.0 12.6 %collective-permute-start.5 = (bf16[2,144,512]{2,1,0:T(8,128)(2,1)S(1)}, bf16[2,144,512]{2,1,0:T(8,128)(2,1)S(1)}, u32[]{:S(2)}, u32[]{:S(2)}) collective-permute-start(bf16[2,144,512]{2,1,0:T(8,128)(2,1)S(1)} %shard_map.81), channel_id=1, source_target_pairs={{0,4},{1,13},{2,6},{3,15},{4,8},{5,1},{6,10},{7,3},{8,12},{9,5},{1... | collective-permute-start | bytes 884744 | tf_op jit(solution)/shard_map/ppermute | solution.py:244
  75.6 1.0 copy-start.4
  77.7 37.8 %all-to-all-start.1 = ((bf16[64,4,384]{2,1,0:T(4,128)(2,1)}), bf16[64,4,384]{2,1,0:T(4,128)(2,1)S(1)}, u32[]{:S(2)}, u32[]{:S(2)}) async-start(bf16[64,4,384]{2,1,0:T(4,128)(2,1)} %reshape.22), calls=%async_computation.1 | async-start | bytes 393216 | tf_op jit(solution)/shard_map/all_to_all | solution.py:250
  90.0 13.2 %collective-permute-start.6 = (bf16[4,144,512]{2,1,0:T(8,128)(2,1)S(1)}, bf16[4,144,512]{2,1,0:T(8,128)(2,1)S(1)}, u32[]{:S(2)}, u32[]{:S(2)}) collective-permute-start(bf16[4,144,512]{2,1,0:T(8,128)(2,1)S(1)} %pad_maximum_fusion), channel_id=1, source_target_pairs={{0,2},{1,15},{2,0},{3,5},{4,6},{5,3},{6,4},{7,9},{8,10},{9,7},{10,... | collective-permute-start | bytes 1769480 | tf_op jit(solution)/shard_map/ppermute | solution.py:295
  103.2 12.4 %copy-start.2 = (bf16[384,512]{1,0:T(8,128)(2,1)S(1)}, bf16[384,512]{1,0:T(8,128)(2,1)}, u32[]{:S(2)}) copy-start(bf16[384,512]{1,0:T(8,128)(2,1)} %text_ref.1) | copy-start | bytes 1179652
  103.2 12.4 %copy-start.6 = (s32[1,192]{1,0:T(1,128)S(1)}, s32[1,192]{1,0:T(1,128)}, u32[]{:S(2)}) copy-start(s32[1,192]{1,0:T(1,128)} %offsets_ref.3) | copy-start | bytes 2308
  106.6 8.1 %collective-permute-start.7 = (bf16[144,512]{1,0:T(8,128)(2,1)S(1)}, bf16[144,512]{1,0:T(8,128)(2,1)S(1)}, u32[]{:S(2)}, u32[]{:S(2)}) collective-permute-start(bf16[144,512]{1,0:T(8,128)(2,1)S(1)} %get-tuple-element.26), channel_id=1, source_target_pairs={{0,1},{1,0},{2,3},{3,2},{4,5},{5,4},{6,7},{7,6},{8,9},{9,8},{10,11... | collective-permute-start | bytes 442376 | tf_op jit(solution)/shard_map/ppermute | solution.py:315

commit v6 on v3

--- a/solution.py
+++ b/solution.py
@@ -125,15 +125,15 @@
         out_ref[j] = total.astype(BF16)
 
 
-def add_kernel(kept_ref, beside_ref, total_ref, *term_refs):
+def add_kernel(kept_ref, beside_ref, token_ref, total_ref, *term_refs):
+    token_ref[...] = jnp.zeros_like(token_ref)
     total_ref[...] = kept_ref[0].astype(F32) + beside_ref[0].astype(F32)
     for j, term_ref in enumerate(term_refs, 1):
         total = kept_ref[j].astype(F32) + beside_ref[j].astype(F32)
         term_ref[...] = total.astype(term_ref.dtype)
 
 
-def relay_kernel(held_ref, arrived_ref, total_ref, back_ref, out_ref, sum_ref, token_ref):
-    token_ref[...] = jnp.zeros_like(token_ref)
+def relay_kernel(held_ref, arrived_ref, total_ref, back_ref, out_ref, sum_ref):
     out_ref[...] = (held_ref[...] + arrived_ref[...].astype(F32)).astype(BF16)
     sum_ref[...] = total_ref[...] + back_ref[...].astype(F32)
 
@@ -271,17 +271,17 @@
     )
     beside_terms = lax.ppermute(sent, ("line", "core"), beside)
     kept = product(forward_second_kernel, [terms_out], same, (act,), weights, half)
-    total, first, second, third = call(
+    token, total, first, second, third = call(
         add_kernel,
-        [((rows, width), F32)] * 2 + [((rows, width), BF16)] * 2,
+        [((8, 128), F32)] + [((rows, width), F32)] * 2 + [((rows, width), BF16)] * 2,
         kept,
         beside_terms,
     )
     passed = relay(second, 2)
     back = relay(third, -2)
-    first, total, token = call(
+    first, total = call(
         relay_kernel,
-        [((rows, width), BF16), ((rows, width), F32), ((8, 128), F32)],
+        [((rows, width), BF16), ((rows, width), F32)],
         first,
         passed,
         total,

time: 116 us -> 114 us (0.983)
  waiting for transfers between devices: 18 us -> 13.3 us
  starting transfers between devices: 76.2 us -> 78.7 us
    ppermute x6, waiting for transfers between devices: 7.2 us -> 1.43 us  [relay(): return lax.ppermute(x, ('line', 'core'), pairs)]
    ppermute x1, starting transfers between devices: 4.37 us -> 6.01 us  [on_device(): other = lax.ppermute(other, 'core', cores)]
where the time goes in v6:
time: 114 us; the launch traced here: 113 us
  starting transfers between devices  78.7 us (69%)
  Pallas kernels  17.6 us (15%)
  waiting for transfers between devices  13.3 us (12%)
  local copies, waits for them, and re-layouts  2.76 us (2%)
    all_to_all x2, starting transfers between devices, exchange(): x = lax.all_to_all(x, 'group', split_axis=0, concat_axis=0, tiled=True)  24.1 us
    ppermute x6, starting transfers between devices, relay(): return lax.ppermute(x, ('line', 'core'), pairs)  23.5 us
    ppermute x1, starting transfers between devices, on_device(): w_other = lax.ppermute(proj_weight, 'core', cores)  16.1 us
    pallas_call x4, Pallas kernels, product(): pl.pallas_call(kernel, in_specs=[SMEM] + [VMEM] * len(args) + [HBM] * 2,...  13.4 us
    ppermute x1, waiting for transfers between devices, on_device(): far = lax.ppermute(jnp.stack(near), ('line', 'core'), beside)  6.47 us
    ppermute x1, starting transfers between devices, on_device(): other = lax.ppermute(other, 'core', cores)  6.01 us
    ppermute x1, starting transfers between devices, on_device(): beside_terms = lax.ppermute(sent, ('line', 'core'), beside)  5.1 us
    ppermute x1, waiting for transfers between devices, on_device(): beside_terms = lax.ppermute(sent, ('line', 'core'), beside)  4.37 us
  transfers between devices with their start and end apart: 13, of which 4 were waited for; matrix products, arithmetic and copies ran while one was open for 2% of the time, Pallas kernels for 14%

profile of v6, /device:TPU:1, one launch (start us, length us, event | category | flops | bytes accessed | tf_op | source)
XLA Modules:
  0.0 113.3 jit_solution(13184496653030020360)
XLA Ops:
  0.6 16.1 %collective-permute-start.1 = (bf16[512,8192]{1,0:T(8,128)(2,1)}, bf16[512,8192]{1,0:T(8,128)(2,1)}, u32[]{:S(2)}, u32[]{:S(2)}) collective-permute-start(bf16[512,8192]{1,0:T(8,128)(2,1)} %w_own_ref.5), channel_id=1, source_target_pairs={{0,1},{1,0},{2,3},{3,2},{4,5},{5,4},{6,7},{7,6},{8,9},{9,8},{10,11... | collective-permute-start | bytes 25165832 | tf_op jit(solution)/shard_map/ppermute | solution.py:256
  16.7 1.9 %collective-permute-start = (bf16[144,512]{1,0:T(8,128)(2,1)}, bf16[144,512]{1,0:T(8,128)(2,1)S(1)}, u32[]{:S(2)}, u32[]{:S(2)}) collective-permute-start(bf16[144,512]{1,0:T(8,128)(2,1)} %refs_4_.1), channel_id=1, source_target_pairs={{0,1},{1,0},{2,3},{3,2},{4,5},{5,4},{6,7},{7,6},{8,9},{9,8},{10,11... | collective-permute-start | bytes 442376 | tf_op jit(solution)/shard_map/ppermute | solution.py:257
  18.6 1.3 %shard_map.83 = bf16[192,512]{1,0:T(8,128)(2,1)S(1)} custom-call(s32[1,192]{1,0:T(1,128)} %offsets_ref.3, bf16[384,512]{1,0:T(8,128)(2,1)} %grad_ref.1), custom_call_target="tpu_custom_call" | custom-call | tf_op jit(solution)/shard_map/pallas_call | solution.py:190
  20.7 9.3 %all-to-all-start.1 = ((bf16[64,4,384]{2,1,0:T(4,128)(2,1)}), bf16[64,4,384]{2,1,0:T(4,128)(2,1)S(1)}, u32[]{:S(2)}, u32[]{:S(2)}) async-start(bf16[64,4,384]{2,1,0:T(4,128)(2,1)} %reshape.22), calls=%async_computation.1 | async-start | bytes 393216 | tf_op jit(solution)/shard_map/all_to_all | solution.py:253
  30.1 0.9 copy-done
  31.0 3.1 %shard_map.77 = (bf16[4,144,512]{2,1,0:T(8,128)(2,1)S(1)}, bf16[144,1024]{1,0:T(8,128)(2,1)S(1)}) custom-call(s32[4]{0:T(128)S(1)} %fusion.5.at_ref, bf16[144,512]{1,0:T(8,128)(2,1)S(1)} %copy-done, bf16[144,512]{1,0:T(8,128)(2,1)S(1)} %collective-permute-done.other_ref, bf16[512,8192]{1,0:T(8,128)(2,1)} %w_own_ref.5, ...), custom_call_target="tpu_custom_call" | custom-call | flops 603979776 | bytes 4194304 | tf_op jit(solution)/shard_map/pallas_call | solution.py:202
  34.1 5.1 %collective-permute-start.2 = (bf16[4,144,512]{2,1,0:T(8,128)(2,1)S(1)}, bf16[4,144,512]{2,1,0:T(8,128)(2,1)S(1)}, u32[]{:S(2)}, u32[]{:S(2)}) collective-permute-start(bf16[4,144,512]{2,1,0:T(8,128)(2,1)S(1)} %get-tuple-element.17), channel_id=1, source_target_pairs={{0,2},{1,15},{2,0},{3,5},{4,6},{5,3},{6,4},{7,9},{8,10},{9,7},{10,... | collective-permute-start | bytes 1769480 | tf_op jit(solution)/shard_map/ppermute | solution.py:272
  39.3 3.1 %shard_map.78.kept_ref = bf16[4,144,512]{2,1,0:T(8,128)(2,1)S(1)} custom-call(s32[4]{0:T(128)S(1)} %fusion.2.at_ref, bf16[144,1024]{1,0:T(8,128)(2,1)S(1)} %get-tuple-element.16.act_ref, bf16[512,8192]{1,0:T(8,128)(2,1)} %w_own_ref.5, bf16[512,8192]{1,0:T(8,128)(2,1)} %collective-permute-done.1.w_other_ref.refs_6_), custom_call_target="tpu_custom_call" | custom-call | flops 603979776 | bytes 4194304 | tf_op jit(solution)/shard_map/pallas_call | solution.py:202
  42.4 4.4 %collective-permute-done.2.beside_ref = bf16[4,144,512]{2,1,0:T(8,128)(2,1)S(1)} collective-permute-done((bf16[4,144,512]{2,1,0:T(8,128)(2,1)S(1)}, bf16[4,144,512]{2,1,0:T(8,128)(2,1)S(1)}, u32[]{:S(2)}, u32[]{:S(2)}) %collective-permute-start.2) | collective-permute-done | bytes 589856 | tf_op jit(solution)/shard_map/ppermute | solution.py:272
  47.0 4.1 %collective-permute-start.3 = (bf16[144,512]{1,0:T(8,128)(2,1)S(1)}, bf16[144,512]{1,0:T(8,128)(2,1)S(1)}, u32[]{:S(2)}, u32[]{:S(2)}) collective-permute-start(bf16[144,512]{1,0:T(8,128)(2,1)S(1)} %get-tuple-element.19), channel_id=1, source_target_pairs={{0,4},{1,13},{2,6},{3,15},{4,8},{5,1},{6,10},{7,3},{8,12},{9,5},{1... | collective-permute-start | bytes 442376 | tf_op jit(solution)/shard_map/ppermute | solution.py:247
  51.1 2.0 %collective-permute-start.4 = (bf16[144,512]{1,0:T(8,128)(2,1)S(1)}, bf16[144,512]{1,0:T(8,128)(2,1)S(1)}, u32[]{:S(2)}, u32[]{:S(2)}) collective-permute-start(bf16[144,512]{1,0:T(8,128)(2,1)S(1)} %get-tuple-element.21), channel_id=1, source_target_pairs={{0,12},{1,5},{2,14},{3,7},{4,0},{5,9},{6,2},{7,11},{8,4},{9,13},{1... | collective-permute-start | bytes 442376 | tf_op jit(solution)/shard_map/ppermute | solution.py:247
  53.7 5.3 %collective-permute-start.7 = (bf16[144,512]{1,0:T(8,128)(2,1)S(1)}, bf16[144,512]{1,0:T(8,128)(2,1)S(1)}, u32[]{:S(2)}, u32[]{:S(2)}) collective-permute-start(bf16[144,512]{1,0:T(8,128)(2,1)S(1)} %shard_map.84.refs_0_), channel_id=1, source_target_pairs={{0,4},{1,13},{2,6},{3,15},{4,8},{5,1},{6,10},{7,3},{8,12},{9,5},{1... | collective-permute-start | bytes 442376 | tf_op jit(solution)/shard_map/ppermute | solution.py:247
  59.1 1.4 %collective-permute-done.4.back_ref = bf16[144,512]{1,0:T(8,128)(2,1)S(1)} collective-permute-done((bf16[144,512]{1,0:T(8,128)(2,1)S(1)}, bf16[144,512]{1,0:T(8,128)(2,1)S(1)}, u32[]{:S(2)}, u32[]{:S(2)}) %collective-permute-start.4) | collective-permute-done | bytes 147488 | tf_op jit(solution)/shard_map/ppermute | solution.py:247
  60.6 4.3 %collective-permute-start.5 = (bf16[144,512]{1,0:T(8,128)(2,1)S(1)}, bf16[144,512]{1,0:T(8,128)(2,1)S(1)}, u32[]{:S(2)}, u32[]{:S(2)}) collective-permute-start(bf16[144,512]{1,0:T(8,128)(2,1)S(1)} %get-tuple-element.23), channel_id=1, source_target_pairs={{0,4},{1,13},{2,6},{3,15},{4,8},{5,1},{6,10},{7,3},{8,12},{9,5},{1... | collective-permute-start | bytes 442376 | tf_op jit(solution)/shard_map/ppermute | solution.py:247
  64.8 1.9 %collective-permute-start.6 = (bf16[144,512]{1,0:T(8,128)(2,1)S(1)}, bf16[144,512]{1,0:T(8,128)(2,1)S(1)}, u32[]{:S(2)}, u32[]{:S(2)}) collective-permute-start(bf16[144,512]{1,0:T(8,128)(2,1)S(1)} %shard_map.84.refs_0_), channel_id=1, source_target_pairs={{0,12},{1,5},{2,14},{3,7},{4,0},{5,9},{6,2},{7,11},{8,4},{9,13},{1... | collective-permute-start | bytes 442376 | tf_op jit(solution)/shard_map/ppermute | solution.py:247
  66.8 5.8 %collective-permute-start.8 = (bf16[144,512]{1,0:T(8,128)(2,1)S(1)}, bf16[144,512]{1,0:T(8,128)(2,1)S(1)}, u32[]{:S(2)}, u32[]{:S(2)}) collective-permute-start(bf16[144,512]{1,0:T(8,128)(2,1)S(1)} %collective-permute-done.7.refs_3_), channel_id=1, source_target_pairs={{0,4},{1,13},{2,6},{3,15},{4,8},{5,1},{6,10},{7,3},{8,12},{9,5},{1... | collective-permute-start | bytes 442376 | tf_op jit(solution)/shard_map/ppermute | solution.py:247
  73.7 14.8 %all-to-all-start = ((bf16[64,4,384]{2,1,0:T(4,128)(2,1)}), bf16[64,4,384]{2,1,0:T(4,128)(2,1)S(1)}, u32[]{:S(2)}, u32[]{:S(2)}) async-start(bf16[64,4,384]{2,1,0:T(4,128)(2,1)} %reshape.20), calls=%async_computation | async-start | bytes 393216 | tf_op jit(solution)/shard_map/all_to_all | solution.py:253
  88.7 1.9 %collective-permute-start.9 = (bf16[4,144,512]{2,1,0:T(8,128)(2,1)S(1)}, bf16[4,144,512]{2,1,0:T(8,128)(2,1)S(1)}, u32[]{:S(2)}, u32[]{:S(2)}) collective-permute-start(bf16[4,144,512]{2,1,0:T(8,128)(2,1)S(1)} %pad_maximum_fusion), channel_id=1, source_target_pairs={{0,2},{1,15},{2,0},{3,5},{4,6},{5,3},{6,4},{7,9},{8,10},{9,7},{10,... | collective-permute-start | bytes 1769480 | tf_op jit(solution)/shard_map/ppermute | solution.py:310
  90.6 3.7 %shard_map.85 = (f32[144,512]{1,0:T(8,128)S(1)}, f32[144,512]{1,0:T(8,128)S(1)}, f32[144,512]{1,0:T(8,128)S(1)}) custom-call(s32[4]{0:T(128)S(1)} %fusion.2.at_ref, bf16[144,512]{1,0:T(8,128)(2,1)S(1)} %shard_map.84.refs_0_, bf16[144,512]{1,0:T(8,128)(2,1)S(1)} %collective-permute-done.6.refs_1_, bf16[144,512]{1,0:T(8,128)(2,1)S(1)} %collective-permute-done.8.refs_2_, ...), custom_call_target="tpu_custom_call" | custom-call | flops 603979 | bytes 4194 | tf_op jit(solution)/shard_map/pallas_call | solution.py:202
  94.4 6.5 %collective-permute-done.9.grad_ref = bf16[4,144,512]{2,1,0:T(8,128)(2,1)S(1)} collective-permute-done((bf16[4,144,512]{2,1,0:T(8,128)(2,1)S(1)}, bf16[4,144,512]{2,1,0:T(8,128)(2,1)S(1)}, u32[]{:S(2)}, u32[]{:S(2)}) %collective-permute-start.9) | collective-permute-done | bytes 589856 | tf_op jit(solution)/shard_map/ppermute | solution.py:310
  100.8 3.4 %shard_map.86 = (f32[144,512]{1,0:T(8,128)S(1)}, bf16[144,512]{1,0:T(8,128)(2,1)S(1)}) custom-call(s32[4]{0:T(128)S(1)} %fusion.5.at_ref, bf16[4,144,512]{2,1,0:T(8,128)(2,1)S(1)} %collective-permute-done.9.grad_ref, f32[144,512]{1,0:T(8,128)S(1)} %get-tuple-element.25.own_in, f32[144,512]{1,0:T(8,128)S(1)} %get-tuple-element.26.other_in, ...), custom_call_target="tpu_custom_call" | custom-call | flops 603979 | bytes 4194 | tf_op jit(solution)/shard_map/pallas_call | solution.py:202
  104.3 6.0 %collective-permute-start.10 = (bf16[144,512]{1,0:T(8,128)(2,1)S(1)}, bf16[144,512]{1,0:T(8,128)(2,1)S(1)}, u32[]{:S(2)}, u32[]{:S(2)}) collective-permute-start(bf16[144,512]{1,0:T(8,128)(2,1)S(1)} %get-tuple-element.28), channel_id=1, source_target_pairs={{0,1},{1,0},{2,3},{3,2},{4,5},{5,4},{6,7},{7,6},{8,9},{9,8},{10,11... | collective-permute-start | bytes 442376 | tf_op jit(solution)/shard_map/ppermute | solution.py:330
  110.3 1.0 collective-permute-done.10.other_ref
  112.1 1.2 %shard_map.82 = bf16[384,512]{1,0:T(8,128)(2,1)} custom-call(s32[1,192]{1,0:T(1,128)S(1)} %copy-done.4, bf16[192,512]{1,0:T(8,128)(2,1)S(1)} %reshape.21.arrived_ref, bf16[384,512]{1,0:T(8,128)(2,1)S(1)} %copy-done.2), custom_call_target="tpu_custom_call" | custom-call | tf_op jit(solution)/shard_map/pallas_call | solution.py:190
  (30 shorter events, 3.6 us)
Async XLA Ops:
  0.6 29.5 %collective-permute-start.1 = (bf16[512,8192]{1,0:T(8,128)(2,1)}, bf16[512,8192]{1,0:T(8,128)(2,1)}, u32[]{:S(2)}, u32[]{:S(2)}) collective-permute-start(bf16[512,8192]{1,0:T(8,128)(2,1)} %w_own_ref.5), channel_id=1, source_target_pairs={{0,1},{1,0},{2,3},{3,2},{4,5},{5,4},{6,7},{7,6},{8,9},{9,8},{10,11... | collective-permute-start | bytes 25165832 | tf_op jit(solution)/shard_map/ppermute | solution.py:256
  16.7 13.4 %collective-permute-start = (bf16[144,512]{1,0:T(8,128)(2,1)}, bf16[144,512]{1,0:T(8,128)(2,1)S(1)}, u32[]{:S(2)}, u32[]{:S(2)}) collective-permute-start(bf16[144,512]{1,0:T(8,128)(2,1)} %refs_4_.1), channel_id=1, source_target_pairs={{0,1},{1,0},{2,3},{3,2},{4,5},{5,4},{6,7},{7,6},{8,9},{9,8},{10,11... | collective-permute-start | bytes 442376 | tf_op jit(solution)/shard_map/ppermute | solution.py:257
  20.7 32.4 %all-to-all-start.1 = ((bf16[64,4,384]{2,1,0:T(4,128)(2,1)}), bf16[64,4,384]{2,1,0:T(4,128)(2,1)S(1)}, u32[]{:S(2)}, u32[]{:S(2)}) async-start(bf16[64,4,384]{2,1,0:T(4,128)(2,1)} %reshape.22), calls=%async_computation.1 | async-start | bytes 393216 | tf_op jit(solution)/shard_map/all_to_all | solution.py:253
  30.1 0.9 copy-start
  34.1 12.7 %collective-permute-start.2 = (bf16[4,144,512]{2,1,0:T(8,128)(2,1)S(1)}, bf16[4,144,512]{2,1,0:T(8,128)(2,1)S(1)}, u32[]{:S(2)}, u32[]{:S(2)}) collective-permute-start(bf16[4,144,512]{2,1,0:T(8,128)(2,1)S(1)} %get-tuple-element.17), channel_id=1, source_target_pairs={{0,2},{1,15},{2,0},{3,5},{4,6},{5,3},{6,4},{7,9},{8,10},{9,7},{10,... | collective-permute-start | bytes 1769480 | tf_op jit(solution)/shard_map/ppermute | solution.py:272
  39.3 14.0 %copy-start.3 = (s32[144,1]{0,1:T(1,128)S(1)}, s32[144,1]{0,1:T(1,128)}, u32[]{:S(2)}) copy-start(s32[144,1]{0,1:T(1,128)} %param.9) | copy-start | bytes 1732
  39.3 51.3 %copy-start.1 = (bf16[144,512]{1,0:T(8,128)(2,1)S(1)}, bf16[144,512]{1,0:T(8,128)(2,1)}, u32[]{:S(2)}) copy-start(bf16[144,512]{1,0:T(8,128)(2,1)} %refs_4_.1) | copy-start | bytes 442372
  47.0 12.1 %collective-permute-start.3 = (bf16[144,512]{1,0:T(8,128)(2,1)S(1)}, bf16[144,512]{1,0:T(8,128)(2,1)S(1)}, u32[]{:S(2)}, u32[]{:S(2)}) collective-permute-start(bf16[144,512]{1,0:T(8,128)(2,1)S(1)} %get-tuple-element.19), channel_id=1, source_target_pairs={{0,4},{1,13},{2,6},{3,15},{4,8},{5,1},{6,10},{7,3},{8,12},{9,5},{1... | collective-permute-start | bytes 442376 | tf_op jit(solution)/shard_map/ppermute | solution.py:247
  51.1 9.4 %collective-permute-start.4 = (bf16[144,512]{1,0:T(8,128)(2,1)S(1)}, bf16[144,512]{1,0:T(8,128)(2,1)S(1)}, u32[]{:S(2)}, u32[]{:S(2)}) collective-permute-start(bf16[144,512]{1,0:T(8,128)(2,1)S(1)} %get-tuple-element.21), channel_id=1, source_target_pairs={{0,12},{1,5},{2,14},{3,7},{4,0},{5,9},{6,2},{7,11},{8,4},{9,13},{1... | collective-permute-start | bytes 442376 | tf_op jit(solution)/shard_map/ppermute | solution.py:247
  53.7 13.0 %collective-permute-start.7 = (bf16[144,512]{1,0:T(8,128)(2,1)S(1)}, bf16[144,512]{1,0:T(8,128)(2,1)S(1)}, u32[]{:S(2)}, u32[]{:S(2)}) collective-permute-start(bf16[144,512]{1,0:T(8,128)(2,1)S(1)} %shard_map.84.refs_0_), channel_id=1, source_target_pairs={{0,4},{1,13},{2,6},{3,15},{4,8},{5,1},{6,10},{7,3},{8,12},{9,5},{1... | collective-permute-start | bytes 442376 | tf_op jit(solution)/shard_map/ppermute | solution.py:247
  60.6 12.0 %collective-permute-start.5 = (bf16[144,512]{1,0:T(8,128)(2,1)S(1)}, bf16[144,512]{1,0:T(8,128)(2,1)S(1)}, u32[]{:S(2)}, u32[]{:S(2)}) collective-permute-start(bf16[144,512]{1,0:T(8,128)(2,1)S(1)} %get-tuple-element.23), channel_id=1, source_target_pairs={{0,4},{1,13},{2,6},{3,15},{4,8},{5,1},{6,10},{7,3},{8,12},{9,5},{1... | collective-permute-start | bytes 442376 | tf_op jit(solution)/shard_map/ppermute | solution.py:247
  64.8 23.8 %collective-permute-start.6 = (bf16[144,512]{1,0:T(8,128)(2,1)S(1)}, bf16[144,512]{1,0:T(8,128)(2,1)S(1)}, u32[]{:S(2)}, u32[]{:S(2)}) collective-permute-start(bf16[144,512]{1,0:T(8,128)(2,1)S(1)} %shard_map.84.refs_0_), channel_id=1, source_target_pairs={{0,12},{1,5},{2,14},{3,7},{4,0},{5,9},{6,2},{7,11},{8,4},{9,13},{1... | collective-permute-start | bytes 442376 | tf_op jit(solution)/shard_map/ppermute | solution.py:247
  66.8 21.8 %collective-permute-start.8 = (bf16[144,512]{1,0:T(8,128)(2,1)S(1)}, bf16[144,512]{1,0:T(8,128)(2,1)S(1)}, u32[]{:S(2)}, u32[]{:S(2)}) collective-permute-start(bf16[144,512]{1,0:T(8,128)(2,1)S(1)} %collective-permute-done.7.refs_3_), channel_id=1, source_target_pairs={{0,4},{1,13},{2,6},{3,15},{4,8},{5,1},{6,10},{7,3},{8,12},{9,5},{1... | collective-permute-start | bytes 442376 | tf_op jit(solution)/shard_map/ppermute | solution.py:247
  73.7 38.2 %all-to-all-start = ((bf16[64,4,384]{2,1,0:T(4,128)(2,1)}), bf16[64,4,384]{2,1,0:T(4,128)(2,1)S(1)}, u32[]{:S(2)}, u32[]{:S(2)}) async-start(bf16[64,4,384]{2,1,0:T(4,128)(2,1)} %reshape.20), calls=%async_computation | async-start | bytes 393216 | tf_op jit(solution)/shard_map/all_to_all | solution.py:253
  88.7 12.1 %collective-permute-start.9 = (bf16[4,144,512]{2,1,0:T(8,128)(2,1)S(1)}, bf16[4,144,512]{2,1,0:T(8,128)(2,1)S(1)}, u32[]{:S(2)}, u32[]{:S(2)}) collective-permute-start(bf16[4,144,512]{2,1,0:T(8,128)(2,1)S(1)} %pad_maximum_fusion), channel_id=1, source_target_pairs={{0,2},{1,15},{2,0},{3,5},{4,6},{5,3},{6,4},{7,9},{8,10},{9,7},{10,... | collective-permute-start | bytes 1769480 | tf_op jit(solution)/shard_map/ppermute | solution.py:310
  100.8 11.3 %copy-start.2 = (bf16[384,512]{1,0:T(8,128)(2,1)S(1)}, bf16[384,512]{1,0:T(8,128)(2,1)}, u32[]{:S(2)}) copy-start(bf16[384,512]{1,0:T(8,128)(2,1)} %text_ref.1) | copy-start | bytes 1179652
  100.8 11.3 %copy-start.4 = (s32[1,192]{1,0:T(1,128)S(1)}, s32[1,192]{1,0:T(1,128)}, u32[]{:S(2)}) copy-start(s32[1,192]{1,0:T(1,128)} %offsets_ref.3) | copy-start | bytes 2308
  104.3 7.0 %collective-permute-start.10 = (bf16[144,512]{1,0:T(8,128)(2,1)S(1)}, bf16[144,512]{1,0:T(8,128)(2,1)S(1)}, u32[]{:S(2)}, u32[]{:S(2)}) collective-permute-start(bf16[144,512]{1,0:T(8,128)(2,1)S(1)} %get-tuple-element.28), channel_id=1, source_target_pairs={{0,1},{1,0},{2,3},{3,2},{4,5},{5,4},{6,7},{7,6},{8,9},{9,8},{10,11... | collective-permute-start | bytes 442376 | tf_op jit(solution)/shard_map/ppermute | solution.py:330

commit v7 on v6

--- a/solution.py
+++ b/solution.py
@@ -58,9 +58,9 @@
     out_ref[...] = rows
 
 
-def route_kernel(groups, capacity, dest_ref, total_ref, last_ref, out_ref):
+def route_kernel(groups, capacity, dest_ref, total_ref, back_ref, last_ref, out_ref):
     slots = out_ref.shape[0]
-    total = total_ref[...] + last_ref[...].astype(F32)
+    total = total_ref[...] + back_ref[...].astype(F32) + last_ref[...].astype(F32)
     hit = rows_by_target(dest_ref[...], groups, capacity, slots)
     pick = jnp.where(hit, 1.0, 0.0)
     sent = jnp.dot(pick.astype(BF16), total.astype(BF16), preferred_element_type=F32)
@@ -133,9 +133,8 @@
         term_ref[...] = total.astype(term_ref.dtype)
 
 
-def relay_kernel(held_ref, arrived_ref, total_ref, back_ref, out_ref, sum_ref):
+def relay_kernel(held_ref, arrived_ref, out_ref):
     out_ref[...] = (held_ref[...] + arrived_ref[...].astype(F32)).astype(BF16)
-    sum_ref[...] = total_ref[...] + back_ref[...].astype(F32)
 
 
 def backward_first_kernel(blocks, at_ref, *refs):
@@ -279,20 +278,14 @@
     )
     passed = relay(second, 2)
     back = relay(third, -2)
-    first, total = call(
-        relay_kernel,
-        [((rows, width), BF16), ((rows, width), F32)],
-        first,
-        passed,
-        total,
-        back,
-    )
+    first = call(relay_kernel, [((rows, width), BF16)], first, passed)
     last = relay(first, 2)
     outgoing = call(
         functools.partial(route_kernel, groups, capacity),
         [((slots, width), BF16)],
         dest_row,
         total,
+        back,
         last,
     )
     outgoing = by_group(outgoing)

time: 114 us -> 109 us (0.956)
  starting transfers between devices: 78.7 us -> 75.7 us
  waiting for transfers between devices: 13.3 us -> 11.9 us
    ppermute x1, starting transfers between devices: 6.01 us -> 3.19 us  [on_device(): other = lax.ppermute(other, 'core', cores)]
    ppermute x6, waiting for transfers between devices: 1.43 us -> 0.02 us  [relay(): return lax.ppermute(x, ('line', 'core'), pairs)]
  transfers between devices with their start and end apart: 13 -> 13, of which waited for: 4 -> 3; matrix products, arithmetic and copies ran while one was open for 2% -> 2% of each run, Pallas kernels for 14% -> 15%
where the time goes in v7:
time: 109 us
  starting transfers between devices  75.7 us (69%)
  Pallas kernels  17.6 us (16%)
  waiting for transfers between devices  11.9 us (11%)
  local copies, waits for them, and re-layouts  2.76 us (3%)
    ppermute x6, starting transfers between devices, relay(): return lax.ppermute(x, ('line', 'core'), pairs)  23.9 us
    all_to_all x2, starting transfers between devices, exchange(): x = lax.all_to_all(x, 'group', split_axis=0, concat_axis=0, tiled=True)  23.6 us
    ppermute x1, starting transfers between devices, on_device(): w_other = lax.ppermute(proj_weight, 'core', cores)  16.1 us
    pallas_call x4, Pallas kernels, product(): pl.pallas_call(kernel, in_specs=[SMEM] + [VMEM] * len(args) + [HBM] * 2,...  13.4 us
    ppermute x1, waiting for transfers between devices, on_device(): far = lax.ppermute(jnp.stack(near), ('line', 'core'), beside)  6.46 us
    ppermute x1, starting transfers between devices, on_device(): beside_terms = lax.ppermute(sent, ('line', 'core'), beside)  5.1 us
    ppermute x1, waiting for transfers between devices, on_device(): beside_terms = lax.ppermute(sent, ('line', 'core'), beside)  4.37 us
    pallas_call x7, Pallas kernels, call(): pl.pallas_call(kernel, in_specs=[VMEM] * len(args), out_specs=[VMEM] * le...  4.14 us
  transfers between devices with their start and end apart: 13, of which 3 were waited for; matrix products, arithmetic and copies ran while one was open for 2% of the time, Pallas kernels for 15%

profile of v7, /device:TPU:1, one launch (start us, length us, event | category | flops | bytes accessed | tf_op | source)
XLA Modules:
  0.0 108.9 jit_solution(12448465114526009184)
XLA Ops:
  0.6 16.1 %collective-permute-start.1 = (bf16[512,8192]{1,0:T(8,128)(2,1)}, bf16[512,8192]{1,0:T(8,128)(2,1)}, u32[]{:S(2)}, u32[]{:S(2)}) collective-permute-start(bf16[512,8192]{1,0:T(8,128)(2,1)} %w_own_ref.5), channel_id=1, source_target_pairs={{0,1},{1,0},{2,3},{3,2},{4,5},{5,4},{6,7},{7,6},{8,9},{9,8},{10,11... | collective-permute-start | bytes 25165832 | tf_op jit(solution)/shard_map/ppermute | solution.py:255
  16.7 1.9 %collective-permute-start = (bf16[144,512]{1,0:T(8,128)(2,1)}, bf16[144,512]{1,0:T(8,128)(2,1)S(1)}, u32[]{:S(2)}, u32[]{:S(2)}) collective-permute-start(bf16[144,512]{1,0:T(8,128)(2,1)} %refs_4_.1), channel_id=1, source_target_pairs={{0,1},{1,0},{2,3},{3,2},{4,5},{5,4},{6,7},{7,6},{8,9},{9,8},{10,11... | collective-permute-start | bytes 442376 | tf_op jit(solution)/shard_map/ppermute | solution.py:256
  18.6 1.3 %shard_map.83 = bf16[192,512]{1,0:T(8,128)(2,1)S(1)} custom-call(s32[1,192]{1,0:T(1,128)} %offsets_ref.3, bf16[384,512]{1,0:T(8,128)(2,1)} %grad_ref.1), custom_call_target="tpu_custom_call" | custom-call | tf_op jit(solution)/shard_map/pallas_call | solution.py:189
  19.9 0.8 reshape.22
  20.7 9.3 %all-to-all-start.1 = ((bf16[64,4,384]{2,1,0:T(4,128)(2,1)}), bf16[64,4,384]{2,1,0:T(4,128)(2,1)S(1)}, u32[]{:S(2)}, u32[]{:S(2)}) async-start(bf16[64,4,384]{2,1,0:T(4,128)(2,1)} %reshape.22), calls=%async_computation.1 | async-start | bytes 393216 | tf_op jit(solution)/shard_map/all_to_all | solution.py:252
  30.1 0.9 copy-done
  31.0 3.1 %shard_map.77 = (bf16[4,144,512]{2,1,0:T(8,128)(2,1)S(1)}, bf16[144,1024]{1,0:T(8,128)(2,1)S(1)}) custom-call(s32[4]{0:T(128)S(1)} %fusion.5.at_ref, bf16[144,512]{1,0:T(8,128)(2,1)S(1)} %copy-done, bf16[144,512]{1,0:T(8,128)(2,1)S(1)} %collective-permute-done.other_ref, bf16[512,8192]{1,0:T(8,128)(2,1)} %w_own_ref.5, ...), custom_call_target="tpu_custom_call" | custom-call | flops 603979776 | bytes 4194304 | tf_op jit(solution)/shard_map/pallas_call | solution.py:201
  34.1 5.1 %collective-permute-start.2 = (bf16[4,144,512]{2,1,0:T(8,128)(2,1)S(1)}, bf16[4,144,512]{2,1,0:T(8,128)(2,1)S(1)}, u32[]{:S(2)}, u32[]{:S(2)}) collective-permute-start(bf16[4,144,512]{2,1,0:T(8,128)(2,1)S(1)} %get-tuple-element.15), channel_id=1, source_target_pairs={{0,2},{1,15},{2,0},{3,5},{4,6},{5,3},{6,4},{7,9},{8,10},{9,7},{10,... | collective-permute-start | bytes 1769480 | tf_op jit(solution)/shard_map/ppermute | solution.py:271
  39.3 3.1 %shard_map.78.kept_ref = bf16[4,144,512]{2,1,0:T(8,128)(2,1)S(1)} custom-call(s32[4]{0:T(128)S(1)} %fusion.2.at_ref, bf16[144,1024]{1,0:T(8,128)(2,1)S(1)} %get-tuple-element.14.act_ref, bf16[512,8192]{1,0:T(8,128)(2,1)} %w_own_ref.5, bf16[512,8192]{1,0:T(8,128)(2,1)} %collective-permute-done.1.w_other_ref.refs_6_), custom_call_target="tpu_custom_call" | custom-call | flops 603979776 | bytes 4194304 | tf_op jit(solution)/shard_map/pallas_call | solution.py:201
  42.4 4.4 %collective-permute-done.2.beside_ref = bf16[4,144,512]{2,1,0:T(8,128)(2,1)S(1)} collective-permute-done((bf16[4,144,512]{2,1,0:T(8,128)(2,1)S(1)}, bf16[4,144,512]{2,1,0:T(8,128)(2,1)S(1)}, u32[]{:S(2)}, u32[]{:S(2)}) %collective-permute-start.2) | collective-permute-done | bytes 589856 | tf_op jit(solution)/shard_map/ppermute | solution.py:271
  47.0 4.1 %collective-permute-start.4 = (bf16[144,512]{1,0:T(8,128)(2,1)S(1)}, bf16[144,512]{1,0:T(8,128)(2,1)S(1)}, u32[]{:S(2)}, u32[]{:S(2)}) collective-permute-start(bf16[144,512]{1,0:T(8,128)(2,1)S(1)} %get-tuple-element.19), channel_id=1, source_target_pairs={{0,4},{1,13},{2,6},{3,15},{4,8},{5,1},{6,10},{7,3},{8,12},{9,5},{1... | collective-permute-start | bytes 442376 | tf_op jit(solution)/shard_map/ppermute | solution.py:246
  51.7 5.0 %collective-permute-start.7 = (bf16[144,512]{1,0:T(8,128)(2,1)S(1)}, bf16[144,512]{1,0:T(8,128)(2,1)S(1)}, u32[]{:S(2)}, u32[]{:S(2)}) collective-permute-start(bf16[144,512]{1,0:T(8,128)(2,1)S(1)} %shard_map.84.refs_0_), channel_id=1, source_target_pairs={{0,4},{1,13},{2,6},{3,15},{4,8},{5,1},{6,10},{7,3},{8,12},{9,5},{1... | collective-permute-start | bytes 442376 | tf_op jit(solution)/shard_map/ppermute | solution.py:246
  56.6 1.9 %collective-permute-start.3 = (bf16[144,512]{1,0:T(8,128)(2,1)S(1)}, bf16[144,512]{1,0:T(8,128)(2,1)S(1)}, u32[]{:S(2)}, u32[]{:S(2)}) collective-permute-start(bf16[144,512]{1,0:T(8,128)(2,1)S(1)} %get-tuple-element.17), channel_id=1, source_target_pairs={{0,12},{1,5},{2,14},{3,7},{4,0},{5,9},{6,2},{7,11},{8,4},{9,13},{1... | collective-permute-start | bytes 442376 | tf_op jit(solution)/shard_map/ppermute | solution.py:246
  58.6 5.5 %collective-permute-start.5 = (bf16[144,512]{1,0:T(8,128)(2,1)S(1)}, bf16[144,512]{1,0:T(8,128)(2,1)S(1)}, u32[]{:S(2)}, u32[]{:S(2)}) collective-permute-start(bf16[144,512]{1,0:T(8,128)(2,1)S(1)} %shard_map.80), channel_id=1, source_target_pairs={{0,4},{1,13},{2,6},{3,15},{4,8},{5,1},{6,10},{7,3},{8,12},{9,5},{1... | collective-permute-start | bytes 442376 | tf_op jit(solution)/shard_map/ppermute | solution.py:246
  64.1 1.9 %collective-permute-start.6 = (bf16[144,512]{1,0:T(8,128)(2,1)S(1)}, bf16[144,512]{1,0:T(8,128)(2,1)S(1)}, u32[]{:S(2)}, u32[]{:S(2)}) collective-permute-start(bf16[144,512]{1,0:T(8,128)(2,1)S(1)} %shard_map.84.refs_0_), channel_id=1, source_target_pairs={{0,12},{1,5},{2,14},{3,7},{4,0},{5,9},{6,2},{7,11},{8,4},{9,13},{1... | collective-permute-start | bytes 442376 | tf_op jit(solution)/shard_map/ppermute | solution.py:246
  66.0 5.5 %collective-permute-start.8 = (bf16[144,512]{1,0:T(8,128)(2,1)S(1)}, bf16[144,512]{1,0:T(8,128)(2,1)S(1)}, u32[]{:S(2)}, u32[]{:S(2)}) collective-permute-start(bf16[144,512]{1,0:T(8,128)(2,1)S(1)} %collective-permute-done.7.refs_3_), channel_id=1, source_target_pairs={{0,4},{1,13},{2,6},{3,15},{4,8},{5,1},{6,10},{7,3},{8,12},{9,5},{1... | collective-permute-start | bytes 442376 | tf_op jit(solution)/shard_map/ppermute | solution.py:246
  72.7 14.3 %all-to-all-start = ((bf16[64,4,384]{2,1,0:T(4,128)(2,1)}), bf16[64,4,384]{2,1,0:T(4,128)(2,1)S(1)}, u32[]{:S(2)}, u32[]{:S(2)}) async-start(bf16[64,4,384]{2,1,0:T(4,128)(2,1)} %reshape.20), calls=%async_computation | async-start | bytes 393216 | tf_op jit(solution)/shard_map/all_to_all | solution.py:252
  87.1 1.9 %collective-permute-start.9 = (bf16[4,144,512]{2,1,0:T(8,128)(2,1)S(1)}, bf16[4,144,512]{2,1,0:T(8,128)(2,1)S(1)}, u32[]{:S(2)}, u32[]{:S(2)}) collective-permute-start(bf16[4,144,512]{2,1,0:T(8,128)(2,1)S(1)} %pad_maximum_fusion), channel_id=1, source_target_pairs={{0,2},{1,15},{2,0},{3,5},{4,6},{5,3},{6,4},{7,9},{8,10},{9,7},{10,... | collective-permute-start | bytes 1769480 | tf_op jit(solution)/shard_map/ppermute | solution.py:303
  89.0 3.7 %shard_map.85 = (f32[144,512]{1,0:T(8,128)S(1)}, f32[144,512]{1,0:T(8,128)S(1)}, f32[144,512]{1,0:T(8,128)S(1)}) custom-call(s32[4]{0:T(128)S(1)} %fusion.2.at_ref, bf16[144,512]{1,0:T(8,128)(2,1)S(1)} %shard_map.84.refs_0_, bf16[144,512]{1,0:T(8,128)(2,1)S(1)} %collective-permute-done.6.refs_1_, bf16[144,512]{1,0:T(8,128)(2,1)S(1)} %collective-permute-done.8.refs_2_, ...), custom_call_target="tpu_custom_call" | custom-call | flops 603979 | bytes 4194 | tf_op jit(solution)/shard_map/pallas_call | solution.py:201
  92.7 6.5 %collective-permute-done.9.grad_ref = bf16[4,144,512]{2,1,0:T(8,128)(2,1)S(1)} collective-permute-done((bf16[4,144,512]{2,1,0:T(8,128)(2,1)S(1)}, bf16[4,144,512]{2,1,0:T(8,128)(2,1)S(1)}, u32[]{:S(2)}, u32[]{:S(2)}) %collective-permute-start.9) | collective-permute-done | bytes 589856 | tf_op jit(solution)/shard_map/ppermute | solution.py:303
  99.2 3.4 %shard_map.86 = (f32[144,512]{1,0:T(8,128)S(1)}, bf16[144,512]{1,0:T(8,128)(2,1)S(1)}) custom-call(s32[4]{0:T(128)S(1)} %fusion.5.at_ref, bf16[4,144,512]{2,1,0:T(8,128)(2,1)S(1)} %collective-permute-done.9.grad_ref, f32[144,512]{1,0:T(8,128)S(1)} %get-tuple-element.21.own_in, f32[144,512]{1,0:T(8,128)S(1)} %get-tuple-element.22.other_in, ...), custom_call_target="tpu_custom_call" | custom-call | flops 603979 | bytes 4194 | tf_op jit(solution)/shard_map/pallas_call | solution.py:201
  102.7 3.2 %collective-permute-start.10 = (bf16[144,512]{1,0:T(8,128)(2,1)S(1)}, bf16[144,512]{1,0:T(8,128)(2,1)S(1)}, u32[]{:S(2)}, u32[]{:S(2)}) collective-permute-start(bf16[144,512]{1,0:T(8,128)(2,1)S(1)} %get-tuple-element.24), channel_id=1, source_target_pairs={{0,1},{1,0},{2,3},{3,2},{4,5},{5,4},{6,7},{7,6},{8,9},{9,8},{10,11... | collective-permute-start | bytes 442376 | tf_op jit(solution)/shard_map/ppermute | solution.py:323
  105.9 1.0 collective-permute-done.10.other_ref
  107.7 1.2 %shard_map.82 = bf16[384,512]{1,0:T(8,128)(2,1)} custom-call(s32[1,192]{1,0:T(1,128)S(1)} %copy-done.4, bf16[192,512]{1,0:T(8,128)(2,1)S(1)} %reshape.21.arrived_ref, bf16[384,512]{1,0:T(8,128)(2,1)S(1)} %copy-done.2), custom_call_target="tpu_custom_call" | custom-call | tf_op jit(solution)/shard_map/pallas_call | solution.py:189
  (30 shorter events, 2.8 us)
Async XLA Ops:
  0.6 29.5 %collective-permute-start.1 = (bf16[512,8192]{1,0:T(8,128)(2,1)}, bf16[512,8192]{1,0:T(8,128)(2,1)}, u32[]{:S(2)}, u32[]{:S(2)}) collective-permute-start(bf16[512,8192]{1,0:T(8,128)(2,1)} %w_own_ref.5), channel_id=1, source_target_pairs={{0,1},{1,0},{2,3},{3,2},{4,5},{5,4},{6,7},{7,6},{8,9},{9,8},{10,11... | collective-permute-start | bytes 25165832 | tf_op jit(solution)/shard_map/ppermute | solution.py:255
  16.7 13.4 %collective-permute-start = (bf16[144,512]{1,0:T(8,128)(2,1)}, bf16[144,512]{1,0:T(8,128)(2,1)S(1)}, u32[]{:S(2)}, u32[]{:S(2)}) collective-permute-start(bf16[144,512]{1,0:T(8,128)(2,1)} %refs_4_.1), channel_id=1, source_target_pairs={{0,1},{1,0},{2,3},{3,2},{4,5},{5,4},{6,7},{7,6},{8,9},{9,8},{10,11... | collective-permute-start | bytes 442376 | tf_op jit(solution)/shard_map/ppermute | solution.py:256
  20.7 30.4 %all-to-all-start.1 = ((bf16[64,4,384]{2,1,0:T(4,128)(2,1)}), bf16[64,4,384]{2,1,0:T(4,128)(2,1)S(1)}, u32[]{:S(2)}, u32[]{:S(2)}) async-start(bf16[64,4,384]{2,1,0:T(4,128)(2,1)} %reshape.22), calls=%async_computation.1 | async-start | bytes 393216 | tf_op jit(solution)/shard_map/all_to_all | solution.py:252
  30.1 0.9 copy-start
  34.1 12.7 %collective-permute-start.2 = (bf16[4,144,512]{2,1,0:T(8,128)(2,1)S(1)}, bf16[4,144,512]{2,1,0:T(8,128)(2,1)S(1)}, u32[]{:S(2)}, u32[]{:S(2)}) collective-permute-start(bf16[4,144,512]{2,1,0:T(8,128)(2,1)S(1)} %get-tuple-element.15), channel_id=1, source_target_pairs={{0,2},{1,15},{2,0},{3,5},{4,6},{5,3},{6,4},{7,9},{8,10},{9,7},{10,... | collective-permute-start | bytes 1769480 | tf_op jit(solution)/shard_map/ppermute | solution.py:271
  39.3 12.0 %copy-start.3 = (s32[144,1]{0,1:T(1,128)S(1)}, s32[144,1]{0,1:T(1,128)}, u32[]{:S(2)}) copy-start(s32[144,1]{0,1:T(1,128)} %param.9) | copy-start | bytes 1732
  39.3 49.7 %copy-start.1 = (bf16[144,512]{1,0:T(8,128)(2,1)S(1)}, bf16[144,512]{1,0:T(8,128)(2,1)}, u32[]{:S(2)}) copy-start(bf16[144,512]{1,0:T(8,128)(2,1)} %refs_4_.1) | copy-start | bytes 442372
  47.0 11.6 %collective-permute-start.4 = (bf16[144,512]{1,0:T(8,128)(2,1)S(1)}, bf16[144,512]{1,0:T(8,128)(2,1)S(1)}, u32[]{:S(2)}, u32[]{:S(2)}) collective-permute-start(bf16[144,512]{1,0:T(8,128)(2,1)S(1)} %get-tuple-element.19), channel_id=1, source_target_pairs={{0,4},{1,13},{2,6},{3,15},{4,8},{5,1},{6,10},{7,3},{8,12},{9,5},{1... | collective-permute-start | bytes 442376 | tf_op jit(solution)/shard_map/ppermute | solution.py:246
  51.7 14.4 %collective-permute-start.7 = (bf16[144,512]{1,0:T(8,128)(2,1)S(1)}, bf16[144,512]{1,0:T(8,128)(2,1)S(1)}, u32[]{:S(2)}, u32[]{:S(2)}) collective-permute-start(bf16[144,512]{1,0:T(8,128)(2,1)S(1)} %shard_map.84.refs_0_), channel_id=1, source_target_pairs={{0,4},{1,13},{2,6},{3,15},{4,8},{5,1},{6,10},{7,3},{8,12},{9,5},{1... | collective-permute-start | bytes 442376 | tf_op jit(solution)/shard_map/ppermute | solution.py:246
  56.6 14.9 %collective-permute-start.3 = (bf16[144,512]{1,0:T(8,128)(2,1)S(1)}, bf16[144,512]{1,0:T(8,128)(2,1)S(1)}, u32[]{:S(2)}, u32[]{:S(2)}) collective-permute-start(bf16[144,512]{1,0:T(8,128)(2,1)S(1)} %get-tuple-element.17), channel_id=1, source_target_pairs={{0,12},{1,5},{2,14},{3,7},{4,0},{5,9},{6,2},{7,11},{8,4},{9,13},{1... | collective-permute-start | bytes 442376 | tf_op jit(solution)/shard_map/ppermute | solution.py:246
  58.6 12.9 %collective-permute-start.5 = (bf16[144,512]{1,0:T(8,128)(2,1)S(1)}, bf16[144,512]{1,0:T(8,128)(2,1)S(1)}, u32[]{:S(2)}, u32[]{:S(2)}) collective-permute-start(bf16[144,512]{1,0:T(8,128)(2,1)S(1)} %shard_map.80), channel_id=1, source_target_pairs={{0,4},{1,13},{2,6},{3,15},{4,8},{5,1},{6,10},{7,3},{8,12},{9,5},{1... | collective-permute-start | bytes 442376 | tf_op jit(solution)/shard_map/ppermute | solution.py:246
  64.1 22.9 %collective-permute-start.6 = (bf16[144,512]{1,0:T(8,128)(2,1)S(1)}, bf16[144,512]{1,0:T(8,128)(2,1)S(1)}, u32[]{:S(2)}, u32[]{:S(2)}) collective-permute-start(bf16[144,512]{1,0:T(8,128)(2,1)S(1)} %shard_map.84.refs_0_), channel_id=1, source_target_pairs={{0,12},{1,5},{2,14},{3,7},{4,0},{5,9},{6,2},{7,11},{8,4},{9,13},{1... | collective-permute-start | bytes 442376 | tf_op jit(solution)/shard_map/ppermute | solution.py:246
  66.0 20.9 %collective-permute-start.8 = (bf16[144,512]{1,0:T(8,128)(2,1)S(1)}, bf16[144,512]{1,0:T(8,128)(2,1)S(1)}, u32[]{:S(2)}, u32[]{:S(2)}) collective-permute-start(bf16[144,512]{1,0:T(8,128)(2,1)S(1)} %collective-permute-done.7.refs_3_), channel_id=1, source_target_pairs={{0,4},{1,13},{2,6},{3,15},{4,8},{5,1},{6,10},{7,3},{8,12},{9,5},{1... | collective-permute-start | bytes 442376 | tf_op jit(solution)/shard_map/ppermute | solution.py:246
  72.7 34.8 %all-to-all-start = ((bf16[64,4,384]{2,1,0:T(4,128)(2,1)}), bf16[64,4,384]{2,1,0:T(4,128)(2,1)S(1)}, u32[]{:S(2)}, u32[]{:S(2)}) async-start(bf16[64,4,384]{2,1,0:T(4,128)(2,1)} %reshape.20), calls=%async_computation | async-start | bytes 393216 | tf_op jit(solution)/shard_map/all_to_all | solution.py:252
  87.1 12.1 %collective-permute-start.9 = (bf16[4,144,512]{2,1,0:T(8,128)(2,1)S(1)}, bf16[4,144,512]{2,1,0:T(8,128)(2,1)S(1)}, u32[]{:S(2)}, u32[]{:S(2)}) collective-permute-start(bf16[4,144,512]{2,1,0:T(8,128)(2,1)S(1)} %pad_maximum_fusion), channel_id=1, source_target_pairs={{0,2},{1,15},{2,0},{3,5},{4,6},{5,3},{6,4},{7,9},{8,10},{9,7},{10,... | collective-permute-start | bytes 1769480 | tf_op jit(solution)/shard_map/ppermute | solution.py:303
  99.2 8.5 %copy-start.2 = (bf16[384,512]{1,0:T(8,128)(2,1)S(1)}, bf16[384,512]{1,0:T(8,128)(2,1)}, u32[]{:S(2)}) copy-start(bf16[384,512]{1,0:T(8,128)(2,1)} %text_ref.1) | copy-start | bytes 1179652
  99.2 8.5 %copy-start.4 = (s32[1,192]{1,0:T(1,128)S(1)}, s32[1,192]{1,0:T(1,128)}, u32[]{:S(2)}) copy-start(s32[1,192]{1,0:T(1,128)} %offsets_ref.3) | copy-start | bytes 2308
  102.7 4.2 %collective-permute-start.10 = (bf16[144,512]{1,0:T(8,128)(2,1)S(1)}, bf16[144,512]{1,0:T(8,128)(2,1)S(1)}, u32[]{:S(2)}, u32[]{:S(2)}) collective-permute-start(bf16[144,512]{1,0:T(8,128)(2,1)S(1)} %get-tuple-element.24), channel_id=1, source_target_pairs={{0,1},{1,0},{2,3},{3,2},{4,5},{5,4},{6,7},{7,6},{8,9},{9,8},{10,11... | collective-permute-start | bytes 442376 | tf_op jit(solution)/shard_map/ppermute | solution.py:323

commit v8 on v7

--- a/solution.py
+++ b/solution.py
@@ -68,7 +68,8 @@
     out_ref[...] = jnp.where(used > 0.5, sent, EMPTY).astype(BF16)
 
 
-def place_kernel(offsets_ref, arrived_ref, text_ref, out_ref):
+def place_kernel(offsets_ref, arrived_ref, text_ref, out_ref, token_ref):
+    token_ref[...] = jnp.zeros_like(token_ref)
     length, slots = text_ref.shape[0], offsets_ref.shape[1]
     arrived = arrived_ref[...].astype(F32)
     used = arrived[:, 0:1] < LIMIT
@@ -100,12 +101,15 @@
 
 
 def forward_first_kernel(
-    at_ref, own_ref, other_ref, w_own_ref, w_other_ref, out_ref, act_ref, held_ref, sems
+    at_ref, other_ref, w_own_ref, w_other_ref, own_ref, out_ref, act_ref, held_ref, sems
 ):
+    half = other_ref.shape[1]
+    own = pltpu.make_async_copy(own_ref, act_ref.at[:, :half], sems.at[2, 0])
+    own.start()
     copies = fetch(at_ref, (w_own_ref, w_other_ref), held_ref, sems)
-    half = own_ref.shape[1]
-    act_ref[:, :half] = gelu(own_ref[...].astype(F32)).astype(BF16)
     act_ref[:, half:] = gelu(other_ref[...].astype(F32)).astype(BF16)
+    own.wait()
+    act_ref[:, :half] = gelu(act_ref[:, :half].astype(F32)).astype(BF16)
     for j, pair in enumerate(copies):
         for copy in pair:
             copy.wait()
@@ -166,7 +170,7 @@
     other_ref[...] = other.astype(BF16)
 
 
-def slope_kernel(own_ref, other_ref, slope_ref, out_ref):
+def slope_kernel(own_ref, other_ref, slope_ref, token_ref, out_ref):
     total = own_ref[...] + other_ref[...].astype(F32)
     out_ref[...] = (total * slope_ref[...]).astype(BF16)
 
@@ -185,7 +189,10 @@
 
 
 def call(kernel, outs, *args, final=False, first=False):
-    out_shape = [jax.ShapeDtypeStruct(*o) if final else pltpu.VMEM(*o) for o in outs]
+    out_shape = [
+        jax.ShapeDtypeStruct(*o) if final and i == 0 else pltpu.VMEM(*o)
+        for i, o in enumerate(outs)
+    ]
     got = pl.pallas_call(
         kernel,
         in_specs=[VMEM] * len(args),
@@ -195,17 +202,17 @@
     return got if len(outs) > 1 else got[0]
 
 
-def product(kernel, outs, at, args, weights, blocks, share=1):
-    hid, width = weights[0].shape[0], weights[0].shape[1] // (4 * blocks)
+def product(kernel, outs, at, args, sources, blocks, share=1):
+    hid, width = sources[0].shape[0], sources[0].shape[1] // (4 * blocks)
     rows = args[0].shape[-2]
     got = pl.pallas_call(
         kernel,
-        in_specs=[SMEM] + [VMEM] * len(args) + [HBM] * 2,
+        in_specs=[SMEM] + [VMEM] * len(args) + [HBM] * len(sources),
         out_specs=[VMEM] * len(outs),
         out_shape=[pltpu.VMEM(*o) for o in outs],
         scratch_shapes=[
             pltpu.VMEM((2, blocks, hid, width), BF16),
-            pltpu.SemaphoreType.DMA((2, blocks)),
+            pltpu.SemaphoreType.DMA((3, blocks)),
         ],
         cost_estimate=pl.CostEstimate(
             flops=2 * rows * blocks * width * 2 * hid // share,
@@ -213,7 +220,7 @@
             transcendentals=0,
         ),
         compiler_params=pltpu.CompilerParams(vmem_limit_bytes=24 * 1024 * 1024),
-    )(at, *[near_core(a) for a in args], *[in_hbm(w) for w in weights])
+    )(at, *[near_core(a) for a in args], *[in_hbm(x) for x in sources])
     return got if len(outs) > 1 else got[0]
 
 
@@ -264,8 +271,8 @@
         forward_first_kernel,
         [terms_out, ((rows, 2 * hid), BF16)],
         opposite,
-        (pre_hidden, pre_other),
-        weights,
+        (pre_other,),
+        (*weights, pre_hidden),
         half,
     )
     beside_terms = lax.ppermute(sent, ("line", "core"), beside)
@@ -321,11 +328,15 @@
         1000,
     )
     other = lax.ppermute(other, "core", cores)
-    grad_hidden = call(slope_kernel, [((rows, hid), BF16)], own, other, slope, final=True)
-
-    packed = call(
-        place_kernel, [(text_embed.shape, BF16)], place, arrived, text_embed, final=True
-    )
+    packed, token = call(
+        place_kernel,
+        [(text_embed.shape, BF16), ((8, 128), F32)],
+        place,
+        arrived,
+        text_embed,
+        final=True,
+    )
+    grad_hidden = call(slope_kernel, [((rows, hid), BF16)], own, other, slope, token, final=True)
     return (packed, grad_hidden)
 
 

time: 109 us -> 108 us (level)
  waiting for transfers between devices: 11.9 us -> 10.8 us
  transfers between devices with their start and end apart: 13 -> 13, of which waited for: 3 -> 2; matrix products, arithmetic and copies ran while one was open for 2% -> 2% of each run, Pallas kernels for 15% -> 16%
where the time goes in v8:
time: 108 us; the launch traced here: 107 us
  starting transfers between devices  75.5 us (70%)
  Pallas kernels  17.8 us (16%)
  waiting for transfers between devices  10.8 us (10%)
  local copies, waits for them, and re-layouts  1.85 us (2%)
    ppermute x6, starting transfers between devices, relay(): return lax.ppermute(x, ('line', 'core'), pairs)  23.9 us
    all_to_all x2, starting transfers between devices, exchange(): x = lax.all_to_all(x, 'group', split_axis=0, concat_axis=0, tiled=True)  23.6 us
    ppermute x1, starting transfers between devices, on_device(): w_other = lax.ppermute(proj_weight, 'core', cores)  16.1 us
    pallas_call x4, Pallas kernels, product(): pl.pallas_call(kernel, in_specs=[SMEM] + [VMEM] * len(args) + [HBM] * len...  13.6 us
    ppermute x1, waiting for transfers between devices, on_device(): far = lax.ppermute(jnp.stack(near), ('line', 'core'), beside)  6.43 us
    ppermute x1, starting transfers between devices, on_device(): beside_terms = lax.ppermute(sent, ('line', 'core'), beside)  5.1 us
    ppermute x1, waiting for transfers between devices, on_device(): beside_terms = lax.ppermute(sent, ('line', 'core'), beside)  4.33 us
    pallas_call x7, Pallas kernels, call(): pl.pallas_call(kernel, in_specs=[VMEM] * len(args), out_specs=[VMEM] * le...  4.14 us
  transfers between devices with their start and end apart: 13, of which 2 were waited for; matrix products, arithmetic and copies ran while one was open for 2% of the time, Pallas kernels for 16%

profile of v8, /device:TPU:1, one launch (start us, length us, event | category | flops | bytes accessed | tf_op | source)
XLA Modules:
  0.0 107.0 jit_solution(1048742748461418652)
XLA Ops:
  0.6 16.1 %collective-permute-start.1 = (bf16[512,8192]{1,0:T(8,128)(2,1)}, bf16[512,8192]{1,0:T(8,128)(2,1)}, u32[]{:S(2)}, u32[]{:S(2)}) collective-permute-start(bf16[512,8192]{1,0:T(8,128)(2,1)} %w_own_ref.5), channel_id=1, source_target_pairs={{0,1},{1,0},{2,3},{3,2},{4,5},{5,4},{6,7},{7,6},{8,9},{9,8},{10,11... | collective-permute-start | bytes 25165832 | tf_op jit(solution)/shard_map/ppermute | solution.py:262
  16.7 1.9 %collective-permute-start = (bf16[144,512]{1,0:T(8,128)(2,1)}, bf16[144,512]{1,0:T(8,128)(2,1)S(1)}, u32[]{:S(2)}, u32[]{:S(2)}) collective-permute-start(bf16[144,512]{1,0:T(8,128)(2,1)} %refs_4_.1), channel_id=1, source_target_pairs={{0,1},{1,0},{2,3},{3,2},{4,5},{5,4},{6,7},{7,6},{8,9},{9,8},{10,11... | collective-permute-start | bytes 442376 | tf_op jit(solution)/shard_map/ppermute | solution.py:263
  18.6 1.3 %shard_map.83 = bf16[192,512]{1,0:T(8,128)(2,1)S(1)} custom-call(s32[1,192]{1,0:T(1,128)} %offsets_ref.3, bf16[384,512]{1,0:T(8,128)(2,1)} %grad_ref.1), custom_call_target="tpu_custom_call" | custom-call | tf_op jit(solution)/shard_map/pallas_call | solution.py:196
  19.9 0.8 reshape.22
  20.7 9.3 %all-to-all-start.1 = ((bf16[64,4,384]{2,1,0:T(4,128)(2,1)}), bf16[64,4,384]{2,1,0:T(4,128)(2,1)S(1)}, u32[]{:S(2)}, u32[]{:S(2)}) async-start(bf16[64,4,384]{2,1,0:T(4,128)(2,1)} %reshape.22), calls=%async_computation.1 | async-start | bytes 393216 | tf_op jit(solution)/shard_map/all_to_all | solution.py:259
  30.1 3.2 %shard_map.77 = (bf16[4,144,512]{2,1,0:T(8,128)(2,1)S(1)}, bf16[144,1024]{1,0:T(8,128)(2,1)S(1)}) custom-call(s32[4]{0:T(128)S(1)} %fusion.5.at_ref, bf16[144,512]{1,0:T(8,128)(2,1)S(1)} %collective-permute-done.other_ref, bf16[512,8192]{1,0:T(8,128)(2,1)} %w_own_ref.5, bf16[512,8192]{1,0:T(8,128)(2,1)} %collective-permute-done.1.w_other_ref.refs_6_, ...), custom_call_target="tpu_custom_call" | custom-call | flops 603979776 | bytes 4194304 | tf_op jit(solution)/shard_map/pallas_call | solution.py:208
  33.4 5.1 %collective-permute-start.2 = (bf16[4,144,512]{2,1,0:T(8,128)(2,1)S(1)}, bf16[4,144,512]{2,1,0:T(8,128)(2,1)S(1)}, u32[]{:S(2)}, u32[]{:S(2)}) collective-permute-start(bf16[4,144,512]{2,1,0:T(8,128)(2,1)S(1)} %get-tuple-element.17), channel_id=1, source_target_pairs={{0,2},{1,15},{2,0},{3,5},{4,6},{5,3},{6,4},{7,9},{8,10},{9,7},{10,... | collective-permute-start | bytes 1769480 | tf_op jit(solution)/shard_map/ppermute | solution.py:278
  38.5 3.2 %shard_map.78.kept_ref = bf16[4,144,512]{2,1,0:T(8,128)(2,1)S(1)} custom-call(s32[4]{0:T(128)S(1)} %fusion.2.at_ref, bf16[144,1024]{1,0:T(8,128)(2,1)S(1)} %get-tuple-element.16.act_ref, bf16[512,8192]{1,0:T(8,128)(2,1)} %w_own_ref.5, bf16[512,8192]{1,0:T(8,128)(2,1)} %collective-permute-done.1.w_other_ref.refs_6_), custom_call_target="tpu_custom_call" | custom-call | flops 603979776 | bytes 4194304 | tf_op jit(solution)/shard_map/pallas_call | solution.py:208
  41.7 4.3 %collective-permute-done.2.beside_ref = bf16[4,144,512]{2,1,0:T(8,128)(2,1)S(1)} collective-permute-done((bf16[4,144,512]{2,1,0:T(8,128)(2,1)S(1)}, bf16[4,144,512]{2,1,0:T(8,128)(2,1)S(1)}, u32[]{:S(2)}, u32[]{:S(2)}) %collective-permute-start.2) | collective-permute-done | bytes 589856 | tf_op jit(solution)/shard_map/ppermute | solution.py:278
  46.2 4.1 %collective-permute-start.4 = (bf16[144,512]{1,0:T(8,128)(2,1)S(1)}, bf16[144,512]{1,0:T(8,128)(2,1)S(1)}, u32[]{:S(2)}, u32[]{:S(2)}) collective-permute-start(bf16[144,512]{1,0:T(8,128)(2,1)S(1)} %get-tuple-element.21), channel_id=1, source_target_pairs={{0,4},{1,13},{2,6},{3,15},{4,8},{5,1},{6,10},{7,3},{8,12},{9,5},{1... | collective-permute-start | bytes 442376 | tf_op jit(solution)/shard_map/ppermute | solution.py:253
  50.9 5.0 %collective-permute-start.7 = (bf16[144,512]{1,0:T(8,128)(2,1)S(1)}, bf16[144,512]{1,0:T(8,128)(2,1)S(1)}, u32[]{:S(2)}, u32[]{:S(2)}) collective-permute-start(bf16[144,512]{1,0:T(8,128)(2,1)S(1)} %shard_map.84.refs_0_), channel_id=1, source_target_pairs={{0,4},{1,13},{2,6},{3,15},{4,8},{5,1},{6,10},{7,3},{8,12},{9,5},{1... | collective-permute-start | bytes 442376 | tf_op jit(solution)/shard_map/ppermute | solution.py:253
  55.8 1.9 %collective-permute-start.3 = (bf16[144,512]{1,0:T(8,128)(2,1)S(1)}, bf16[144,512]{1,0:T(8,128)(2,1)S(1)}, u32[]{:S(2)}, u32[]{:S(2)}) collective-permute-start(bf16[144,512]{1,0:T(8,128)(2,1)S(1)} %get-tuple-element.19), channel_id=1, source_target_pairs={{0,12},{1,5},{2,14},{3,7},{4,0},{5,9},{6,2},{7,11},{8,4},{9,13},{1... | collective-permute-start | bytes 442376 | tf_op jit(solution)/shard_map/ppermute | solution.py:253
  57.8 5.5 %collective-permute-start.5 = (bf16[144,512]{1,0:T(8,128)(2,1)S(1)}, bf16[144,512]{1,0:T(8,128)(2,1)S(1)}, u32[]{:S(2)}, u32[]{:S(2)}) collective-permute-start(bf16[144,512]{1,0:T(8,128)(2,1)S(1)} %shard_map.80), channel_id=1, source_target_pairs={{0,4},{1,13},{2,6},{3,15},{4,8},{5,1},{6,10},{7,3},{8,12},{9,5},{1... | collective-permute-start | bytes 442376 | tf_op jit(solution)/shard_map/ppermute | solution.py:253
  63.3 1.9 %collective-permute-start.6 = (bf16[144,512]{1,0:T(8,128)(2,1)S(1)}, bf16[144,512]{1,0:T(8,128)(2,1)S(1)}, u32[]{:S(2)}, u32[]{:S(2)}) collective-permute-start(bf16[144,512]{1,0:T(8,128)(2,1)S(1)} %shard_map.84.refs_0_), channel_id=1, source_target_pairs={{0,12},{1,5},{2,14},{3,7},{4,0},{5,9},{6,2},{7,11},{8,4},{9,13},{1... | collective-permute-start | bytes 442376 | tf_op jit(solution)/shard_map/ppermute | solution.py:253
  65.2 5.5 %collective-permute-start.8 = (bf16[144,512]{1,0:T(8,128)(2,1)S(1)}, bf16[144,512]{1,0:T(8,128)(2,1)S(1)}, u32[]{:S(2)}, u32[]{:S(2)}) collective-permute-start(bf16[144,512]{1,0:T(8,128)(2,1)S(1)} %collective-permute-done.7.refs_3_), channel_id=1, source_target_pairs={{0,4},{1,13},{2,6},{3,15},{4,8},{5,1},{6,10},{7,3},{8,12},{9,5},{1... | collective-permute-start | bytes 442376 | tf_op jit(solution)/shard_map/ppermute | solution.py:253
  71.1 0.8 reshape.20
  71.9 14.3 %all-to-all-start = ((bf16[64,4,384]{2,1,0:T(4,128)(2,1)}), bf16[64,4,384]{2,1,0:T(4,128)(2,1)S(1)}, u32[]{:S(2)}, u32[]{:S(2)}) async-start(bf16[64,4,384]{2,1,0:T(4,128)(2,1)} %reshape.20), calls=%async_computation | async-start | bytes 393216 | tf_op jit(solution)/shard_map/all_to_all | solution.py:259
  86.3 1.9 %collective-permute-start.9 = (bf16[4,144,512]{2,1,0:T(8,128)(2,1)S(1)}, bf16[4,144,512]{2,1,0:T(8,128)(2,1)S(1)}, u32[]{:S(2)}, u32[]{:S(2)}) collective-permute-start(bf16[4,144,512]{2,1,0:T(8,128)(2,1)S(1)} %pad_maximum_fusion), channel_id=1, source_target_pairs={{0,2},{1,15},{2,0},{3,5},{4,6},{5,3},{6,4},{7,9},{8,10},{9,7},{10,... | collective-permute-start | bytes 1769480 | tf_op jit(solution)/shard_map/ppermute | solution.py:310
  88.2 3.8 %shard_map.85 = (f32[144,512]{1,0:T(8,128)S(1)}, f32[144,512]{1,0:T(8,128)S(1)}, f32[144,512]{1,0:T(8,128)S(1)}) custom-call(s32[4]{0:T(128)S(1)} %fusion.2.at_ref, bf16[144,512]{1,0:T(8,128)(2,1)S(1)} %shard_map.84.refs_0_, bf16[144,512]{1,0:T(8,128)(2,1)S(1)} %collective-permute-done.6.refs_1_, bf16[144,512]{1,0:T(8,128)(2,1)S(1)} %collective-permute-done.8.refs_2_, ...), custom_call_target="tpu_custom_call" | custom-call | flops 603979 | bytes 4194 | tf_op jit(solution)/shard_map/pallas_call | solution.py:208
  92.0 6.4 %collective-permute-done.9.grad_ref = bf16[4,144,512]{2,1,0:T(8,128)(2,1)S(1)} collective-permute-done((bf16[4,144,512]{2,1,0:T(8,128)(2,1)S(1)}, bf16[4,144,512]{2,1,0:T(8,128)(2,1)S(1)}, u32[]{:S(2)}, u32[]{:S(2)}) %collective-permute-start.9) | collective-permute-done | bytes 589856 | tf_op jit(solution)/shard_map/ppermute | solution.py:310
  98.4 3.5 %shard_map.86 = (f32[144,512]{1,0:T(8,128)S(1)}, bf16[144,512]{1,0:T(8,128)(2,1)S(1)}) custom-call(s32[4]{0:T(128)S(1)} %fusion.5.at_ref, bf16[4,144,512]{2,1,0:T(8,128)(2,1)S(1)} %collective-permute-done.9.grad_ref, f32[144,512]{1,0:T(8,128)S(1)} %get-tuple-element.24.own_in, f32[144,512]{1,0:T(8,128)S(1)} %get-tuple-element.25.other_in, ...), custom_call_target="tpu_custom_call" | custom-call | flops 603979 | bytes 4194 | tf_op jit(solution)/shard_map/pallas_call | solution.py:208
  101.9 3.1 %collective-permute-start.10 = (bf16[144,512]{1,0:T(8,128)(2,1)S(1)}, bf16[144,512]{1,0:T(8,128)(2,1)S(1)}, u32[]{:S(2)}, u32[]{:S(2)}) collective-permute-start(bf16[144,512]{1,0:T(8,128)(2,1)S(1)} %get-tuple-element.27), channel_id=1, source_target_pairs={{0,1},{1,0},{2,3},{3,2},{4,5},{5,4},{6,7},{7,6},{8,9},{9,8},{10,11... | collective-permute-start | bytes 442376 | tf_op jit(solution)/shard_map/ppermute | solution.py:330
  105.1 1.2 %shard_map.82 = (bf16[384,512]{1,0:T(8,128)(2,1)}, f32[8,128]{1,0:T(8,128)S(1)}) custom-call(s32[1,192]{1,0:T(1,128)S(1)} %copy-done.3, bf16[192,512]{1,0:T(8,128)(2,1)S(1)} %reshape.21.arrived_ref, bf16[384,512]{1,0:T(8,128)(2,1)S(1)} %copy-done.1), custom_call_target="tpu_custom_call" | custom-call | tf_op jit(solution)/shard_map/pallas_call | solution.py:196
  106.3 0.7 shard_map.87
  (28 shorter events, 1.3 us)
Async XLA Ops:
  0.6 29.5 %collective-permute-start.1 = (bf16[512,8192]{1,0:T(8,128)(2,1)}, bf16[512,8192]{1,0:T(8,128)(2,1)}, u32[]{:S(2)}, u32[]{:S(2)}) collective-permute-start(bf16[512,8192]{1,0:T(8,128)(2,1)} %w_own_ref.5), channel_id=1, source_target_pairs={{0,1},{1,0},{2,3},{3,2},{4,5},{5,4},{6,7},{7,6},{8,9},{9,8},{10,11... | collective-permute-start | bytes 25165832 | tf_op jit(solution)/shard_map/ppermute | solution.py:262
  16.7 13.4 %collective-permute-start = (bf16[144,512]{1,0:T(8,128)(2,1)}, bf16[144,512]{1,0:T(8,128)(2,1)S(1)}, u32[]{:S(2)}, u32[]{:S(2)}) collective-permute-start(bf16[144,512]{1,0:T(8,128)(2,1)} %refs_4_.1), channel_id=1, source_target_pairs={{0,1},{1,0},{2,3},{3,2},{4,5},{5,4},{6,7},{7,6},{8,9},{9,8},{10,11... | collective-permute-start | bytes 442376 | tf_op jit(solution)/shard_map/ppermute | solution.py:263
  20.7 29.6 %all-to-all-start.1 = ((bf16[64,4,384]{2,1,0:T(4,128)(2,1)}), bf16[64,4,384]{2,1,0:T(4,128)(2,1)S(1)}, u32[]{:S(2)}, u32[]{:S(2)}) async-start(bf16[64,4,384]{2,1,0:T(4,128)(2,1)} %reshape.22), calls=%async_computation.1 | async-start | bytes 393216 | tf_op jit(solution)/shard_map/all_to_all | solution.py:259
  33.4 12.7 %collective-permute-start.2 = (bf16[4,144,512]{2,1,0:T(8,128)(2,1)S(1)}, bf16[4,144,512]{2,1,0:T(8,128)(2,1)S(1)}, u32[]{:S(2)}, u32[]{:S(2)}) collective-permute-start(bf16[4,144,512]{2,1,0:T(8,128)(2,1)S(1)} %get-tuple-element.17), channel_id=1, source_target_pairs={{0,2},{1,15},{2,0},{3,5},{4,6},{5,3},{6,4},{7,9},{8,10},{9,7},{10,... | collective-permute-start | bytes 1769480 | tf_op jit(solution)/shard_map/ppermute | solution.py:278
  38.5 12.0 %copy-start.2 = (s32[144,1]{0,1:T(1,128)S(1)}, s32[144,1]{0,1:T(1,128)}, u32[]{:S(2)}) copy-start(s32[144,1]{0,1:T(1,128)} %param.9) | copy-start | bytes 1732
  38.5 49.7 %copy-start = (bf16[144,512]{1,0:T(8,128)(2,1)S(1)}, bf16[144,512]{1,0:T(8,128)(2,1)}, u32[]{:S(2)}) copy-start(bf16[144,512]{1,0:T(8,128)(2,1)} %refs_4_.1) | copy-start | bytes 442372
  46.2 11.6 %collective-permute-start.4 = (bf16[144,512]{1,0:T(8,128)(2,1)S(1)}, bf16[144,512]{1,0:T(8,128)(2,1)S(1)}, u32[]{:S(2)}, u32[]{:S(2)}) collective-permute-start(bf16[144,512]{1,0:T(8,128)(2,1)S(1)} %get-tuple-element.21), channel_id=1, source_target_pairs={{0,4},{1,13},{2,6},{3,15},{4,8},{5,1},{6,10},{7,3},{8,12},{9,5},{1... | collective-permute-start | bytes 442376 | tf_op jit(solution)/shard_map/ppermute | solution.py:253
  50.9 14.4 %collective-permute-start.7 = (bf16[144,512]{1,0:T(8,128)(2,1)S(1)}, bf16[144,512]{1,0:T(8,128)(2,1)S(1)}, u32[]{:S(2)}, u32[]{:S(2)}) collective-permute-start(bf16[144,512]{1,0:T(8,128)(2,1)S(1)} %shard_map.84.refs_0_), channel_id=1, source_target_pairs={{0,4},{1,13},{2,6},{3,15},{4,8},{5,1},{6,10},{7,3},{8,12},{9,5},{1... | collective-permute-start | bytes 442376 | tf_op jit(solution)/shard_map/ppermute | solution.py:253
  55.8 14.9 %collective-permute-start.3 = (bf16[144,512]{1,0:T(8,128)(2,1)S(1)}, bf16[144,512]{1,0:T(8,128)(2,1)S(1)}, u32[]{:S(2)}, u32[]{:S(2)}) collective-permute-start(bf16[144,512]{1,0:T(8,128)(2,1)S(1)} %get-tuple-element.19), channel_id=1, source_target_pairs={{0,12},{1,5},{2,14},{3,7},{4,0},{5,9},{6,2},{7,11},{8,4},{9,13},{1... | collective-permute-start | bytes 442376 | tf_op jit(solution)/shard_map/ppermute | solution.py:253
  57.8 12.9 %collective-permute-start.5 = (bf16[144,512]{1,0:T(8,128)(2,1)S(1)}, bf16[144,512]{1,0:T(8,128)(2,1)S(1)}, u32[]{:S(2)}, u32[]{:S(2)}) collective-permute-start(bf16[144,512]{1,0:T(8,128)(2,1)S(1)} %shard_map.80), channel_id=1, source_target_pairs={{0,4},{1,13},{2,6},{3,15},{4,8},{5,1},{6,10},{7,3},{8,12},{9,5},{1... | collective-permute-start | bytes 442376 | tf_op jit(solution)/shard_map/ppermute | solution.py:253
  63.3 22.9 %collective-permute-start.6 = (bf16[144,512]{1,0:T(8,128)(2,1)S(1)}, bf16[144,512]{1,0:T(8,128)(2,1)S(1)}, u32[]{:S(2)}, u32[]{:S(2)}) collective-permute-start(bf16[144,512]{1,0:T(8,128)(2,1)S(1)} %shard_map.84.refs_0_), channel_id=1, source_target_pairs={{0,12},{1,5},{2,14},{3,7},{4,0},{5,9},{6,2},{7,11},{8,4},{9,13},{1... | collective-permute-start | bytes 442376 | tf_op jit(solution)/shard_map/ppermute | solution.py:253
  65.2 20.9 %collective-permute-start.8 = (bf16[144,512]{1,0:T(8,128)(2,1)S(1)}, bf16[144,512]{1,0:T(8,128)(2,1)S(1)}, u32[]{:S(2)}, u32[]{:S(2)}) collective-permute-start(bf16[144,512]{1,0:T(8,128)(2,1)S(1)} %collective-permute-done.7.refs_3_), channel_id=1, source_target_pairs={{0,4},{1,13},{2,6},{3,15},{4,8},{5,1},{6,10},{7,3},{8,12},{9,5},{1... | collective-permute-start | bytes 442376 | tf_op jit(solution)/shard_map/ppermute | solution.py:253
  71.9 33.1 %all-to-all-start = ((bf16[64,4,384]{2,1,0:T(4,128)(2,1)}), bf16[64,4,384]{2,1,0:T(4,128)(2,1)S(1)}, u32[]{:S(2)}, u32[]{:S(2)}) async-start(bf16[64,4,384]{2,1,0:T(4,128)(2,1)} %reshape.20), calls=%async_computation | async-start | bytes 393216 | tf_op jit(solution)/shard_map/all_to_all | solution.py:259
  86.3 12.1 %collective-permute-start.9 = (bf16[4,144,512]{2,1,0:T(8,128)(2,1)S(1)}, bf16[4,144,512]{2,1,0:T(8,128)(2,1)S(1)}, u32[]{:S(2)}, u32[]{:S(2)}) collective-permute-start(bf16[4,144,512]{2,1,0:T(8,128)(2,1)S(1)} %pad_maximum_fusion), channel_id=1, source_target_pairs={{0,2},{1,15},{2,0},{3,5},{4,6},{5,3},{6,4},{7,9},{8,10},{9,7},{10,... | collective-permute-start | bytes 1769480 | tf_op jit(solution)/shard_map/ppermute | solution.py:310
  98.4 6.7 %copy-start.1 = (bf16[384,512]{1,0:T(8,128)(2,1)S(1)}, bf16[384,512]{1,0:T(8,128)(2,1)}, u32[]{:S(2)}) copy-start(bf16[384,512]{1,0:T(8,128)(2,1)} %text_ref.1) | copy-start | bytes 1179652
  98.4 6.7 %copy-start.3 = (s32[1,192]{1,0:T(1,128)S(1)}, s32[1,192]{1,0:T(1,128)}, u32[]{:S(2)}) copy-start(s32[1,192]{1,0:T(1,128)} %offsets_ref.3) | copy-start | bytes 2308
  101.9 4.4 %collective-permute-start.10 = (bf16[144,512]{1,0:T(8,128)(2,1)S(1)}, bf16[144,512]{1,0:T(8,128)(2,1)S(1)}, u32[]{:S(2)}, u32[]{:S(2)}) collective-permute-start(bf16[144,512]{1,0:T(8,128)(2,1)S(1)} %get-tuple-element.27), channel_id=1, source_target_pairs={{0,1},{1,0},{2,3},{3,2},{4,5},{5,4},{6,7},{7,6},{8,9},{9,8},{10,11... | collective-permute-start | bytes 442376 | tf_op jit(solution)/shard_map/ppermute | solution.py:330

commit v9 on v8

--- a/solution.py
+++ b/solution.py
@@ -83,6 +83,9 @@
 
 
 TRANS = (((1,), (1,)), ((), ()))
+
+
+WIDTHS = 16
 
 
 def fetch(at_ref, sources, held_ref, sems):
@@ -129,12 +132,16 @@
         out_ref[j] = total.astype(BF16)
 
 
-def add_kernel(kept_ref, beside_ref, token_ref, total_ref, *term_refs):
+def add_sent_kernel(kept_ref, beside_ref, second_ref, third_ref):
+    for j, term_ref in enumerate((second_ref, third_ref)):
+        total = kept_ref[2 + j].astype(F32) + beside_ref[j].astype(F32)
+        term_ref[...] = total.astype(BF16)
+
+
+def add_held_kernel(kept_ref, beside_ref, token_ref, total_ref, first_ref):
     token_ref[...] = jnp.zeros_like(token_ref)
-    total_ref[...] = kept_ref[0].astype(F32) + beside_ref[0].astype(F32)
-    for j, term_ref in enumerate(term_refs, 1):
-        total = kept_ref[j].astype(F32) + beside_ref[j].astype(F32)
-        term_ref[...] = total.astype(term_ref.dtype)
+    for j, term_ref in enumerate((total_ref, first_ref)):
+        term_ref[...] = kept_ref[j].astype(F32) + beside_ref[j].astype(F32)
 
 
 def relay_kernel(held_ref, arrived_ref, out_ref):
@@ -203,7 +210,7 @@
 
 
 def product(kernel, outs, at, args, sources, blocks, share=1):
-    hid, width = sources[0].shape[0], sources[0].shape[1] // (4 * blocks)
+    hid, width = sources[0].shape[0], sources[0].shape[1] // WIDTHS
     rows = args[0].shape[-2]
     got = pl.pallas_call(
         kernel,
@@ -267,21 +274,22 @@
     returned = exchange(by_group(gathered))
 
     terms_out = ((half, rows, width), BF16)
+    two_out = ((2, rows, width), BF16)
     sent, act = product(
         forward_first_kernel,
-        [terms_out, ((rows, 2 * hid), BF16)],
-        opposite,
+        [two_out, ((rows, 2 * hid), BF16)],
+        opposite[2:],
         (pre_other,),
         (*weights, pre_hidden),
-        half,
-    )
-    beside_terms = lax.ppermute(sent, ("line", "core"), beside)
+        2,
+    )
+    beside_sent = lax.ppermute(sent, ("line", "core"), beside)
+    held = product(forward_second_kernel, [two_out], opposite[:2], (act,), weights, 2)
+    beside_held = lax.ppermute(held, ("line", "core"), beside)
     kept = product(forward_second_kernel, [terms_out], same, (act,), weights, half)
-    token, total, first, second, third = call(
-        add_kernel,
-        [((8, 128), F32)] + [((rows, width), F32)] * 2 + [((rows, width), BF16)] * 2,
-        kept,
-        beside_terms,
+    second, third = call(add_sent_kernel, [((rows, width), BF16)] * 2, kept, beside_sent)
+    token, total, first = call(
+        add_held_kernel, [((8, 128), F32)] + [((rows, width), F32)] * 2, kept, beside_held
     )
     passed = relay(second, 2)
     back = relay(third, -2)

time: 108 us -> 108 us (level)
  waiting for transfers between devices: 10.8 us -> 7.67 us
  Pallas kernels: 17.8 us -> 19.6 us
  starting transfers between devices: 75.5 us -> 77.1 us
    ppermute x1 -> x2, waiting for transfers between devices: 4.33 us -> 0.01 us  [the longest x1 0.01 us: on_device(): beside_sent = lax.ppermute(sent, ('line', 'core'), beside)]
    ppermute x1 -> x2, starting transfers between devices: 5.1 us -> 7.02 us  [the longest x1 5.1 us: on_device(): beside_sent = lax.ppermute(sent, ('line', 'core'), beside)]
    pallas_call x4 -> x5, Pallas kernels: 13.6 us -> 15.4 us  [product(): pl.pallas_call(kernel, in_specs=[SMEM] + [VMEM] * len(args) + [HBM] * len...]
    ppermute x1, waiting for transfers between devices: 0.01 us -> 1.17 us  [on_device(): pre_other = lax.ppermute(pre_hidden, 'core', cores)]
    ppermute x1, starting transfers between devices: 3.07 us -> 1.92 us  [on_device(): other = lax.ppermute(other, 'core', cores)]
    pallas_call x7 -> x8, Pallas kernels: 4.14 us -> 4.13 us  [call(): pl.pallas_call(kernel, in_specs=[VMEM] * len(args), out_specs=[VMEM] * le...]
  transfers between devices with their start and end apart: 13 -> 14, of which waited for: 2 -> 2; matrix products, arithmetic and copies ran while one was open for 2% -> 2% of each run, Pallas kernels for 16% -> 18%
where the time goes in v9:
time: 108 us; the launch traced here: 107 us
  starting transfers between devices  77.1 us (71%)
  Pallas kernels  19.6 us (18%)
  waiting for transfers between devices  7.67 us (7%)
  local copies, waits for them, and re-layouts  1.92 us (2%)
    all_to_all x2, starting transfers between devices, exchange(): x = lax.all_to_all(x, 'group', split_axis=0, concat_axis=0, tiled=True)  24.1 us
    ppermute x6, starting transfers between devices, relay(): return lax.ppermute(x, ('line', 'core'), pairs)  23.9 us
    ppermute x1, starting transfers between devices, on_device(): w_other = lax.ppermute(proj_weight, 'core', cores)  16.1 us
    pallas_call x5, Pallas kernels, product(): pl.pallas_call(kernel, in_specs=[SMEM] + [VMEM] * len(args) + [HBM] * len...  15.4 us
    ppermute x1, waiting for transfers between devices, on_device(): far = lax.ppermute(jnp.stack(near), ('line', 'core'), beside)  6.43 us
    ppermute x1, starting transfers between devices, on_device(): beside_sent = lax.ppermute(sent, ('line', 'core'), beside)  5.1 us
    pallas_call x8, Pallas kernels, call(): pl.pallas_call(kernel, in_specs=[VMEM] * len(args), out_specs=[VMEM] * le...  4.13 us
    ppermute x1, starting transfers between devices, on_device(): pre_other = lax.ppermute(pre_hidden, 'core', cores)  2.2 us
  transfers between devices with their start and end apart: 14, of which 2 were waited for; matrix products, arithmetic and copies ran while one was open for 2% of the time, Pallas kernels for 18%

profile of v9, /device:TPU:1, one launch (start us, length us, event | category | flops | bytes accessed | tf_op | source)
XLA Modules:
  0.0 107.3 jit_solution(10442944307906236363)
XLA Ops:
  0.6 16.1 %collective-permute-start.1 = (bf16[512,8192]{1,0:T(8,128)(2,1)}, bf16[512,8192]{1,0:T(8,128)(2,1)}, u32[]{:S(2)}, u32[]{:S(2)}) collective-permute-start(bf16[512,8192]{1,0:T(8,128)(2,1)} %w_own_ref.7), channel_id=1, source_target_pairs={{0,1},{1,0},{2,3},{3,2},{4,5},{5,4},{6,7},{7,6},{8,9},{9,8},{10,11... | collective-permute-start | bytes 25165832 | tf_op jit(solution)/shard_map/ppermute | solution.py:269
  16.7 1.3 %shard_map.85 = bf16[192,512]{1,0:T(8,128)(2,1)S(1)} custom-call(s32[1,192]{1,0:T(1,128)} %offsets_ref.3, bf16[384,512]{1,0:T(8,128)(2,1)} %grad_ref.1), custom_call_target="tpu_custom_call" | custom-call | tf_op jit(solution)/shard_map/pallas_call | solution.py:203
  18.0 0.8 reshape.22
  18.8 9.3 %all-to-all-start.1 = ((bf16[64,4,384]{2,1,0:T(4,128)(2,1)}), bf16[64,4,384]{2,1,0:T(4,128)(2,1)S(1)}, u32[]{:S(2)}, u32[]{:S(2)}) async-start(bf16[64,4,384]{2,1,0:T(4,128)(2,1)} %reshape.22), calls=%async_computation.1 | async-start | bytes 393216 | tf_op jit(solution)/shard_map/all_to_all | solution.py:266
  28.1 2.2 %collective-permute-start = (bf16[144,512]{1,0:T(8,128)(2,1)}, bf16[144,512]{1,0:T(8,128)(2,1)S(1)}, u32[]{:S(2)}, u32[]{:S(2)}) collective-permute-start(bf16[144,512]{1,0:T(8,128)(2,1)} %refs_4_.1), channel_id=1, source_target_pairs={{0,1},{1,0},{2,3},{3,2},{4,5},{5,4},{6,7},{7,6},{8,9},{9,8},{10,11... | collective-permute-start | bytes 442376 | tf_op jit(solution)/shard_map/ppermute | solution.py:270
  30.4 1.2 %collective-permute-done.other_ref = bf16[144,512]{1,0:T(8,128)(2,1)S(1)} collective-permute-done((bf16[144,512]{1,0:T(8,128)(2,1)}, bf16[144,512]{1,0:T(8,128)(2,1)S(1)}, u32[]{:S(2)}, u32[]{:S(2)}) %collective-permute-start) | collective-permute-done | bytes 147488 | tf_op jit(solution)/shard_map/ppermute | solution.py:270
  31.6 2.5 %shard_map.77 = (bf16[2,144,512]{2,1,0:T(8,128)(2,1)S(1)}, bf16[144,1024]{1,0:T(8,128)(2,1)S(1)}) custom-call(s32[2]{0:T(128)S(1)} %get-tuple-element.31.at_ref, bf16[144,512]{1,0:T(8,128)(2,1)S(1)} %collective-permute-done.other_ref, bf16[512,8192]{1,0:T(8,128)(2,1)} %w_own_ref.7, bf16[512,8192]{1,0:T(8,128)(2,1)} %collective-permute-done.1.w_other_ref.refs_6_, ...), custom_call_target="tpu_custom_call" | custom-call | flops 301989888 | bytes 2097152 | tf_op jit(solution)/shard_map/pallas_call | solution.py:215
  34.1 5.1 %collective-permute-start.3 = (bf16[2,144,512]{2,1,0:T(8,128)(2,1)S(1)}, bf16[2,144,512]{2,1,0:T(8,128)(2,1)S(1)}, u32[]{:S(2)}, u32[]{:S(2)}) collective-permute-start(bf16[2,144,512]{2,1,0:T(8,128)(2,1)S(1)} %get-tuple-element.18), channel_id=1, source_target_pairs={{0,2},{1,15},{2,0},{3,5},{4,6},{5,3},{6,4},{7,9},{8,10},{9,7},{10,... | collective-permute-start | bytes 884744 | tf_op jit(solution)/shard_map/ppermute | solution.py:286
  39.3 2.5 %shard_map.79 = bf16[2,144,512]{2,1,0:T(8,128)(2,1)S(1)} custom-call(s32[2]{0:T(128)S(1)} %get-tuple-element.30.at_ref, bf16[144,1024]{1,0:T(8,128)(2,1)S(1)} %get-tuple-element.16.act_ref, bf16[512,8192]{1,0:T(8,128)(2,1)} %w_own_ref.7, bf16[512,8192]{1,0:T(8,128)(2,1)} %collective-permute-done.1.w_other_ref.refs_6_), custom_call_target="tpu_custom_call" | custom-call | flops 301989888 | bytes 2097152 | tf_op jit(solution)/shard_map/pallas_call | solution.py:215
  41.7 1.9 %collective-permute-start.2 = (bf16[2,144,512]{2,1,0:T(8,128)(2,1)S(1)}, bf16[2,144,512]{2,1,0:T(8,128)(2,1)S(1)}, u32[]{:S(2)}, u32[]{:S(2)}) collective-permute-start(bf16[2,144,512]{2,1,0:T(8,128)(2,1)S(1)} %shard_map.79), channel_id=1, source_target_pairs={{0,2},{1,15},{2,0},{3,5},{4,6},{5,3},{6,4},{7,9},{8,10},{9,7},{10,... | collective-permute-start | bytes 884744 | tf_op jit(solution)/shard_map/ppermute | solution.py:288
  43.7 3.2 %shard_map.78.kept_ref = bf16[4,144,512]{2,1,0:T(8,128)(2,1)S(1)} custom-call(s32[4]{0:T(128)S(1)} %fusion.2.at_ref, bf16[144,1024]{1,0:T(8,128)(2,1)S(1)} %get-tuple-element.16.act_ref, bf16[512,8192]{1,0:T(8,128)(2,1)} %w_own_ref.7, bf16[512,8192]{1,0:T(8,128)(2,1)} %collective-permute-done.1.w_other_ref.refs_6_), custom_call_target="tpu_custom_call" | custom-call | flops 603979776 | bytes 4194304 | tf_op jit(solution)/shard_map/pallas_call | solution.py:215
  47.0 4.1 %collective-permute-start.5 = (bf16[144,512]{1,0:T(8,128)(2,1)S(1)}, bf16[144,512]{1,0:T(8,128)(2,1)S(1)}, u32[]{:S(2)}, u32[]{:S(2)}) collective-permute-start(bf16[144,512]{1,0:T(8,128)(2,1)S(1)} %get-tuple-element.21), channel_id=1, source_target_pairs={{0,4},{1,13},{2,6},{3,15},{4,8},{5,1},{6,10},{7,3},{8,12},{9,5},{1... | collective-permute-start | bytes 442376 | tf_op jit(solution)/shard_map/ppermute | solution.py:260
  51.8 5.0 %collective-permute-start.8 = (bf16[144,512]{1,0:T(8,128)(2,1)S(1)}, bf16[144,512]{1,0:T(8,128)(2,1)S(1)}, u32[]{:S(2)}, u32[]{:S(2)}) collective-permute-start(bf16[144,512]{1,0:T(8,128)(2,1)S(1)} %shard_map.86.refs_0_), channel_id=1, source_target_pairs={{0,4},{1,13},{2,6},{3,15},{4,8},{5,1},{6,10},{7,3},{8,12},{9,5},{1... | collective-permute-start | bytes 442376 | tf_op jit(solution)/shard_map/ppermute | solution.py:260
  56.8 1.9 %collective-permute-start.4 = (bf16[144,512]{1,0:T(8,128)(2,1)S(1)}, bf16[144,512]{1,0:T(8,128)(2,1)S(1)}, u32[]{:S(2)}, u32[]{:S(2)}) collective-permute-start(bf16[144,512]{1,0:T(8,128)(2,1)S(1)} %get-tuple-element.19), channel_id=1, source_target_pairs={{0,12},{1,5},{2,14},{3,7},{4,0},{5,9},{6,2},{7,11},{8,4},{9,13},{1... | collective-permute-start | bytes 442376 | tf_op jit(solution)/shard_map/ppermute | solution.py:260
  58.7 5.5 %collective-permute-start.6 = (bf16[144,512]{1,0:T(8,128)(2,1)S(1)}, bf16[144,512]{1,0:T(8,128)(2,1)S(1)}, u32[]{:S(2)}, u32[]{:S(2)}) collective-permute-start(bf16[144,512]{1,0:T(8,128)(2,1)S(1)} %shard_map.82), channel_id=1, source_target_pairs={{0,4},{1,13},{2,6},{3,15},{4,8},{5,1},{6,10},{7,3},{8,12},{9,5},{1... | collective-permute-start | bytes 442376 | tf_op jit(solution)/shard_map/ppermute | solution.py:260
  64.2 1.9 %collective-permute-start.7 = (bf16[144,512]{1,0:T(8,128)(2,1)S(1)}, bf16[144,512]{1,0:T(8,128)(2,1)S(1)}, u32[]{:S(2)}, u32[]{:S(2)}) collective-permute-start(bf16[144,512]{1,0:T(8,128)(2,1)S(1)} %shard_map.86.refs_0_), channel_id=1, source_target_pairs={{0,12},{1,5},{2,14},{3,7},{4,0},{5,9},{6,2},{7,11},{8,4},{9,13},{1... | collective-permute-start | bytes 442376 | tf_op jit(solution)/shard_map/ppermute | solution.py:260
  66.2 5.5 %collective-permute-start.9 = (bf16[144,512]{1,0:T(8,128)(2,1)S(1)}, bf16[144,512]{1,0:T(8,128)(2,1)S(1)}, u32[]{:S(2)}, u32[]{:S(2)}) collective-permute-start(bf16[144,512]{1,0:T(8,128)(2,1)S(1)} %collective-permute-done.8.refs_3_), channel_id=1, source_target_pairs={{0,4},{1,13},{2,6},{3,15},{4,8},{5,1},{6,10},{7,3},{8,12},{9,5},{1... | collective-permute-start | bytes 442376 | tf_op jit(solution)/shard_map/ppermute | solution.py:260
  72.8 14.8 %all-to-all-start = ((bf16[64,4,384]{2,1,0:T(4,128)(2,1)}), bf16[64,4,384]{2,1,0:T(4,128)(2,1)S(1)}, u32[]{:S(2)}, u32[]{:S(2)}) async-start(bf16[64,4,384]{2,1,0:T(4,128)(2,1)} %reshape.20), calls=%async_computation | async-start | bytes 393216 | tf_op jit(solution)/shard_map/all_to_all | solution.py:266
  87.7 1.9 %collective-permute-start.10 = (bf16[4,144,512]{2,1,0:T(8,128)(2,1)S(1)}, bf16[4,144,512]{2,1,0:T(8,128)(2,1)S(1)}, u32[]{:S(2)}, u32[]{:S(2)}) collective-permute-start(bf16[4,144,512]{2,1,0:T(8,128)(2,1)S(1)} %pad_maximum_fusion), channel_id=1, source_target_pairs={{0,2},{1,15},{2,0},{3,5},{4,6},{5,3},{6,4},{7,9},{8,10},{9,7},{10,... | collective-permute-start | bytes 1769480 | tf_op jit(solution)/shard_map/ppermute | solution.py:318
  89.6 3.8 %shard_map.87 = (f32[144,512]{1,0:T(8,128)S(1)}, f32[144,512]{1,0:T(8,128)S(1)}, f32[144,512]{1,0:T(8,128)S(1)}) custom-call(s32[4]{0:T(128)S(1)} %fusion.2.at_ref, bf16[144,512]{1,0:T(8,128)(2,1)S(1)} %shard_map.86.refs_0_, bf16[144,512]{1,0:T(8,128)(2,1)S(1)} %collective-permute-done.7.refs_1_, bf16[144,512]{1,0:T(8,128)(2,1)S(1)} %collective-permute-done.9.refs_2_, ...), custom_call_target="tpu_custom_call" | custom-call | flops 603979 | bytes 4194 | tf_op jit(solution)/shard_map/pallas_call | solution.py:215
  93.4 6.4 %collective-permute-done.10.grad_ref = bf16[4,144,512]{2,1,0:T(8,128)(2,1)S(1)} collective-permute-done((bf16[4,144,512]{2,1,0:T(8,128)(2,1)S(1)}, bf16[4,144,512]{2,1,0:T(8,128)(2,1)S(1)}, u32[]{:S(2)}, u32[]{:S(2)}) %collective-permute-start.10) | collective-permute-done | bytes 589856 | tf_op jit(solution)/shard_map/ppermute | solution.py:318
  99.8 3.5 %shard_map.88 = (f32[144,512]{1,0:T(8,128)S(1)}, bf16[144,512]{1,0:T(8,128)(2,1)S(1)}) custom-call(s32[4]{0:T(128)S(1)} %fusion.5.at_ref, bf16[4,144,512]{2,1,0:T(8,128)(2,1)S(1)} %collective-permute-done.10.grad_ref, f32[144,512]{1,0:T(8,128)S(1)} %get-tuple-element.24.own_in, f32[144,512]{1,0:T(8,128)S(1)} %get-tuple-element.25.other_in, ...), custom_call_target="tpu_custom_call" | custom-call | flops 603979 | bytes 4194 | tf_op jit(solution)/shard_map/pallas_call | solution.py:215
  103.3 1.9 %collective-permute-start.11 = (bf16[144,512]{1,0:T(8,128)(2,1)S(1)}, bf16[144,512]{1,0:T(8,128)(2,1)S(1)}, u32[]{:S(2)}, u32[]{:S(2)}) collective-permute-start(bf16[144,512]{1,0:T(8,128)(2,1)S(1)} %get-tuple-element.27), channel_id=1, source_target_pairs={{0,1},{1,0},{2,3},{3,2},{4,5},{5,4},{6,7},{7,6},{8,9},{9,8},{10,11... | collective-permute-start | bytes 442376 | tf_op jit(solution)/shard_map/ppermute | solution.py:338
  105.4 1.2 %shard_map.84 = (bf16[384,512]{1,0:T(8,128)(2,1)}, f32[8,128]{1,0:T(8,128)S(1)}) custom-call(s32[1,192]{1,0:T(1,128)S(1)} %copy-done.3, bf16[192,512]{1,0:T(8,128)(2,1)S(1)} %reshape.21.arrived_ref, bf16[384,512]{1,0:T(8,128)(2,1)S(1)} %copy-done.1), custom_call_target="tpu_custom_call" | custom-call | tf_op jit(solution)/shard_map/pallas_call | solution.py:203
  (33 shorter events, 2.9 us)
Async XLA Ops:
  0.6 31.0 %collective-permute-start.1 = (bf16[512,8192]{1,0:T(8,128)(2,1)}, bf16[512,8192]{1,0:T(8,128)(2,1)}, u32[]{:S(2)}, u32[]{:S(2)}) collective-permute-start(bf16[512,8192]{1,0:T(8,128)(2,1)} %w_own_ref.7), channel_id=1, source_target_pairs={{0,1},{1,0},{2,3},{3,2},{4,5},{5,4},{6,7},{7,6},{8,9},{9,8},{10,11... | collective-permute-start | bytes 25165832 | tf_op jit(solution)/shard_map/ppermute | solution.py:269
  18.8 32.3 %all-to-all-start.1 = ((bf16[64,4,384]{2,1,0:T(4,128)(2,1)}), bf16[64,4,384]{2,1,0:T(4,128)(2,1)S(1)}, u32[]{:S(2)}, u32[]{:S(2)}) async-start(bf16[64,4,384]{2,1,0:T(4,128)(2,1)} %reshape.22), calls=%async_computation.1 | async-start | bytes 393216 | tf_op jit(solution)/shard_map/all_to_all | solution.py:266
  28.1 3.5 %collective-permute-start = (bf16[144,512]{1,0:T(8,128)(2,1)}, bf16[144,512]{1,0:T(8,128)(2,1)S(1)}, u32[]{:S(2)}, u32[]{:S(2)}) collective-permute-start(bf16[144,512]{1,0:T(8,128)(2,1)} %refs_4_.1), channel_id=1, source_target_pairs={{0,1},{1,0},{2,3},{3,2},{4,5},{5,4},{6,7},{7,6},{8,9},{9,8},{10,11... | collective-permute-start | bytes 442376 | tf_op jit(solution)/shard_map/ppermute | solution.py:270
  34.1 12.8 %collective-permute-start.3 = (bf16[2,144,512]{2,1,0:T(8,128)(2,1)S(1)}, bf16[2,144,512]{2,1,0:T(8,128)(2,1)S(1)}, u32[]{:S(2)}, u32[]{:S(2)}) collective-permute-start(bf16[2,144,512]{2,1,0:T(8,128)(2,1)S(1)} %get-tuple-element.18), channel_id=1, source_target_pairs={{0,2},{1,15},{2,0},{3,5},{4,6},{5,3},{6,4},{7,9},{8,10},{9,7},{10,... | collective-permute-start | bytes 884744 | tf_op jit(solution)/shard_map/ppermute | solution.py:286
  41.7 9.6 %collective-permute-start.2 = (bf16[2,144,512]{2,1,0:T(8,128)(2,1)S(1)}, bf16[2,144,512]{2,1,0:T(8,128)(2,1)S(1)}, u32[]{:S(2)}, u32[]{:S(2)}) collective-permute-start(bf16[2,144,512]{2,1,0:T(8,128)(2,1)S(1)} %shard_map.79), channel_id=1, source_target_pairs={{0,2},{1,15},{2,0},{3,5},{4,6},{5,3},{6,4},{7,9},{8,10},{9,7},{10,... | collective-permute-start | bytes 884744 | tf_op jit(solution)/shard_map/ppermute | solution.py:288
  43.7 7.7 %copy-start.2 = (s32[144,1]{0,1:T(1,128)S(1)}, s32[144,1]{0,1:T(1,128)}, u32[]{:S(2)}) copy-start(s32[144,1]{0,1:T(1,128)} %param.9) | copy-start | bytes 1732
  43.7 45.9 %copy-start = (bf16[144,512]{1,0:T(8,128)(2,1)S(1)}, bf16[144,512]{1,0:T(8,128)(2,1)}, u32[]{:S(2)}) copy-start(bf16[144,512]{1,0:T(8,128)(2,1)} %refs_4_.1) | copy-start | bytes 442372
  47.0 11.7 %collective-permute-start.5 = (bf16[144,512]{1,0:T(8,128)(2,1)S(1)}, bf16[144,512]{1,0:T(8,128)(2,1)S(1)}, u32[]{:S(2)}, u32[]{:S(2)}) collective-permute-start(bf16[144,512]{1,0:T(8,128)(2,1)S(1)} %get-tuple-element.21), channel_id=1, source_target_pairs={{0,4},{1,13},{2,6},{3,15},{4,8},{5,1},{6,10},{7,3},{8,12},{9,5},{1... | collective-permute-start | bytes 442376 | tf_op jit(solution)/shard_map/ppermute | solution.py:260
  51.8 14.4 %collective-permute-start.8 = (bf16[144,512]{1,0:T(8,128)(2,1)S(1)}, bf16[144,512]{1,0:T(8,128)(2,1)S(1)}, u32[]{:S(2)}, u32[]{:S(2)}) collective-permute-start(bf16[144,512]{1,0:T(8,128)(2,1)S(1)} %shard_map.86.refs_0_), channel_id=1, source_target_pairs={{0,4},{1,13},{2,6},{3,15},{4,8},{5,1},{6,10},{7,3},{8,12},{9,5},{1... | collective-permute-start | bytes 442376 | tf_op jit(solution)/shard_map/ppermute | solution.py:260
  56.8 14.9 %collective-permute-start.4 = (bf16[144,512]{1,0:T(8,128)(2,1)S(1)}, bf16[144,512]{1,0:T(8,128)(2,1)S(1)}, u32[]{:S(2)}, u32[]{:S(2)}) collective-permute-start(bf16[144,512]{1,0:T(8,128)(2,1)S(1)} %get-tuple-element.19), channel_id=1, source_target_pairs={{0,12},{1,5},{2,14},{3,7},{4,0},{5,9},{6,2},{7,11},{8,4},{9,13},{1... | collective-permute-start | bytes 442376 | tf_op jit(solution)/shard_map/ppermute | solution.py:260
  58.7 12.9 %collective-permute-start.6 = (bf16[144,512]{1,0:T(8,128)(2,1)S(1)}, bf16[144,512]{1,0:T(8,128)(2,1)S(1)}, u32[]{:S(2)}, u32[]{:S(2)}) collective-permute-start(bf16[144,512]{1,0:T(8,128)(2,1)S(1)} %shard_map.82), channel_id=1, source_target_pairs={{0,4},{1,13},{2,6},{3,15},{4,8},{5,1},{6,10},{7,3},{8,12},{9,5},{1... | collective-permute-start | bytes 442376 | tf_op jit(solution)/shard_map/ppermute | solution.py:260
  64.2 23.4 %collective-permute-start.7 = (bf16[144,512]{1,0:T(8,128)(2,1)S(1)}, bf16[144,512]{1,0:T(8,128)(2,1)S(1)}, u32[]{:S(2)}, u32[]{:S(2)}) collective-permute-start(bf16[144,512]{1,0:T(8,128)(2,1)S(1)} %shard_map.86.refs_0_), channel_id=1, source_target_pairs={{0,12},{1,5},{2,14},{3,7},{4,0},{5,9},{6,2},{7,11},{8,4},{9,13},{1... | collective-permute-start | bytes 442376 | tf_op jit(solution)/shard_map/ppermute | solution.py:260
  66.2 21.5 %collective-permute-start.9 = (bf16[144,512]{1,0:T(8,128)(2,1)S(1)}, bf16[144,512]{1,0:T(8,128)(2,1)S(1)}, u32[]{:S(2)}, u32[]{:S(2)}) collective-permute-start(bf16[144,512]{1,0:T(8,128)(2,1)S(1)} %collective-permute-done.8.refs_3_), channel_id=1, source_target_pairs={{0,4},{1,13},{2,6},{3,15},{4,8},{5,1},{6,10},{7,3},{8,12},{9,5},{1... | collective-permute-start | bytes 442376 | tf_op jit(solution)/shard_map/ppermute | solution.py:260
  72.8 32.5 %all-to-all-start = ((bf16[64,4,384]{2,1,0:T(4,128)(2,1)}), bf16[64,4,384]{2,1,0:T(4,128)(2,1)S(1)}, u32[]{:S(2)}, u32[]{:S(2)}) async-start(bf16[64,4,384]{2,1,0:T(4,128)(2,1)} %reshape.20), calls=%async_computation | async-start | bytes 393216 | tf_op jit(solution)/shard_map/all_to_all | solution.py:266
  87.7 12.1 %collective-permute-start.10 = (bf16[4,144,512]{2,1,0:T(8,128)(2,1)S(1)}, bf16[4,144,512]{2,1,0:T(8,128)(2,1)S(1)}, u32[]{:S(2)}, u32[]{:S(2)}) collective-permute-start(bf16[4,144,512]{2,1,0:T(8,128)(2,1)S(1)} %pad_maximum_fusion), channel_id=1, source_target_pairs={{0,2},{1,15},{2,0},{3,5},{4,6},{5,3},{6,4},{7,9},{8,10},{9,7},{10,... | collective-permute-start | bytes 1769480 | tf_op jit(solution)/shard_map/ppermute | solution.py:318
  99.8 5.6 %copy-start.1 = (bf16[384,512]{1,0:T(8,128)(2,1)S(1)}, bf16[384,512]{1,0:T(8,128)(2,1)}, u32[]{:S(2)}) copy-start(bf16[384,512]{1,0:T(8,128)(2,1)} %text_ref.1) | copy-start | bytes 1179652
  99.8 5.6 %copy-start.3 = (s32[1,192]{1,0:T(1,128)S(1)}, s32[1,192]{1,0:T(1,128)}, u32[]{:S(2)}) copy-start(s32[1,192]{1,0:T(1,128)} %offsets_ref.3) | copy-start | bytes 2308
  103.3 3.3 %collective-permute-start.11 = (bf16[144,512]{1,0:T(8,128)(2,1)S(1)}, bf16[144,512]{1,0:T(8,128)(2,1)S(1)}, u32[]{:S(2)}, u32[]{:S(2)}) collective-permute-start(bf16[144,512]{1,0:T(8,128)(2,1)S(1)} %get-tuple-element.27), channel_id=1, source_target_pairs={{0,1},{1,0},{2,3},{3,2},{4,5},{5,4},{6,7},{7,6},{8,9},{9,8},{10,11... | collective-permute-start | bytes 442376 | tf_op jit(solution)/shard_map/ppermute | solution.py:338

commit v10 on v8

--- a/solution.py
+++ b/solution.py
@@ -85,15 +85,15 @@
 TRANS = (((1,), (1,)), ((), ()))
 
 
-def fetch(at_ref, sources, held_ref, sems):
+def fetch(at_ref, sources, held_ref, sems, first=0):
     blocks, width = held_ref.shape[1], held_ref.shape[3]
     copies = []
     for j in range(blocks):
-        columns = pl.ds(pl.multiple_of(at_ref[j] * width, width), width)
+        columns = pl.ds(pl.multiple_of(at_ref[first + j] * width, width), width)
         pair = []
         for k, source in enumerate(sources):
             pair.append(
-                pltpu.make_async_copy(source.at[:, columns], held_ref.at[k, j], sems.at[k, j])
+                pltpu.make_async_copy(source.at[:, columns], held_ref.at[k, j], sems.at[k, first + j])
             )
             pair[-1].start()
         copies.append(pair)
@@ -143,8 +143,10 @@
 
 def backward_first_kernel(blocks, at_ref, *refs):
     grad_refs, refs = refs[:blocks], refs[blocks:]
-    pre_ref, w_own_ref, w_other_ref, own_ref, other_ref, slope_ref, held_ref, sems = refs
+    pre_ref, w_own_ref, w_other_ref = refs[:3]
+    own_ref, other_ref, slope_ref, next_ref, held_ref, sems = refs[3:]
     copies = fetch(at_ref, (w_own_ref, w_other_ref), held_ref, sems)
+    later = fetch(at_ref, (w_own_ref, w_other_ref), next_ref, sems, blocks)
     slope_ref[...] = gelu_slope(pre_ref[...].astype(F32))
     own, other = 0.0, 0.0
     for grad_ref, j, pair in zip(grad_refs, range(blocks), copies):
@@ -154,16 +156,14 @@
         other += lax.dot_general(grad_ref[...], held_ref[1, j], TRANS, preferred_element_type=F32)
     own_ref[...] = own
     other_ref[...] = other
-
-
-def backward_second_kernel(
-    at_ref, grad_ref, own_in, other_in, w_own_ref, w_other_ref, own_ref, other_ref, held_ref, sems
-):
-    copies = fetch(at_ref, (w_own_ref, w_other_ref), held_ref, sems)
-    own, other = own_in[...], other_in[...]
-    for j, pair in enumerate(copies):
+    for pair in later:
         for copy in pair:
             copy.wait()
+
+
+def backward_second_kernel(grad_ref, own_in, other_in, held_ref, own_ref, other_ref):
+    own, other = own_in[...], other_in[...]
+    for j in range(grad_ref.shape[0]):
         own += lax.dot_general(grad_ref[j], held_ref[0, j], TRANS, preferred_element_type=F32)
         other += lax.dot_general(grad_ref[j], held_ref[1, j], TRANS, preferred_element_type=F32)
     own_ref[...] = own
@@ -198,6 +198,7 @@
         in_specs=[VMEM] * len(args),
         out_specs=[VMEM] * len(outs),
         out_shape=out_shape,
+        compiler_params=pltpu.CompilerParams(vmem_limit_bytes=24 * 1024 * 1024),
     )(*[a if first else near_core(a) for a in args])
     return got if len(outs) > 1 else got[0]
 
@@ -212,7 +213,7 @@
         out_shape=[pltpu.VMEM(*o) for o in outs],
         scratch_shapes=[
             pltpu.VMEM((2, blocks, hid, width), BF16),
-            pltpu.SemaphoreType.DMA((3, blocks)),
+            pltpu.SemaphoreType.DMA((3, 2 * blocks)),
         ],
         cost_estimate=pl.CostEstimate(
             flops=2 * rows * blocks * width * 2 * hid // share,
@@ -309,23 +310,17 @@
     near = [mine, relay(mine, -2), relay(last, 2), last]
     far = lax.ppermute(jnp.stack(near), ("line", "core"), beside)
     wide = ((rows, hid), F32)
-    own, other, slope = product(
+    own, other, slope, held = product(
         functools.partial(backward_first_kernel, half),
-        [wide] * 3,
-        same,
+        [wide] * 3 + [((2, half, hid, width), BF16)],
+        jnp.concatenate([same, opposite]),
         (*near, pre_hidden),
         weights,
         half,
         1000,
     )
-    own, other = product(
-        backward_second_kernel,
-        [wide, ((rows, hid), BF16)],
-        opposite,
-        (far, own, other),
-        weights,
-        half,
-        1000,
+    own, other = call(
+        backward_second_kernel, [wide, ((rows, hid), BF16)], far, own, other, held
     )
     other = lax.ppermute(other, "core", cores)
     packed, token = call(

time: 108 us -> 107 us (level)
  Pallas kernels: 17.8 us -> 15.4 us
  local copies, waits for them, and re-layouts: 1.85 us -> 3.52 us
    pallas_call x4 -> x3, Pallas kernels: 13.6 us -> 10.9 us  [product(): pl.pallas_call(kernel, in_specs=[SMEM] + [VMEM] * len(args) + [HBM] * len...]
    unnamed x8 -> x12, local copies, waits for them, and re-layouts: 0.02 us -> 1.69 us
    all_to_all x2, waiting for transfers between devices: 0.01 us -> 1.42 us  [exchange(): x = lax.all_to_all(x, 'group', split_axis=0, concat_axis=0, tiled=True)]
    pallas_call x7 -> x8, Pallas kernels: 4.14 us -> 4.58 us  [call(): pl.pallas_call(kernel, in_specs=[VMEM] * len(args), out_specs=[VMEM] * le...]
  transfers between devices with their start and end apart: 13 -> 13, of which waited for: 2 -> 3; matrix products, arithmetic and copies ran while one was open for 2% -> 2% of each run, Pallas kernels for 16% -> 14%
where the time goes in v10:
time: 107 us; the launch traced here: 106 us
  starting transfers between devices  74.6 us (70%)
  Pallas kernels  15.4 us (14%)
  waiting for transfers between devices  11.6 us (11%)
  local copies, waits for them, and re-layouts  3.52 us (3%)
    ppermute x6, starting transfers between devices, relay(): return lax.ppermute(x, ('line', 'core'), pairs)  23.9 us
    all_to_all x2, starting transfers between devices, exchange(): x = lax.all_to_all(x, 'group', split_axis=0, concat_axis=0, tiled=True)  23.6 us
    ppermute x1, starting transfers between devices, on_device(): w_other = lax.ppermute(proj_weight, 'core', cores)  16.1 us
    pallas_call x3, Pallas kernels, product(): pl.pallas_call(kernel, in_specs=[SMEM] + [VMEM] * len(args) + [HBM] * len...  10.9 us
    ppermute x1, waiting for transfers between devices, on_device(): far = lax.ppermute(jnp.stack(near), ('line', 'core'), beside)  5.92 us
    ppermute x1, starting transfers between devices, on_device(): beside_terms = lax.ppermute(sent, ('line', 'core'), beside)  5.09 us
    pallas_call x8, Pallas kernels, call(): pl.pallas_call(kernel, in_specs=[VMEM] * len(args), out_specs=[VMEM] * le...  4.58 us
    ppermute x1, waiting for transfers between devices, on_device(): beside_terms = lax.ppermute(sent, ('line', 'core'), beside)  4.21 us
  transfers between devices with their start and end apart: 13, of which 3 were waited for; matrix products, arithmetic and copies ran while one was open for 2% of the time, Pallas kernels for 14%

profile of v10, /device:TPU:1, one launch (start us, length us, event | category | flops | bytes accessed | tf_op | source)
XLA Modules:
  0.0 106.2 jit_solution(13829029636602942869)
XLA Ops:
  0.6 16.1 %collective-permute-start.1 = (bf16[512,8192]{1,0:T(8,128)(2,1)}, bf16[512,8192]{1,0:T(8,128)(2,1)}, u32[]{:S(2)}, u32[]{:S(2)}) collective-permute-start(bf16[512,8192]{1,0:T(8,128)(2,1)} %refs_5_.1), channel_id=1, source_target_pairs={{0,1},{1,0},{2,3},{3,2},{4,5},{5,4},{6,7},{7,6},{8,9},{9,8},{10,11... | collective-permute-start | bytes 25165832 | tf_op jit(solution)/shard_map/ppermute | solution.py:263
  16.7 1.9 %collective-permute-start = (bf16[144,512]{1,0:T(8,128)(2,1)}, bf16[144,512]{1,0:T(8,128)(2,1)S(1)}, u32[]{:S(2)}, u32[]{:S(2)}) collective-permute-start(bf16[144,512]{1,0:T(8,128)(2,1)} %refs_4_.1), channel_id=1, source_target_pairs={{0,1},{1,0},{2,3},{3,2},{4,5},{5,4},{6,7},{7,6},{8,9},{9,8},{10,11... | collective-permute-start | bytes 442376 | tf_op jit(solution)/shard_map/ppermute | solution.py:264
  18.6 1.0 copy-done.1
  20.6 0.8 reshape.22
  21.4 9.3 %all-to-all-start.1 = ((bf16[64,4,384]{2,1,0:T(4,128)(2,1)}), bf16[64,4,384]{2,1,0:T(4,128)(2,1)S(1)}, u32[]{:S(2)}, u32[]{:S(2)}) async-start(bf16[64,4,384]{2,1,0:T(4,128)(2,1)} %reshape.22), calls=%async_computation.1 | async-start | bytes 393216 | tf_op jit(solution)/shard_map/all_to_all | solution.py:260
  30.8 3.4 %shard_map.77 = (bf16[4,144,512]{2,1,0:T(8,128)(2,1)S(1)}, bf16[144,1024]{1,0:T(8,128)(2,1)S(1)}) custom-call(s32[4]{0:T(128)S(1)} %fusion.5.at_ref, bf16[144,512]{1,0:T(8,128)(2,1)S(1)} %collective-permute-done.other_ref, bf16[512,8192]{1,0:T(8,128)(2,1)} %refs_5_.1, bf16[512,8192]{1,0:T(8,128)(2,1)} %collective-permute-done.1.w_other_ref.refs_6_, ...), custom_call_target="tpu_custom_call" | custom-call | flops 603979776 | bytes 4194304 | tf_op jit(solution)/shard_map/pallas_call | solution.py:209
  34.1 5.1 %collective-permute-start.2 = (bf16[4,144,512]{2,1,0:T(8,128)(2,1)S(1)}, bf16[4,144,512]{2,1,0:T(8,128)(2,1)S(1)}, u32[]{:S(2)}, u32[]{:S(2)}) collective-permute-start(bf16[4,144,512]{2,1,0:T(8,128)(2,1)S(1)} %get-tuple-element.18), channel_id=1, source_target_pairs={{0,2},{1,15},{2,0},{3,5},{4,6},{5,3},{6,4},{7,9},{8,10},{9,7},{10,... | collective-permute-start | bytes 1769480 | tf_op jit(solution)/shard_map/ppermute | solution.py:279
  39.3 3.3 %shard_map.78.kept_ref = bf16[4,144,512]{2,1,0:T(8,128)(2,1)S(1)} custom-call(s32[4]{0:T(128)S(1)} %fusion.2.at_ref, bf16[144,1024]{1,0:T(8,128)(2,1)S(1)} %get-tuple-element.17.act_ref, bf16[512,8192]{1,0:T(8,128)(2,1)} %refs_5_.1, bf16[512,8192]{1,0:T(8,128)(2,1)} %collective-permute-done.1.w_other_ref.refs_6_), custom_call_target="tpu_custom_call" | custom-call | flops 603979776 | bytes 4194304 | tf_op jit(solution)/shard_map/pallas_call | solution.py:209
  42.6 4.2 %collective-permute-done.2.beside_ref = bf16[4,144,512]{2,1,0:T(8,128)(2,1)S(1)} collective-permute-done((bf16[4,144,512]{2,1,0:T(8,128)(2,1)S(1)}, bf16[4,144,512]{2,1,0:T(8,128)(2,1)S(1)}, u32[]{:S(2)}, u32[]{:S(2)}) %collective-permute-start.2) | collective-permute-done | bytes 589856 | tf_op jit(solution)/shard_map/ppermute | solution.py:279
  46.9 4.2 %collective-permute-start.4 = (bf16[144,512]{1,0:T(8,128)(2,1)S(1)}, bf16[144,512]{1,0:T(8,128)(2,1)S(1)}, u32[]{:S(2)}, u32[]{:S(2)}) collective-permute-start(bf16[144,512]{1,0:T(8,128)(2,1)S(1)} %get-tuple-element.22), channel_id=1, source_target_pairs={{0,4},{1,13},{2,6},{3,15},{4,8},{5,1},{6,10},{7,3},{8,12},{9,5},{1... | collective-permute-start | bytes 442376 | tf_op jit(solution)/shard_map/ppermute | solution.py:254
  51.6 5.0 %collective-permute-start.7 = (bf16[144,512]{1,0:T(8,128)(2,1)S(1)}, bf16[144,512]{1,0:T(8,128)(2,1)S(1)}, u32[]{:S(2)}, u32[]{:S(2)}) collective-permute-start(bf16[144,512]{1,0:T(8,128)(2,1)S(1)} %shard_map.84.refs_0_), channel_id=1, source_target_pairs={{0,4},{1,13},{2,6},{3,15},{4,8},{5,1},{6,10},{7,3},{8,12},{9,5},{1... | collective-permute-start | bytes 442376 | tf_op jit(solution)/shard_map/ppermute | solution.py:254
  56.6 1.9 %collective-permute-start.3 = (bf16[144,512]{1,0:T(8,128)(2,1)S(1)}, bf16[144,512]{1,0:T(8,128)(2,1)S(1)}, u32[]{:S(2)}, u32[]{:S(2)}) collective-permute-start(bf16[144,512]{1,0:T(8,128)(2,1)S(1)} %get-tuple-element.20), channel_id=1, source_target_pairs={{0,12},{1,5},{2,14},{3,7},{4,0},{5,9},{6,2},{7,11},{8,4},{9,13},{1... | collective-permute-start | bytes 442376 | tf_op jit(solution)/shard_map/ppermute | solution.py:254
  58.6 5.5 %collective-permute-start.5 = (bf16[144,512]{1,0:T(8,128)(2,1)S(1)}, bf16[144,512]{1,0:T(8,128)(2,1)S(1)}, u32[]{:S(2)}, u32[]{:S(2)}) collective-permute-start(bf16[144,512]{1,0:T(8,128)(2,1)S(1)} %shard_map.80), channel_id=1, source_target_pairs={{0,4},{1,13},{2,6},{3,15},{4,8},{5,1},{6,10},{7,3},{8,12},{9,5},{1... | collective-permute-start | bytes 442376 | tf_op jit(solution)/shard_map/ppermute | solution.py:254
  64.1 1.9 %collective-permute-start.6 = (bf16[144,512]{1,0:T(8,128)(2,1)S(1)}, bf16[144,512]{1,0:T(8,128)(2,1)S(1)}, u32[]{:S(2)}, u32[]{:S(2)}) collective-permute-start(bf16[144,512]{1,0:T(8,128)(2,1)S(1)} %shard_map.84.refs_0_), channel_id=1, source_target_pairs={{0,12},{1,5},{2,14},{3,7},{4,0},{5,9},{6,2},{7,11},{8,4},{9,13},{1... | collective-permute-start | bytes 442376 | tf_op jit(solution)/shard_map/ppermute | solution.py:254
  66.0 5.5 %collective-permute-start.8 = (bf16[144,512]{1,0:T(8,128)(2,1)S(1)}, bf16[144,512]{1,0:T(8,128)(2,1)S(1)}, u32[]{:S(2)}, u32[]{:S(2)}) collective-permute-start(bf16[144,512]{1,0:T(8,128)(2,1)S(1)} %collective-permute-done.7.refs_3_), channel_id=1, source_target_pairs={{0,4},{1,13},{2,6},{3,15},{4,8},{5,1},{6,10},{7,3},{8,12},{9,5},{1... | collective-permute-start | bytes 442376 | tf_op jit(solution)/shard_map/ppermute | solution.py:254
  71.9 0.8 reshape.20
  72.7 14.3 %all-to-all-start = ((bf16[64,4,384]{2,1,0:T(4,128)(2,1)}), bf16[64,4,384]{2,1,0:T(4,128)(2,1)S(1)}, u32[]{:S(2)}, u32[]{:S(2)}) async-start(bf16[64,4,384]{2,1,0:T(4,128)(2,1)} %reshape.20), calls=%async_computation | async-start | bytes 393216 | tf_op jit(solution)/shard_map/all_to_all | solution.py:260
  87.0 1.9 %collective-permute-start.9 = (bf16[4,144,512]{2,1,0:T(8,128)(2,1)S(1)}, bf16[4,144,512]{2,1,0:T(8,128)(2,1)S(1)}, u32[]{:S(2)}, u32[]{:S(2)}) collective-permute-start(bf16[4,144,512]{2,1,0:T(8,128)(2,1)S(1)} %pad_maximum_fusion), channel_id=1, source_target_pairs={{0,2},{1,15},{2,0},{3,5},{4,6},{5,3},{6,4},{7,9},{8,10},{9,7},{10,... | collective-permute-start | bytes 1769480 | tf_op jit(solution)/shard_map/ppermute | solution.py:311
  89.1 4.2 %shard_map.85 = (f32[144,512]{1,0:T(8,128)S(1)}, f32[144,512]{1,0:T(8,128)S(1)}, f32[144,512]{1,0:T(8,128)S(1)}, bf16[2,4,512,512]{3,2,1,0:T(8,128)(2,1)S(1)}) custom-call(s32[8]{0:T(128)S(1)} %pad_add_fusion.at_ref, bf16[144,512]{1,0:T(8,128)(2,1)S(1)} %shard_map.84.refs_0_, bf16[144,512]{1,0:T(8,128)(2,1)S(1)} %collective-permute-done.6.refs_1_, ...), custom_call_target="tpu_custom_call" | custom-call | flops 603979 | bytes 4194 | tf_op jit(solution)/shard_map/pallas_call | solution.py:209
  93.3 5.9 %collective-permute-done.9.grad_ref = bf16[4,144,512]{2,1,0:T(8,128)(2,1)S(1)} collective-permute-done((bf16[4,144,512]{2,1,0:T(8,128)(2,1)S(1)}, bf16[4,144,512]{2,1,0:T(8,128)(2,1)S(1)}, u32[]{:S(2)}, u32[]{:S(2)}) %collective-permute-start.9) | collective-permute-done | bytes 589856 | tf_op jit(solution)/shard_map/ppermute | solution.py:311
  99.2 1.5 %shard_map.86 = (f32[144,512]{1,0:T(8,128)S(1)}, bf16[144,512]{1,0:T(8,128)(2,1)S(1)}) custom-call(bf16[4,144,512]{2,1,0:T(8,128)(2,1)S(1)} %collective-permute-done.9.grad_ref, f32[144,512]{1,0:T(8,128)S(1)} %get-tuple-element.25.own_in, f32[144,512]{1,0:T(8,128)S(1)} %get-tuple-element.26.other_in, bf16[2,4,512,512]{3,2,1,0:T(8,128)(2,1)S(1)} %get-tuple-element.27.held_ref), custom_call_target="tpu_custom_call" | custom-call | tf_op jit(solution)/shard_map/pallas_call | solution.py:196
  100.7 2.1 %collective-permute-start.10 = (bf16[144,512]{1,0:T(8,128)(2,1)S(1)}, bf16[144,512]{1,0:T(8,128)(2,1)S(1)}, u32[]{:S(2)}, u32[]{:S(2)}) collective-permute-start(bf16[144,512]{1,0:T(8,128)(2,1)S(1)} %get-tuple-element.29), channel_id=1, source_target_pairs={{0,1},{1,0},{2,3},{3,2},{4,5},{5,4},{6,7},{7,6},{8,9},{9,8},{10,11... | collective-permute-start | bytes 442376 | tf_op jit(solution)/shard_map/ppermute | solution.py:325
  102.8 1.4 %all-to-all-done = bf16[64,4,384]{2,1,0:T(4,128)(2,1)S(1)} async-done(((bf16[64,4,384]{2,1,0:T(4,128)(2,1)}), bf16[64,4,384]{2,1,0:T(4,128)(2,1)S(1)}, u32[]{:S(2)}, u32[]{:S(2)}) %all-to-all-start) | async-done | bytes 196640 | tf_op jit(solution)/shard_map/all_to_all | solution.py:260
  104.3 1.2 %shard_map.82 = (bf16[384,512]{1,0:T(8,128)(2,1)}, f32[8,128]{1,0:T(8,128)S(1)}) custom-call(s32[1,192]{1,0:T(1,128)S(1)} %copy-done.5, bf16[192,512]{1,0:T(8,128)(2,1)S(1)} %reshape.21.arrived_ref, bf16[384,512]{1,0:T(8,128)(2,1)S(1)} %copy-done.2), custom_call_target="tpu_custom_call" | custom-call | tf_op jit(solution)/shard_map/pallas_call | solution.py:196
  (33 shorter events, 3.0 us)
Async XLA Ops:
  0.6 30.1 %collective-permute-start.1 = (bf16[512,8192]{1,0:T(8,128)(2,1)}, bf16[512,8192]{1,0:T(8,128)(2,1)}, u32[]{:S(2)}, u32[]{:S(2)}) collective-permute-start(bf16[512,8192]{1,0:T(8,128)(2,1)} %refs_5_.1), channel_id=1, source_target_pairs={{0,1},{1,0},{2,3},{3,2},{4,5},{5,4},{6,7},{7,6},{8,9},{9,8},{10,11... | collective-permute-start | bytes 25165832 | tf_op jit(solution)/shard_map/ppermute | solution.py:263
  16.7 14.0 %collective-permute-start = (bf16[144,512]{1,0:T(8,128)(2,1)}, bf16[144,512]{1,0:T(8,128)(2,1)S(1)}, u32[]{:S(2)}, u32[]{:S(2)}) collective-permute-start(bf16[144,512]{1,0:T(8,128)(2,1)} %refs_4_.1), channel_id=1, source_target_pairs={{0,1},{1,0},{2,3},{3,2},{4,5},{5,4},{6,7},{7,6},{8,9},{9,8},{10,11... | collective-permute-start | bytes 442376 | tf_op jit(solution)/shard_map/ppermute | solution.py:264
  18.6 1.0 copy-start.1
  19.6 0.7 copy-start.4
  21.4 29.7 %all-to-all-start.1 = ((bf16[64,4,384]{2,1,0:T(4,128)(2,1)}), bf16[64,4,384]{2,1,0:T(4,128)(2,1)S(1)}, u32[]{:S(2)}, u32[]{:S(2)}) async-start(bf16[64,4,384]{2,1,0:T(4,128)(2,1)} %reshape.22), calls=%async_computation.1 | async-start | bytes 393216 | tf_op jit(solution)/shard_map/all_to_all | solution.py:260
  34.1 12.7 %collective-permute-start.2 = (bf16[4,144,512]{2,1,0:T(8,128)(2,1)S(1)}, bf16[4,144,512]{2,1,0:T(8,128)(2,1)S(1)}, u32[]{:S(2)}, u32[]{:S(2)}) collective-permute-start(bf16[4,144,512]{2,1,0:T(8,128)(2,1)S(1)} %get-tuple-element.18), channel_id=1, source_target_pairs={{0,2},{1,15},{2,0},{3,5},{4,6},{5,3},{6,4},{7,9},{8,10},{9,7},{10,... | collective-permute-start | bytes 1769480 | tf_op jit(solution)/shard_map/ppermute | solution.py:279
  39.3 12.0 %copy-start.3 = (s32[144,1]{0,1:T(1,128)S(1)}, s32[144,1]{0,1:T(1,128)}, u32[]{:S(2)}) copy-start(s32[144,1]{0,1:T(1,128)} %param.9) | copy-start | bytes 1732
  39.3 49.8 %copy-start = (bf16[144,512]{1,0:T(8,128)(2,1)S(1)}, bf16[144,512]{1,0:T(8,128)(2,1)}, u32[]{:S(2)}) copy-start(bf16[144,512]{1,0:T(8,128)(2,1)} %refs_4_.1) | copy-start | bytes 442372
  46.9 11.6 %collective-permute-start.4 = (bf16[144,512]{1,0:T(8,128)(2,1)S(1)}, bf16[144,512]{1,0:T(8,128)(2,1)S(1)}, u32[]{:S(2)}, u32[]{:S(2)}) collective-permute-start(bf16[144,512]{1,0:T(8,128)(2,1)S(1)} %get-tuple-element.22), channel_id=1, source_target_pairs={{0,4},{1,13},{2,6},{3,15},{4,8},{5,1},{6,10},{7,3},{8,12},{9,5},{1... | collective-permute-start | bytes 442376 | tf_op jit(solution)/shard_map/ppermute | solution.py:254
  51.6 14.4 %collective-permute-start.7 = (bf16[144,512]{1,0:T(8,128)(2,1)S(1)}, bf16[144,512]{1,0:T(8,128)(2,1)S(1)}, u32[]{:S(2)}, u32[]{:S(2)}) collective-permute-start(bf16[144,512]{1,0:T(8,128)(2,1)S(1)} %shard_map.84.refs_0_), channel_id=1, source_target_pairs={{0,4},{1,13},{2,6},{3,15},{4,8},{5,1},{6,10},{7,3},{8,12},{9,5},{1... | collective-permute-start | bytes 442376 | tf_op jit(solution)/shard_map/ppermute | solution.py:254
  56.6 14.9 %collective-permute-start.3 = (bf16[144,512]{1,0:T(8,128)(2,1)S(1)}, bf16[144,512]{1,0:T(8,128)(2,1)S(1)}, u32[]{:S(2)}, u32[]{:S(2)}) collective-permute-start(bf16[144,512]{1,0:T(8,128)(2,1)S(1)} %get-tuple-element.20), channel_id=1, source_target_pairs={{0,12},{1,5},{2,14},{3,7},{4,0},{5,9},{6,2},{7,11},{8,4},{9,13},{1... | collective-permute-start | bytes 442376 | tf_op jit(solution)/shard_map/ppermute | solution.py:254
  58.6 12.9 %collective-permute-start.5 = (bf16[144,512]{1,0:T(8,128)(2,1)S(1)}, bf16[144,512]{1,0:T(8,128)(2,1)S(1)}, u32[]{:S(2)}, u32[]{:S(2)}) collective-permute-start(bf16[144,512]{1,0:T(8,128)(2,1)S(1)} %shard_map.80), channel_id=1, source_target_pairs={{0,4},{1,13},{2,6},{3,15},{4,8},{5,1},{6,10},{7,3},{8,12},{9,5},{1... | collective-permute-start | bytes 442376 | tf_op jit(solution)/shard_map/ppermute | solution.py:254
  64.1 22.9 %collective-permute-start.6 = (bf16[144,512]{1,0:T(8,128)(2,1)S(1)}, bf16[144,512]{1,0:T(8,128)(2,1)S(1)}, u32[]{:S(2)}, u32[]{:S(2)}) collective-permute-start(bf16[144,512]{1,0:T(8,128)(2,1)S(1)} %shard_map.84.refs_0_), channel_id=1, source_target_pairs={{0,12},{1,5},{2,14},{3,7},{4,0},{5,9},{6,2},{7,11},{8,4},{9,13},{1... | collective-permute-start | bytes 442376 | tf_op jit(solution)/shard_map/ppermute | solution.py:254
  66.0 21.0 %collective-permute-start.8 = (bf16[144,512]{1,0:T(8,128)(2,1)S(1)}, bf16[144,512]{1,0:T(8,128)(2,1)S(1)}, u32[]{:S(2)}, u32[]{:S(2)}) collective-permute-start(bf16[144,512]{1,0:T(8,128)(2,1)S(1)} %collective-permute-done.7.refs_3_), channel_id=1, source_target_pairs={{0,4},{1,13},{2,6},{3,15},{4,8},{5,1},{6,10},{7,3},{8,12},{9,5},{1... | collective-permute-start | bytes 442376 | tf_op jit(solution)/shard_map/ppermute | solution.py:254
  72.7 31.5 %all-to-all-start = ((bf16[64,4,384]{2,1,0:T(4,128)(2,1)}), bf16[64,4,384]{2,1,0:T(4,128)(2,1)S(1)}, u32[]{:S(2)}, u32[]{:S(2)}) async-start(bf16[64,4,384]{2,1,0:T(4,128)(2,1)} %reshape.20), calls=%async_computation | async-start | bytes 393216 | tf_op jit(solution)/shard_map/all_to_all | solution.py:260
  87.0 12.1 %collective-permute-start.9 = (bf16[4,144,512]{2,1,0:T(8,128)(2,1)S(1)}, bf16[4,144,512]{2,1,0:T(8,128)(2,1)S(1)}, u32[]{:S(2)}, u32[]{:S(2)}) collective-permute-start(bf16[4,144,512]{2,1,0:T(8,128)(2,1)S(1)} %pad_maximum_fusion), channel_id=1, source_target_pairs={{0,2},{1,15},{2,0},{3,5},{4,6},{5,3},{6,4},{7,9},{8,10},{9,7},{10,... | collective-permute-start | bytes 1769480 | tf_op jit(solution)/shard_map/ppermute | solution.py:311
  89.1 15.3 %copy-start.2 = (bf16[384,512]{1,0:T(8,128)(2,1)S(1)}, bf16[384,512]{1,0:T(8,128)(2,1)}, u32[]{:S(2)}) copy-start(bf16[384,512]{1,0:T(8,128)(2,1)} %text_ref.1) | copy-start | bytes 1179652
  89.1 15.3 %copy-start.5 = (s32[1,192]{1,0:T(1,128)S(1)}, s32[1,192]{1,0:T(1,128)}, u32[]{:S(2)}) copy-start(s32[1,192]{1,0:T(1,128)} %offsets_ref.3) | copy-start | bytes 2308
  100.7 4.9 %collective-permute-start.10 = (bf16[144,512]{1,0:T(8,128)(2,1)S(1)}, bf16[144,512]{1,0:T(8,128)(2,1)S(1)}, u32[]{:S(2)}, u32[]{:S(2)}) collective-permute-start(bf16[144,512]{1,0:T(8,128)(2,1)S(1)} %get-tuple-element.29), channel_id=1, source_target_pairs={{0,1},{1,0},{2,3},{3,2},{4,5},{5,4},{6,7},{7,6},{8,9},{9,8},{10,11... | collective-permute-start | bytes 442376 | tf_op jit(solution)/shard_map/ppermute | solution.py:325
